TPU v7x, 32 devices: a whole 2x2x4 slice. The times are simulated.
32 devices in a mesh: rows: 8 (over z, core), cols: 4 (over y, x).
Axes of the slice: x: 2, y: 2, z: 4, core: 2. Of those that a mesh axis runs over, the one named last changes fastest.
Arguments:
- inputs: bfloat16 [10240, 512], P('rows'), may hold values from -6 to 6
- reset_flags: int32 [10240], P('rows'), may hold values 0 or 1
- gate_weight: bfloat16 [2, 1024, 4, 4096], P(None, None, None, 'cols'), may hold values from -0.1875 to 0.1875
- gate_bias: float32 [2, 4, 4096], P(None, None, 'cols'), may hold values from -3 to 3
- proj_weight: bfloat16 [2, 4096, 512], P(None, 'cols'), may hold values from -0.25 to 0.25
- grad_out: bfloat16 [10240, 2, 512], P('rows'), may hold values from -6 to 6
Outputs:
- layer_out: bfloat16 [10240, 2, 512], P('rows')
- input_grad: bfloat16 [10240, 512], P('rows', 'cols')
- gate_weight_grad: float32 [2, 1024, 4, 4096], P(None, 'rows', None, 'cols')
- gate_bias_grad: float32 [2, 4, 4096], P(None, None, 'cols')
- proj_weight_grad: float32 [2, 4096, 512], P(None, 'cols', 'rows')
Inputs may be any that keep to these rules, and one draw needn't show every extreme that they name: `reset_flags`: 1 marks the first position of a document.
All inputs are finite; a program needn't handle non-finite values. No bound on the sum of `reset_flags` on one device may be relied on, other than what follows from the above.
Results may differ from a plain program's by a relative error of at most 0.017.
Values may be sent and summed in bfloat16 or wider, within the bound.
No kernel may reach another device: no remote copies, remote signals or barrier semaphores. Data moves between devices by JAX's collectives and lax.ppermute only.
A program may use at most 384 MiB of HBM per device.

v0:
```python
import jax
import jax.numpy as jnp
from jax import lax
from jax.sharding import PartitionSpec as P

STEPS = 20


def soft_clip(amount):
    return 3.0 * jnp.tanh(amount / 3.0)


def clip_slope(amount):
    tangent = jnp.tanh(amount / 3.0)
    return 1.0 - tangent * tangent


def per_device(inputs, reset_flags, gate_weight, gate_bias, proj_weight, grad_out):
    tok_rows, model_width = inputs.shape
    windows = tok_rows // STEPS
    cell_cols = gate_weight.shape[3]
    gate_width = 4 * cell_cols
    share_width = model_width // lax.axis_size("cols")
    column = lax.axis_index("cols") * share_width
    weight = gate_weight.reshape(2, 2 * model_width, gate_width)
    w_input = weight[:, :model_width]
    w_recur = weight[:, model_width:]
    bias_row = gate_bias.reshape(2, 1, gate_width)
    sequence = jnp.swapaxes(inputs.reshape(windows, STEPS, model_width), 0, 1)
    x_stack = jnp.stack([sequence, sequence[::-1]], axis=1)
    flag_grid = jnp.swapaxes(reset_flags.reshape(windows, STEPS), 0, 1).astype(jnp.float32)
    position = lax.broadcasted_iota(jnp.int32, (STEPS, windows), 0)
    keep_ahead = jnp.where(position > 0, 1.0 - flag_grid, 0.0)
    next_flags = jnp.concatenate([flag_grid[1:], jnp.zeros((1, windows), jnp.float32)], axis=0)
    keep_behind = jnp.where(position < STEPS - 1, 1.0 - next_flags, 0.0)
    keep_stack = jnp.stack([keep_ahead, keep_behind[::-1]], axis=1)[..., None]
    input_gates = jnp.einsum("sdwh,dhg->sdwg", x_stack, w_input, preferred_element_type=jnp.float32)

    def forward_step(state_pair, pieces):
        hidden, cell_prev = state_pair
        gates_in, keep_step = pieces
        kept_hidden = hidden * keep_step.astype(jnp.bfloat16)
        gate_pre = (
            gates_in
            + jnp.einsum("dwh,dhg->dwg", kept_hidden, w_recur, preferred_element_type=jnp.float32)
            + bias_row
        )
        in_gate = jax.nn.sigmoid(gate_pre[..., :cell_cols])
        forget = jax.nn.sigmoid(gate_pre[..., cell_cols : 2 * cell_cols])
        update = jnp.tanh(gate_pre[..., 2 * cell_cols : 3 * cell_cols])
        out_gate = jax.nn.sigmoid(gate_pre[..., 3 * cell_cols :])
        kept_cell = cell_prev * keep_step
        cell_new = soft_clip(forget * kept_cell + in_gate * update)
        cell_output = (out_gate * jnp.tanh(cell_new)).astype(jnp.bfloat16)
        partial_raw = jnp.einsum(
            "dwc,dch->dwh", cell_output, proj_weight, preferred_element_type=jnp.float32
        )
        proj_raw = lax.psum(partial_raw, "cols")
        new_hidden = soft_clip(proj_raw).astype(jnp.bfloat16)
        return (
            (new_hidden, cell_new),
            (kept_hidden, gate_pre, kept_cell, cell_new, cell_output, proj_raw, new_hidden),
        )

    init_state = (
        jnp.zeros((2, windows, model_width), jnp.bfloat16),
        jnp.zeros((2, windows, cell_cols), jnp.float32),
    )
    _, fwd_saved = lax.scan(forward_step, init_state, (input_gates, keep_stack))
    kept_all, pre_all, kept_cells, cell_states, cell_outputs, proj_raws, hiddens = fwd_saved
    ahead_hidden = hiddens[:, 0]
    behind_hidden = hiddens[::-1, 1]
    both_outputs = jnp.stack([ahead_hidden, behind_hidden], axis=2).astype(jnp.float32) + sequence[
        :, :, None, :
    ].astype(jnp.float32)
    block_out = (
        jnp.swapaxes(both_outputs, 0, 1).reshape(tok_rows, 2, model_width).astype(jnp.bfloat16)
    )
    out_grid = jnp.transpose(grad_out.reshape(windows, STEPS, 2, model_width), (1, 2, 0, 3))
    grad_stack = jnp.stack([out_grid[:, 0], out_grid[::-1, 1]], axis=1)

    def backward_step(state_pair, pieces):
        recur_part, cell_grad = state_pair
        gate_pre, kept_cell, cell_new, cell_output, proj_raw, grad_step, keep_step = pieces
        recur_sum = lax.psum(recur_part, "cols")
        hidden_grad = grad_step.astype(jnp.float32) + recur_sum
        raw_grad = (hidden_grad * clip_slope(proj_raw)).astype(jnp.bfloat16)
        emit_grad = jnp.einsum(
            "dwh,dch->dwc", raw_grad, proj_weight, preferred_element_type=jnp.float32
        )
        in_gate = jax.nn.sigmoid(gate_pre[..., :cell_cols])
        forget = jax.nn.sigmoid(gate_pre[..., cell_cols : 2 * cell_cols])
        update = jnp.tanh(gate_pre[..., 2 * cell_cols : 3 * cell_cols])
        out_gate = jax.nn.sigmoid(gate_pre[..., 3 * cell_cols :])
        tanh_cell = jnp.tanh(cell_new)
        cell_total = cell_grad + emit_grad * out_gate * (1.0 - tanh_cell * tanh_cell)
        cell_third = cell_new / 3.0
        cell_raw_grad = cell_total * (1.0 - cell_third * cell_third)
        pre_grad = jnp.concatenate(
            [
                cell_raw_grad * update * in_gate * (1.0 - in_gate),
                cell_raw_grad * kept_cell * forget * (1.0 - forget),
                cell_raw_grad * in_gate * (1.0 - update * update),
                emit_grad * tanh_cell * out_gate * (1.0 - out_gate),
            ],
            axis=-1,
        ).astype(jnp.bfloat16)
        recur_next = (
            jnp.einsum("dwg,dhg->dwh", pre_grad, w_recur, preferred_element_type=jnp.float32)
            * keep_step
        )
        cell_next = cell_raw_grad * forget * keep_step
        return ((recur_next, cell_next), (pre_grad, raw_grad))

    zero_state = (
        jnp.zeros((2, windows, model_width), jnp.float32),
        jnp.zeros((2, windows, cell_cols), jnp.float32),
    )
    _, back_saved = lax.scan(
        backward_step,
        zero_state,
        (pre_all, kept_cells, cell_states, cell_outputs, proj_raws, grad_stack, keep_stack),
        reverse=True,
    )
    pre_grads, raw_grads = back_saved
    input_part = jnp.einsum(
        "sdwg,dhg->sdwh", pre_grads, w_input, preferred_element_type=jnp.float32
    )
    input_sum = jnp.swapaxes(input_part[:, 0] + input_part[::-1, 1], 0, 1).reshape(
        tok_rows, model_width
    )
    input_share = lax.psum_scatter(
        input_sum.astype(jnp.bfloat16), "cols", scatter_dimension=1, tiled=True
    ).astype(jnp.float32)
    residual_grad = grad_out[:, 0].astype(jnp.float32) + grad_out[:, 1].astype(jnp.float32)
    input_grad = (
        input_share + lax.dynamic_slice_in_dim(residual_grad, column, share_width, 1)
    ).astype(jnp.bfloat16)
    input_weight_grad = jnp.einsum(
        "sdwh,sdwg->dhg", x_stack, pre_grads, preferred_element_type=jnp.float32
    )
    recur_weight_grad = jnp.einsum(
        "sdwh,sdwg->dhg", kept_all, pre_grads, preferred_element_type=jnp.float32
    )
    weight_grad = jnp.concatenate([input_weight_grad, recur_weight_grad], axis=1).reshape(
        2, 2 * model_width, 4, cell_cols
    )
    proj_grad = jnp.einsum(
        "sdwc,sdwh->dch", cell_outputs, raw_grads, preferred_element_type=jnp.float32
    )
    bias_grad = jnp.sum(pre_grads, axis=(0, 2), dtype=jnp.float32).reshape(2, 4, cell_cols)
    weight_share, proj_share = (
        lax.psum_scatter(
            weight_grad.astype(jnp.bfloat16), "rows", scatter_dimension=1, tiled=True
        ).astype(jnp.float32),
        lax.psum_scatter(
            proj_grad.astype(jnp.bfloat16), "rows", scatter_dimension=2, tiled=True
        ).astype(jnp.float32),
    )
    bias_total = lax.psum(bias_grad, "rows")
    return (block_out, input_grad, weight_share, bias_total, proj_share)


def solution(mesh):
    placed = (
        P("rows", None),
        P("rows"),
        P(None, None, None, "cols"),
        P(None, None, "cols"),
        P(None, "cols", None),
        P("rows", None, None),
    )
    return jax.shard_map(
        per_device,
        mesh=mesh,
        in_specs=placed,
        out_specs=(
            P("rows", None, None),
            P("rows", "cols"),
            P(None, "rows", None, "cols"),
            P(None, None, "cols"),
            P(None, "cols", "rows"),
        ),
        check_vma=False,
    )
```

profile of v0, /device:TPU:0, one launch (start us, length us, event | category | flops | bytes accessed | tf_op | source)
XLA Modules:
  0.0 2807.8 jit_solution(4884574353266580099)
XLA Ops:
  101.2 1153.3 %while.48 = (s32[]{:T(128)}, bf16[2,64,512]{2,1,0:T(8,128)(2,1)S(1)}, f32[2,64,1024]{2,1,0:T(8,128)S(1)}, bf16[20,2,64,512]{3,2,1,0:T(8,128)(2,1)}, f32[20,2,64,...) while((s32[]{:T(128)}, ...), condition=%wide.region_2.3_spmd.clone, body=%wide.region_0.2_spmd.clone.sunk | while | flops 675479680 | bytes 27167732 | solution.py:69
  114.2 44.0 %all-reduce.4.cloned.1.call-done = f32[2,64,512]{2,1,0:T(8,128)} async-done(((f32[2,64,512]{2,1,0:T(8,128)}), f32[2,64,512]{2,1,0:T(8,128)}) %all-reduce.4.cloned.1.call-update) | async-done | bytes 262160 | tf_op jit(solution)/shard_map/while/body/eval_jaxpr/psum | solution.py:58
  289.4 41.3 %all-reduce.4.cloned.1.call-done = f32[2,64,512]{2,1,0:T(8,128)} async-done(((f32[2,64,512]{2,1,0:T(8,128)}), f32[2,64,512]{2,1,0:T(8,128)}) %all-reduce.4.cloned.1.call-update) | async-done | bytes 262160 | tf_op jit(solution)/shard_map/while/body/eval_jaxpr/psum | solution.py:58
  404.6 41.3 %all-reduce.4.cloned.1.call-done = f32[2,64,512]{2,1,0:T(8,128)} async-done(((f32[2,64,512]{2,1,0:T(8,128)}), f32[2,64,512]{2,1,0:T(8,128)}) %all-reduce.4.cloned.1.call-update) | async-done | bytes 262160 | tf_op jit(solution)/shard_map/while/body/eval_jaxpr/psum | solution.py:58
  577.2 41.2 %all-reduce.4.cloned.1.call-done = f32[2,64,512]{2,1,0:T(8,128)} async-done(((f32[2,64,512]{2,1,0:T(8,128)}), f32[2,64,512]{2,1,0:T(8,128)}) %all-reduce.4.cloned.1.call-update) | async-done | bytes 262160 | tf_op jit(solution)/shard_map/while/body/eval_jaxpr/psum | solution.py:58
  749.7 41.3 %all-reduce.4.cloned.1.call-done = f32[2,64,512]{2,1,0:T(8,128)} async-done(((f32[2,64,512]{2,1,0:T(8,128)}), f32[2,64,512]{2,1,0:T(8,128)}) %all-reduce.4.cloned.1.call-update) | async-done | bytes 262160 | tf_op jit(solution)/shard_map/while/body/eval_jaxpr/psum | solution.py:58
  807.2 41.3 %all-reduce.4.cloned.1.call-done = f32[2,64,512]{2,1,0:T(8,128)} async-done(((f32[2,64,512]{2,1,0:T(8,128)}), f32[2,64,512]{2,1,0:T(8,128)}) %all-reduce.4.cloned.1.call-update) | async-done | bytes 262160 | tf_op jit(solution)/shard_map/while/body/eval_jaxpr/psum | solution.py:58
  979.9 41.3 %all-reduce.4.cloned.1.call-done = f32[2,64,512]{2,1,0:T(8,128)} async-done(((f32[2,64,512]{2,1,0:T(8,128)}), f32[2,64,512]{2,1,0:T(8,128)}) %all-reduce.4.cloned.1.call-update) | async-done | bytes 262160 | tf_op jit(solution)/shard_map/while/body/eval_jaxpr/psum | solution.py:58
  1037.4 41.3 %all-reduce.4.cloned.1.call-done = f32[2,64,512]{2,1,0:T(8,128)} async-done(((f32[2,64,512]{2,1,0:T(8,128)}), f32[2,64,512]{2,1,0:T(8,128)}) %all-reduce.4.cloned.1.call-update) | async-done | bytes 262160 | tf_op jit(solution)/shard_map/while/body/eval_jaxpr/psum | solution.py:58
  1210.0 41.3 %all-reduce.4.cloned.1.call-done = f32[2,64,512]{2,1,0:T(8,128)} async-done(((f32[2,64,512]{2,1,0:T(8,128)}), f32[2,64,512]{2,1,0:T(8,128)}) %all-reduce.4.cloned.1.call-update) | async-done | bytes 262160 | tf_op jit(solution)/shard_map/while/body/eval_jaxpr/psum | solution.py:58
  1263.6 1206.5 %while.49 = (s32[]{:T(128)}, f32[2,64,512]{2,1,0:T(8,128)S(1)}, f32[2,64,1024]{2,1,0:T(8,128)S(1)}, bf16[20,2,64,4096]{3,2,1,0:T(8,128)(2,1)}, bf16[20,2,64,512]...) while((s32[]{:T(128)}, f32[2,64,512]{2,1,0:T(8,128)S(1)}, ...), condition=%wide.region_5.6_spmd.clone, body=%wide.region_3.5_spmd.clone.sunk | while | flops 685899776 | bytes 28313840 | solution.py:119
  1267.1 44.0 %all-reduce.6.cloned.1.call-done = f32[2,64,512]{2,1,0:T(8,128)} async-done(((f32[2,64,512]{2,1,0:T(8,128)}), f32[2,64,512]{2,1,0:T(8,128)}) %all-reduce.6.cloned.1.call-update) | async-done | bytes 262160 | tf_op jit(solution)/shard_map/while/body/eval_jaxpr/psum | solution.py:85
  1327.6 44.0 %all-reduce.6.cloned.1.call-done = f32[2,64,512]{2,1,0:T(8,128)} async-done(((f32[2,64,512]{2,1,0:T(8,128)}), f32[2,64,512]{2,1,0:T(8,128)}) %all-reduce.6.cloned.1.call-update) | async-done | bytes 262160 | tf_op jit(solution)/shard_map/while/body/eval_jaxpr/psum | solution.py:85
  1388.0 44.0 %all-reduce.6.cloned.1.call-done = f32[2,64,512]{2,1,0:T(8,128)} async-done(((f32[2,64,512]{2,1,0:T(8,128)}), f32[2,64,512]{2,1,0:T(8,128)}) %all-reduce.6.cloned.1.call-update) | async-done | bytes 262160 | tf_op jit(solution)/shard_map/while/body/eval_jaxpr/psum | solution.py:85
  1448.5 43.7 %all-reduce.6.cloned.1.call-done = f32[2,64,512]{2,1,0:T(8,128)} async-done(((f32[2,64,512]{2,1,0:T(8,128)}), f32[2,64,512]{2,1,0:T(8,128)}) %all-reduce.6.cloned.1.call-update) | async-done | bytes 262160 | tf_op jit(solution)/shard_map/while/body/eval_jaxpr/psum | solution.py:85
  1508.6 44.0 %all-reduce.6.cloned.1.call-done = f32[2,64,512]{2,1,0:T(8,128)} async-done(((f32[2,64,512]{2,1,0:T(8,128)}), f32[2,64,512]{2,1,0:T(8,128)}) %all-reduce.6.cloned.1.call-update) | async-done | bytes 262160 | tf_op jit(solution)/shard_map/while/body/eval_jaxpr/psum | solution.py:85
  1569.0 43.7 %all-reduce.6.cloned.1.call-done = f32[2,64,512]{2,1,0:T(8,128)} async-done(((f32[2,64,512]{2,1,0:T(8,128)}), f32[2,64,512]{2,1,0:T(8,128)}) %all-reduce.6.cloned.1.call-update) | async-done | bytes 262160 | tf_op jit(solution)/shard_map/while/body/eval_jaxpr/psum | solution.py:85
  1629.1 43.7 %all-reduce.6.cloned.1.call-done = f32[2,64,512]{2,1,0:T(8,128)} async-done(((f32[2,64,512]{2,1,0:T(8,128)}), f32[2,64,512]{2,1,0:T(8,128)}) %all-reduce.6.cloned.1.call-update) | async-done | bytes 262160 | tf_op jit(solution)/shard_map/while/body/eval_jaxpr/psum | solution.py:85
  1689.3 44.0 %all-reduce.6.cloned.1.call-done = f32[2,64,512]{2,1,0:T(8,128)} async-done(((f32[2,64,512]{2,1,0:T(8,128)}), f32[2,64,512]{2,1,0:T(8,128)}) %all-reduce.6.cloned.1.call-update) | async-done | bytes 262160 | tf_op jit(solution)/shard_map/while/body/eval_jaxpr/psum | solution.py:85
  1749.8 44.0 %all-reduce.6.cloned.1.call-done = f32[2,64,512]{2,1,0:T(8,128)} async-done(((f32[2,64,512]{2,1,0:T(8,128)}), f32[2,64,512]{2,1,0:T(8,128)}) %all-reduce.6.cloned.1.call-update) | async-done | bytes 262160 | tf_op jit(solution)/shard_map/while/body/eval_jaxpr/psum | solution.py:85
  1810.2 43.7 %all-reduce.6.cloned.1.call-done = f32[2,64,512]{2,1,0:T(8,128)} async-done(((f32[2,64,512]{2,1,0:T(8,128)}), f32[2,64,512]{2,1,0:T(8,128)}) %all-reduce.6.cloned.1.call-update) | async-done | bytes 262160 | tf_op jit(solution)/shard_map/while/body/eval_jaxpr/psum | solution.py:85
  1870.3 44.0 %all-reduce.6.cloned.1.call-done = f32[2,64,512]{2,1,0:T(8,128)} async-done(((f32[2,64,512]{2,1,0:T(8,128)}), f32[2,64,512]{2,1,0:T(8,128)}) %all-reduce.6.cloned.1.call-update) | async-done | bytes 262160 | tf_op jit(solution)/shard_map/while/body/eval_jaxpr/psum | solution.py:85
  1930.8 44.0 %all-reduce.6.cloned.1.call-done = f32[2,64,512]{2,1,0:T(8,128)} async-done(((f32[2,64,512]{2,1,0:T(8,128)}), f32[2,64,512]{2,1,0:T(8,128)}) %all-reduce.6.cloned.1.call-update) | async-done | bytes 262160 | tf_op jit(solution)/shard_map/while/body/eval_jaxpr/psum | solution.py:85
  1991.3 43.7 %all-reduce.6.cloned.1.call-done = f32[2,64,512]{2,1,0:T(8,128)} async-done(((f32[2,64,512]{2,1,0:T(8,128)}), f32[2,64,512]{2,1,0:T(8,128)}) %all-reduce.6.cloned.1.call-update) | async-done | bytes 262160 | tf_op jit(solution)/shard_map/while/body/eval_jaxpr/psum | solution.py:85
  2051.4 44.0 %all-reduce.6.cloned.1.call-done = f32[2,64,512]{2,1,0:T(8,128)} async-done(((f32[2,64,512]{2,1,0:T(8,128)}), f32[2,64,512]{2,1,0:T(8,128)}) %all-reduce.6.cloned.1.call-update) | async-done | bytes 262160 | tf_op jit(solution)/shard_map/while/body/eval_jaxpr/psum | solution.py:85
  2111.9 44.0 %all-reduce.6.cloned.1.call-done = f32[2,64,512]{2,1,0:T(8,128)} async-done(((f32[2,64,512]{2,1,0:T(8,128)}), f32[2,64,512]{2,1,0:T(8,128)}) %all-reduce.6.cloned.1.call-update) | async-done | bytes 262160 | tf_op jit(solution)/shard_map/while/body/eval_jaxpr/psum | solution.py:85
  2172.3 43.7 %all-reduce.6.cloned.1.call-done = f32[2,64,512]{2,1,0:T(8,128)} async-done(((f32[2,64,512]{2,1,0:T(8,128)}), f32[2,64,512]{2,1,0:T(8,128)}) %all-reduce.6.cloned.1.call-update) | async-done | bytes 262160 | tf_op jit(solution)/shard_map/while/body/eval_jaxpr/psum | solution.py:85
  2232.5 43.7 %all-reduce.6.cloned.1.call-done = f32[2,64,512]{2,1,0:T(8,128)} async-done(((f32[2,64,512]{2,1,0:T(8,128)}), f32[2,64,512]{2,1,0:T(8,128)}) %all-reduce.6.cloned.1.call-update) | async-done | bytes 262160 | tf_op jit(solution)/shard_map/while/body/eval_jaxpr/psum | solution.py:85
  2292.6 44.0 %all-reduce.6.cloned.1.call-done = f32[2,64,512]{2,1,0:T(8,128)} async-done(((f32[2,64,512]{2,1,0:T(8,128)}), f32[2,64,512]{2,1,0:T(8,128)}) %all-reduce.6.cloned.1.call-update) | async-done | bytes 262160 | tf_op jit(solution)/shard_map/while/body/eval_jaxpr/psum | solution.py:85
  2353.0 43.7 %all-reduce.6.cloned.1.call-done = f32[2,64,512]{2,1,0:T(8,128)} async-done(((f32[2,64,512]{2,1,0:T(8,128)}), f32[2,64,512]{2,1,0:T(8,128)}) %all-reduce.6.cloned.1.call-update) | async-done | bytes 262160 | tf_op jit(solution)/shard_map/while/body/eval_jaxpr/psum | solution.py:85
  2413.2 44.0 %all-reduce.6.cloned.1.call-done = f32[2,64,512]{2,1,0:T(8,128)} async-done(((f32[2,64,512]{2,1,0:T(8,128)}), f32[2,64,512]{2,1,0:T(8,128)}) %all-reduce.6.cloned.1.call-update) | async-done | bytes 262160 | tf_op jit(solution)/shard_map/while/body/eval_jaxpr/psum | solution.py:85
  2680.2 113.1 %reduce-scatter.13.cloned.1.call-done = bf16[128,8192]{1,0:T(8,128)(2,1)} async-done(((bf16[1024,8192]{1,0:T(8,128)(2,1)}), bf16[128,8192]{1,0:T(8,128)(2,1)}) %reduce-scatter.13.cloned.1.call-update) | async-done | bytes 2097168
  (534 shorter events, 1425.5 us)
Async XLA Ops:
  101.2 56.9 %all-reduce.4.cloned.1.call-start = ((), (), s32[]{:S(2)}) async-start(), calls=%async_computation.6 | async-start | bytes 524288 | tf_op jit(solution)/shard_map/while/body/eval_jaxpr/psum | solution.py:58
  161.5 54.2 %all-reduce.4.cloned.1.call-start = ((), (), s32[]{:S(2)}) async-start(), calls=%async_computation.6 | async-start | bytes 524288 | tf_op jit(solution)/shard_map/while/body/eval_jaxpr/psum | solution.py:58
  219.0 54.2 %all-reduce.4.cloned.1.call-start = ((), (), s32[]{:S(2)}) async-start(), calls=%async_computation.6 | async-start | bytes 524288 | tf_op jit(solution)/shard_map/while/body/eval_jaxpr/psum | solution.py:58
  276.5 54.1 %all-reduce.4.cloned.1.call-start = ((), (), s32[]{:S(2)}) async-start(), calls=%async_computation.6 | async-start | bytes 524288 | tf_op jit(solution)/shard_map/while/body/eval_jaxpr/psum | solution.py:58
  334.0 54.3 %all-reduce.4.cloned.1.call-start = ((), (), s32[]{:S(2)}) async-start(), calls=%async_computation.6 | async-start | bytes 524288 | tf_op jit(solution)/shard_map/while/body/eval_jaxpr/psum | solution.py:58
  391.6 54.2 %all-reduce.4.cloned.1.call-start = ((), (), s32[]{:S(2)}) async-start(), calls=%async_computation.6 | async-start | bytes 524288 | tf_op jit(solution)/shard_map/while/body/eval_jaxpr/psum | solution.py:58
  449.1 54.2 %all-reduce.4.cloned.1.call-start = ((), (), s32[]{:S(2)}) async-start(), calls=%async_computation.6 | async-start | bytes 524288 | tf_op jit(solution)/shard_map/while/body/eval_jaxpr/psum | solution.py:58
  506.7 54.2 %all-reduce.4.cloned.1.call-start = ((), (), s32[]{:S(2)}) async-start(), calls=%async_computation.6 | async-start | bytes 524288 | tf_op jit(solution)/shard_map/while/body/eval_jaxpr/psum | solution.py:58
  564.2 54.2 %all-reduce.4.cloned.1.call-start = ((), (), s32[]{:S(2)}) async-start(), calls=%async_computation.6 | async-start | bytes 524288 | tf_op jit(solution)/shard_map/while/body/eval_jaxpr/psum | solution.py:58
  621.7 54.2 %all-reduce.4.cloned.1.call-start = ((), (), s32[]{:S(2)}) async-start(), calls=%async_computation.6 | async-start | bytes 524288 | tf_op jit(solution)/shard_map/while/body/eval_jaxpr/psum | solution.py:58
  679.2 54.2 %all-reduce.4.cloned.1.call-start = ((), (), s32[]{:S(2)}) async-start(), calls=%async_computation.6 | async-start | bytes 524288 | tf_op jit(solution)/shard_map/while/body/eval_jaxpr/psum | solution.py:58
  736.8 54.2 %all-reduce.4.cloned.1.call-start = ((), (), s32[]{:S(2)}) async-start(), calls=%async_computation.6 | async-start | bytes 524288 | tf_op jit(solution)/shard_map/while/body/eval_jaxpr/psum | solution.py:58
  794.3 54.2 %all-reduce.4.cloned.1.call-start = ((), (), s32[]{:S(2)}) async-start(), calls=%async_computation.6 | async-start | bytes 524288 | tf_op jit(solution)/shard_map/while/body/eval_jaxpr/psum | solution.py:58
  851.8 54.2 %all-reduce.4.cloned.1.call-start = ((), (), s32[]{:S(2)}) async-start(), calls=%async_computation.6 | async-start | bytes 524288 | tf_op jit(solution)/shard_map/while/body/eval_jaxpr/psum | solution.py:58
  909.3 54.2 %all-reduce.4.cloned.1.call-start = ((), (), s32[]{:S(2)}) async-start(), calls=%async_computation.6 | async-start | bytes 524288 | tf_op jit(solution)/shard_map/while/body/eval_jaxpr/psum | solution.py:58
  966.9 54.3 %all-reduce.4.cloned.1.call-start = ((), (), s32[]{:S(2)}) async-start(), calls=%async_computation.6 | async-start | bytes 524288 | tf_op jit(solution)/shard_map/while/body/eval_jaxpr/psum | solution.py:58
  1024.4 54.2 %all-reduce.4.cloned.1.call-start = ((), (), s32[]{:S(2)}) async-start(), calls=%async_computation.6 | async-start | bytes 524288 | tf_op jit(solution)/shard_map/while/body/eval_jaxpr/psum | solution.py:58
  1082.0 54.2 %all-reduce.4.cloned.1.call-start = ((), (), s32[]{:S(2)}) async-start(), calls=%async_computation.6 | async-start | bytes 524288 | tf_op jit(solution)/shard_map/while/body/eval_jaxpr/psum | solution.py:58
  1139.5 54.2 %all-reduce.4.cloned.1.call-start = ((), (), s32[]{:S(2)}) async-start(), calls=%async_computation.6 | async-start | bytes 524288 | tf_op jit(solution)/shard_map/while/body/eval_jaxpr/psum | solution.py:58
  1197.1 54.2 %all-reduce.4.cloned.1.call-start = ((), (), s32[]{:S(2)}) async-start(), calls=%async_computation.6 | async-start | bytes 524288 | tf_op jit(solution)/shard_map/while/body/eval_jaxpr/psum | solution.py:58
  1263.6 47.5 %all-reduce.6.cloned.1.call-start = ((), (), s32[]{:S(2)}) async-start(), calls=%async_computation.7 | async-start | bytes 524288 | tf_op jit(solution)/shard_map/while/body/eval_jaxpr/psum | solution.py:85
  1324.1 47.5 %all-reduce.6.cloned.1.call-start = ((), (), s32[]{:S(2)}) async-start(), calls=%async_computation.7 | async-start | bytes 524288 | tf_op jit(solution)/shard_map/while/body/eval_jaxpr/psum | solution.py:85
  1384.5 47.5 %all-reduce.6.cloned.1.call-start = ((), (), s32[]{:S(2)}) async-start(), calls=%async_computation.7 | async-start | bytes 524288 | tf_op jit(solution)/shard_map/while/body/eval_jaxpr/psum | solution.py:85
  1505.1 47.5 %all-reduce.6.cloned.1.call-start = ((), (), s32[]{:S(2)}) async-start(), calls=%async_computation.7 | async-start | bytes 524288 | tf_op jit(solution)/shard_map/while/body/eval_jaxpr/psum | solution.py:85
  1685.7 47.5 %all-reduce.6.cloned.1.call-start = ((), (), s32[]{:S(2)}) async-start(), calls=%async_computation.7 | async-start | bytes 524288 | tf_op jit(solution)/shard_map/while/body/eval_jaxpr/psum | solution.py:85
  1866.8 47.5 %all-reduce.6.cloned.1.call-start = ((), (), s32[]{:S(2)}) async-start(), calls=%async_computation.7 | async-start | bytes 524288 | tf_op jit(solution)/shard_map/while/body/eval_jaxpr/psum | solution.py:85
  2047.9 47.5 %all-reduce.6.cloned.1.call-start = ((), (), s32[]{:S(2)}) async-start(), calls=%async_computation.7 | async-start | bytes 524288 | tf_op jit(solution)/shard_map/while/body/eval_jaxpr/psum | solution.py:85
  2108.4 47.5 %all-reduce.6.cloned.1.call-start = ((), (), s32[]{:S(2)}) async-start(), calls=%async_computation.7 | async-start | bytes 524288 | tf_op jit(solution)/shard_map/while/body/eval_jaxpr/psum | solution.py:85
  2289.1 47.5 %all-reduce.6.cloned.1.call-start = ((), (), s32[]{:S(2)}) async-start(), calls=%async_computation.7 | async-start | bytes 524288 | tf_op jit(solution)/shard_map/while/body/eval_jaxpr/psum | solution.py:85
  2470.1 206.4 %reduce-scatter.11.cloned.1.call-start = ((), (), s32[]{:S(2)}) async-start(), calls=%async_computation.4 | async-start | bytes 1638400
  2496.0 182.4 %reduce-scatter.9.cloned.1.call-start = ((), (), s32[]{:S(2)}) async-start(), calls=%async_computation.3 | async-start | bytes 2359296 | tf_op jit(solution)/shard_map/reduce_scatter | solution.py:156
  2503.8 289.6 %reduce-scatter.13.cloned.1.call-start = ((), (), s32[]{:S(2)}) async-start(), calls=%async_computation.5 | async-start | bytes 18874368
  (18 other events, 591.9 us)
Sparse Core Ops, SparseCore 0:
  112.5 45.6 all-reduce.3
  172.7 42.9 all-reduce.3
  230.2 42.9 all-reduce.3
  287.7 42.9 all-reduce.3
  345.3 42.9 all-reduce.3
  402.9 42.9 all-reduce.3
  460.4 42.9 all-reduce.3
  517.9 42.9 all-reduce.3
  575.5 42.9 all-reduce.3
  632.9 42.9 all-reduce.3
  690.5 42.9 all-reduce.3
  748.0 42.9 all-reduce.3
  805.5 42.9 all-reduce.3
  863.1 42.9 all-reduce.3
  920.6 42.9 all-reduce.3
  978.1 42.9 all-reduce.3
  1035.7 42.9 all-reduce.3
  1093.2 42.9 all-reduce.3
  1150.8 42.9 all-reduce.3
  1208.3 42.9 all-reduce.3
  1268.2 42.9 all-reduce.5
  1328.6 42.9 all-reduce.5
  1389.1 42.9 all-reduce.5
  1449.2 42.9 all-reduce.5
  1629.9 42.9 all-reduce.5
  1690.3 42.9 all-reduce.5
  1811.0 42.9 all-reduce.5
  1871.4 42.9 all-reduce.5
  2112.9 42.9 all-reduce.5
  2173.1 42.9 all-reduce.5
  2233.2 42.9 all-reduce.5
  2353.8 42.9 all-reduce.5
  (8 shorter events, 342.8 us)
Sparse Core Ops, SparseCore 1:
  2496.1 29.3 reduce-scatter.10
  2527.6 35.4 reduce-scatter.8
  2624.7 168.6 reduce-scatter.12
where the time goes:
time: 2820 us; the launch traced here: 2810 us
  waiting for transfers between devices  1820 us (65%)
  matrix products  455 us (16%)
  other arithmetic  243 us (9%)
  local copies, waits for them, and re-layouts  243 us (9%)
  blocking collectives  30.9 us (1%)
    psum x20, waiting for transfers between devices, backward_step(): recur_sum = lax.psum(recur_part, 'cols')  878 us
    psum x20, waiting for transfers between devices, forward_step(): proj_raw = lax.psum(partial_raw, 'cols')  828 us
    dot_general x20, matrix products, forward_step(): jnp.einsum('dwh,dhg->dwg', kept_hidden, w_recur, preferred_element_type=j...  139 us
    dynamic_update_slice x100, other arithmetic, per_device(): _, fwd_saved = lax.scan(forward_step, init_state, (input_gates, keep_stack))  131 us
    dot_general x20, matrix products, backward_step(): jnp.einsum('dwg,dhg->dwh', pre_grad, w_recur, preferred_element_type=jnp....  121 us
    unnamed x5, waiting for transfers between devices  113 us
  transfers between devices with their start and end apart: 43, of which 41 were waited for; matrix products, arithmetic and copies ran while one was open for 9% of the time, Pallas kernels for 0%

commit v1 on v0

--- a/solution.py
+++ b/solution.py
@@ -1,9 +1,19 @@
+import functools
+
 import jax
 import jax.numpy as jnp
 from jax import lax
+from jax.experimental import pallas as pl
+from jax.experimental.pallas import tpu as pltpu
 from jax.sharding import PartitionSpec as P
 
 STEPS = 20
+BF16 = jnp.bfloat16
+F32 = jnp.float32
+THIRD = 1.0 / 3.0
+LANES = 128
+BLOCKS = 4
+PARTS = 4
 
 
 def soft_clip(amount):
@@ -15,7 +25,7 @@
     return 1.0 - tangent * tangent
 
 
-def per_device(inputs, reset_flags, gate_weight, gate_bias, proj_weight, grad_out):
+def shared_cells(inputs, reset_flags, gate_weight, gate_bias, proj_weight, grad_out):
     tok_rows, model_width = inputs.shape
     windows = tok_rows // STEPS
     cell_cols = gate_weight.shape[3]
@@ -161,6 +171,535 @@
     return (block_out, input_grad, weight_share, bias_total, proj_share)
 
 
+def sigmoid(amount):
+    return 0.5 * jnp.tanh(0.5 * amount) + 0.5
+
+
+def whole(shape):
+    return pl.BlockSpec(shape, lambda *_: (0,) * len(shape), pipeline_mode=pl.Buffered(1))
+
+
+def matmul(a, b):
+    return jnp.dot(a, b, preferred_element_type=F32)
+
+
+def input_kernel(x_ref, w0, w1, w2, w3, bias_ref, out_ref):
+    width = w0.shape[1]
+    for n, w_ref in enumerate((w0, w1, w2, w3)):
+        at = n * width
+        out_ref[:, at : at + width] = (matmul(x_ref[...], w_ref[...]) + bias_ref[:, at : at + width]).astype(BF16)
+
+
+def input_gates(x, weights, bias):
+    rows, model = x.shape
+    width = weights[0].shape[1]
+    tile = rows // 4
+    return pl.pallas_call(
+        input_kernel,
+        grid=(4,),
+        out_shape=jax.ShapeDtypeStruct((rows, PARTS * width), BF16),
+        in_specs=[pl.BlockSpec((tile, model), lambda n: (n, 0))]
+        + [whole(w.shape) for w in weights]
+        + [whole(bias.shape)],
+        out_specs=pl.BlockSpec((tile, PARTS * width), lambda n: (n, 0)),
+        compiler_params=pltpu.CompilerParams(vmem_limit_bytes=32 * 2**20),
+        cost_estimate=pl.CostEstimate(
+            flops=2 * rows * model * PARTS * width,
+            bytes_accessed=2 * (rows + model) * PARTS * width,
+            transcendentals=0,
+        ),
+        name="input_gates",
+    )(x, *weights, bias)
+
+
+def forward_kernel(*refs):
+    px_refs, keep_ref = refs[:BLOCKS], refs[BLOCKS]
+    w_refs = refs[BLOCKS + 1 : BLOCKS + 1 + BLOCKS * PARTS]
+    p_refs = refs[BLOCKS + 1 + BLOCKS * PARTS : BLOCKS + 1 + 2 * BLOCKS * PARTS]
+    outs = refs[BLOCKS + 1 + 2 * BLOCKS * PARTS :]
+    pre_out, cell_out, emit_own, emit_far, raw_out, kept_out, hid_out, c_scr, h_scr = outs
+    step = pl.program_id(0)
+    piece, hidden = p_refs[0].shape
+    cells = piece * PARTS
+    tiles = piece // LANES
+    width = 4 * piece
+    half = cells // 2
+    rows = keep_ref.shape[1]
+
+    @pl.when(step == 0)
+    def _():
+        c_scr[...] = jnp.zeros_like(c_scr)
+        h_scr[...] = jnp.zeros_like(h_scr)
+
+    keep = keep_ref[0][:, :1]
+    kept = (h_scr[...] * keep).astype(BF16)
+    kept_out[0] = kept
+    raw = jnp.zeros((rows, hidden), F32)
+    for b in range(BLOCKS):
+        parts = []
+        for s in range(PARTS):
+            pre = px_refs[b][0, :, s * width : (s + 1) * width].astype(F32) + matmul(kept, w_refs[b * PARTS + s][...])
+            at = b * 4 * cells + s * width
+            pre_out[0, :, at : at + width] = pre.astype(BF16)
+            parts.append(pre)
+        gates = [
+            jnp.concatenate(
+                [part[:, (u * 4 + q) * LANES : (u * 4 + q + 1) * LANES] for part in parts for u in range(tiles)], axis=1
+            )
+            for q in range(4)
+        ]
+        i, f, u, o = sigmoid(gates[0]), sigmoid(gates[1]), jnp.tanh(gates[2]), sigmoid(gates[3])
+        at = b * cells
+        kept_cell = c_scr[:, at : at + cells] * keep
+        cell = 3.0 * jnp.tanh((f * kept_cell + i * u) * THIRD)
+        emit = (o * jnp.tanh(cell)).astype(BF16)
+        c_scr[:, at : at + cells] = cell
+        cell_out[0, :, at : at + cells] = cell
+        emit_own[0, :, b * half : (b + 1) * half] = emit[:, :half]
+        emit_far[0, :, b * half : (b + 1) * half] = emit[:, half:]
+        proj = jnp.concatenate([p_refs[b * PARTS + s][...] for s in range(PARTS)], axis=0)
+        raw = raw + matmul(emit, proj)
+    raw_out[0] = raw
+    hid = 3.0 * jnp.tanh(raw * THIRD)
+    h_scr[...] = hid.astype(BF16).astype(F32)
+    hid_out[0] = hid.astype(BF16)
+
+
+def run_forward(px, keep, weights, projs):
+    steps, rows, wide = px[0].shape
+    hidden = projs[0].shape[1]
+    total = BLOCKS * wide // 4
+    block = lambda n: pl.BlockSpec((1, rows, n), lambda t: (t, 0, 0))
+    sizes = (4 * total, total, total // 2, total // 2, hidden, hidden, hidden)
+    kinds = (BF16, F32, BF16, BF16, F32, BF16, BF16)
+    return pl.pallas_call(
+        forward_kernel,
+        grid=(steps,),
+        out_shape=tuple(jax.ShapeDtypeStruct((steps, rows, n), kind) for n, kind in zip(sizes, kinds)),
+        in_specs=[block(wide)] * BLOCKS + [block(LANES)] + [whole(w.shape) for w in weights + projs],
+        out_specs=tuple(block(n) for n in sizes),
+        scratch_shapes=[pltpu.VMEM((rows, total), F32), pltpu.VMEM((rows, hidden), F32)],
+        compiler_params=pltpu.CompilerParams(vmem_limit_bytes=48 * 2**20, dimension_semantics=("arbitrary",)),
+        cost_estimate=pl.CostEstimate(
+            flops=2 * steps * rows * hidden * 5 * total * 8,
+            bytes_accessed=steps * rows * total * 24 + 10 * total * hidden,
+            transcendentals=steps * rows * total * 6,
+        ),
+        name="forward_chain",
+    )(*px, keep, *weights, *projs)
+
+
+def backward_kernel(*refs):
+    pre_ref, cell_ref, before_ref, raw_ref, grad_ref, keep_ref = refs[:6]
+    wt_refs, pt_refs = refs[6 : 6 + BLOCKS * PARTS], refs[6 + BLOCKS * PARTS : 6 + 2 * BLOCKS * PARTS]
+    outs = refs[6 + 2 * BLOCKS * PARTS :]
+    slabs, draw_out, bias_out, dc_scr, dk_scr = outs[: 4 * BLOCKS], *outs[4 * BLOCKS :]
+    step = pl.program_id(0)
+    hidden, piece = pt_refs[0].shape
+    cells = piece * PARTS
+    tiles = piece // LANES
+    width = 4 * piece
+    chunk = 4 * LANES
+    rows = keep_ref.shape[1]
+
+    @pl.when(step == 0)
+    def _():
+        dc_scr[...] = jnp.zeros_like(dc_scr)
+        dk_scr[...] = jnp.zeros_like(dk_scr)
+        bias_out[...] = jnp.zeros_like(bias_out)
+
+    keep = keep_ref[0][:, :1]
+    tangent = jnp.tanh(raw_ref[0] * THIRD)
+    draw = ((grad_ref[0].astype(F32) + dk_scr[...]) * (1.0 - tangent * tangent)).astype(BF16)
+    draw_out[0] = draw
+    dk = jnp.zeros((rows, hidden), F32)
+    for b in range(BLOCKS):
+        at = b * cells
+        demit = matmul(draw, jnp.concatenate([pt_refs[b * PARTS + s][...] for s in range(PARTS)], axis=1))
+        gates = [
+            jnp.concatenate(
+                [
+                    pre_ref[0, :, 4 * at + s * width + (u * 4 + q) * LANES : 4 * at + s * width + (u * 4 + q + 1) * LANES]
+                    for s in range(PARTS)
+                    for u in range(tiles)
+                ],
+                axis=1,
+            ).astype(F32)
+            for q in range(4)
+        ]
+        i, f, u, o = sigmoid(gates[0]), sigmoid(gates[1]), jnp.tanh(gates[2]), sigmoid(gates[3])
+        cell = cell_ref[0, :, at : at + cells]
+        kept_cell = before_ref[0, :, at : at + cells] * keep
+        tanh_cell = jnp.tanh(cell)
+        third = cell * THIRD
+        dcell = (dc_scr[:, at : at + cells] + demit * o * (1.0 - tanh_cell * tanh_cell)) * (1.0 - third * third)
+        dgates = (
+            dcell * u * i * (1.0 - i),
+            dcell * kept_cell * f * (1.0 - f),
+            dcell * i * (1.0 - u * u),
+            demit * tanh_cell * o * (1.0 - o),
+        )
+        dc_scr[:, at : at + cells] = dcell * f * keep
+        for q in range(4):
+            folded = dgates[q][:8]
+            for r in range(8, rows, 8):
+                folded = folded + dgates[q][r : r + 8]
+            bias_out[:, (b * 4 + q) * cells : (b * 4 + q + 1) * cells] += folded
+        dgates = [dgate.astype(BF16) for dgate in dgates]
+        for s in range(PARTS):
+            part = jnp.concatenate(
+                [
+                    dgates[q][:, s * piece + u * LANES : s * piece + (u + 1) * LANES]
+                    for u in range(tiles)
+                    for q in range(4)
+                ],
+                axis=1,
+            )
+            side, quarter = s // 2, s % 2
+            for u in range(tiles):
+                slabs[(b * 2 + side) * 2 + u][0, :, quarter * chunk : (quarter + 1) * chunk] = part[
+                    :, u * chunk : (u + 1) * chunk
+                ]
+            dk = dk + matmul(part, wt_refs[b * PARTS + s][...])
+    dk_scr[...] = dk * keep
+
+
+def run_backward(pre, cell, raw, grad, keep, weights, projs):
+    steps, rows, gates = pre.shape
+    total = gates // 4
+    hidden, piece = projs[0].shape
+    width = 4 * piece
+    block = lambda n: pl.BlockSpec((1, rows, n), lambda s: (steps - 1 - s, 0, 0))
+    before = pl.BlockSpec((1, rows, total), lambda s: (jnp.maximum(steps - 2 - s, 0), 0, 0))
+    shape = lambda n: jax.ShapeDtypeStruct((steps, rows, n), BF16)
+    out = pl.pallas_call(
+        backward_kernel,
+        grid=(steps,),
+        out_shape=tuple([shape(width)] * (4 * BLOCKS) + [shape(hidden), jax.ShapeDtypeStruct((8, gates), F32)]),
+        in_specs=[block(gates), block(total), before, block(hidden), block(hidden), block(LANES)]
+        + [whole(w.shape) for w in weights + projs],
+        out_specs=tuple([block(width)] * (4 * BLOCKS) + [block(hidden), pl.BlockSpec((8, gates), lambda s: (0, 0))]),
+        scratch_shapes=[pltpu.VMEM((rows, total), F32), pltpu.VMEM((rows, hidden), F32)],
+        compiler_params=pltpu.CompilerParams(vmem_limit_bytes=48 * 2**20, dimension_semantics=("arbitrary",)),
+        cost_estimate=pl.CostEstimate(
+            flops=2 * steps * rows * hidden * 5 * total * 8,
+            bytes_accessed=steps * rows * total * 24 + 10 * total * hidden,
+            transcendentals=steps * rows * total * 6,
+        ),
+        name="backward_chain",
+    )(pre, cell, cell, raw, grad, keep, *weights, *projs)
+    slabs = [[[out[(b * 2 + side) * 2 + u] for u in range(2)] for side in range(2)] for b in range(BLOCKS)]
+    return slabs, out[4 * BLOCKS], out[4 * BLOCKS + 1]
+
+
+def slab_kernel(split, left_ref, draw_ref, own_ref, far_ref, e00, e01, e10, e11, *outs):
+    rows = own_ref.shape[0]
+    blocks = outs[0].shape[0] * (2 if split else 1)
+    depth = left_ref.shape[0] // blocks
+    lines = draw_ref.shape[0] // blocks
+    group = lines // 4
+    chunk = 4 * LANES
+    for quarter, (own_emit, far_emit) in enumerate(((e00, e10), (e01, e11))):
+        columns = slice(quarter * chunk, (quarter + 1) * chunk)
+        dw = matmul(left_ref[:, :rows], own_ref[:, columns]) + matmul(left_ref[:, rows:], far_ref[:, columns])
+        dp = matmul(draw_ref[:, :rows], own_emit[...]) + matmul(draw_ref[:, rows:], far_emit[...])
+        dw, dp = dw.astype(BF16), dp.astype(BF16)
+        for r in range(blocks):
+            if split:
+                out, to = outs[quarter * 2 + r // (blocks // 2)], r % (blocks // 2)
+            else:
+                out, to = outs[quarter], r
+            out[to, :depth, :] = dw[r * depth : (r + 1) * depth]
+            for g in range(4):
+                at = r * lines + g * group
+                out[to, depth : depth + group, g * LANES : (g + 1) * LANES] = dp[at : at + group]
+
+
+def slab_grads(split, left, draw, own, far, emit_own, emit_far, b, u):
+    rows, wide = own.shape
+    chunk = wide // 2
+    blocks = 8
+    lines = left.shape[0] // blocks + draw.shape[0] // blocks // 4
+    at = lambda quarter: (b * 2 + quarter) * 2 + u
+    emit = lambda quarter: pl.BlockSpec((rows, LANES), lambda n, quarter=quarter: (0, at(quarter)))
+    count = blocks // 2 if split else blocks
+    shape = (count, lines, chunk)
+    outs = 4 if split else 2
+    return pl.pallas_call(
+        functools.partial(slab_kernel, split),
+        grid=(1,),
+        out_shape=[jax.ShapeDtypeStruct(shape, BF16)] * outs,
+        in_specs=[whole(left.shape), whole(draw.shape), whole(own.shape), whole(far.shape)]
+        + [emit(0), emit(1), emit(0), emit(1)],
+        out_specs=[whole(shape)] * outs,
+        compiler_params=pltpu.CompilerParams(vmem_limit_bytes=40 * 2**20),
+        cost_estimate=pl.CostEstimate(
+            flops=4 * rows * wide * left.shape[0], bytes_accessed=4 * rows * wide + 4 * left.size, transcendentals=0
+        ),
+        name="weight_gradients",
+    )(left, draw, own, far, emit_own, emit_own, emit_far, emit_far)
+
+
+def input_grad_kernel(has_sum, *refs):
+    slab_refs, w_refs, out_ref = refs[:4], refs[4:8], refs[-1]
+    chunk = 4 * LANES
+    total = refs[8][...] if has_sum else None
+    for side in range(2):
+        for u in range(2):
+            for quarter in range(2):
+                part = lax.dot_general(
+                    slab_refs[side * 2 + u][:, quarter * chunk : (quarter + 1) * chunk],
+                    w_refs[side * 2 + quarter][:, u * chunk : (u + 1) * chunk],
+                    (((1,), (1,)), ((), ())),
+                    preferred_element_type=F32,
+                )
+                total = part if total is None else total + part
+    out_ref[...] = total
+
+
+def add_input_grad(slabs, weights, total):
+    rows = slabs[0].shape[0]
+    model, width = weights[0].shape
+    tile = rows // 4
+    operands = [*slabs, *weights] + ([] if total is None else [total])
+    lines = lambda n: pl.BlockSpec((tile, n), lambda s: (s, 0))
+    return pl.pallas_call(
+        functools.partial(input_grad_kernel, total is not None),
+        grid=(4,),
+        out_shape=jax.ShapeDtypeStruct((rows, model), F32),
+        in_specs=[lines(width)] * 4
+        + [whole(w.shape) for w in weights]
+        + ([] if total is None else [lines(model)]),
+        out_specs=lines(model),
+        compiler_params=pltpu.CompilerParams(vmem_limit_bytes=32 * 2**20),
+        cost_estimate=pl.CostEstimate(
+            flops=8 * rows * width * model, bytes_accessed=8 * rows * width, transcendentals=0
+        ),
+        name="input_gradient",
+    )(*operands)
+
+
+def after(value, *others):
+    return lax.optimization_barrier((value, *others))[0]
+
+
+def one_direction(inputs, reset_flags, gate_weight, gate_bias, proj_weight, grad_out):
+    row, col = lax.axis_index("rows"), lax.axis_index("cols")
+    layer, core = row // 2, row % 2
+    direction, pair = layer // 2, layer % 2
+    model = inputs.shape[1]
+    local = inputs.shape[0] // STEPS
+    share = local // 4
+    rows = 2 * share
+    cells = gate_weight.shape[3]
+    piece = cells // PARTS
+    width = 4 * piece
+    tiles = piece // LANES
+
+    def mask_of(r, near):
+        odd = (r // 2) % 2
+        return (2 if odd else 1) if near else (1 if odd else 2)
+
+    def over_chips(value, near):
+        pairs = [(r * 4 + j, r * 4 + (j ^ mask_of(r, near))) for r in range(8) for j in range(4)]
+        return lax.ppermute(value, ("rows", "cols"), pairs)
+
+    def over_rows(value, mask):
+        return lax.ppermute(value, "rows", [(r, r ^ mask) for r in range(8)])
+
+    core_swap = functools.partial(over_rows, mask=1)
+    pair_swap = functools.partial(over_rows, mask=2)
+    half_swap = functools.partial(over_rows, mask=4)
+    near_mask = jnp.where(pair == 0, 1, 2)
+    block_at = [col, col ^ near_mask, col ^ (3 - near_mask), col ^ 3]
+    by_dir = lambda pair_of: jnp.where(direction == 0, pair_of[0], pair_of[1])
+    by_other = lambda pair_of: jnp.where(direction == 0, pair_of[1], pair_of[0])
+    in_run = lambda value: jnp.where(direction == 0, value, value[::-1])
+
+    def cell_of(part):
+        return (core ^ (part // 2)) * (2 * piece) + (pair ^ (part % 2)) * piece
+
+    def own_gates(part, first):
+        w = lax.dynamic_slice(gate_weight, (direction, first, 0, cell_of(part)), (1, model, 4, piece))
+        w = w.reshape(model, 4, tiles, LANES)
+        return jnp.swapaxes(w, 1, 2).reshape(model, width)
+
+    w_in = [[None] * PARTS for _ in range(BLOCKS)]
+    w_rec = [[None] * PARTS for _ in range(BLOCKS)]
+    w_proj = [[None] * PARTS for _ in range(BLOCKS)]
+    for part in range(PARTS):
+        w_in[0][part] = own_gates(part, 0)
+        w_rec[0][part] = own_gates(part, model)
+        w_proj[0][part] = lax.dynamic_slice(proj_weight, (direction, cell_of(part), 0), (1, piece, model))[0]
+    for store in (w_in, w_rec, w_proj):
+        first = w_in is store
+        mine = store[0][0]
+        store[1][0] = over_chips(mine, True)
+        store[2][0] = over_chips(mine if first else after(mine, w_in[2][0]), False)
+        store[3][0] = over_chips(store[1][0], False)
+        store[1][1] = over_chips(after(store[0][1], store[1][0]), True)
+        store[2][1] = pair_swap(store[1][0])
+        store[3][1] = pair_swap(store[3][0])
+        for b in range(1, BLOCKS):
+            for part in range(2):
+                store[b][2 + part] = core_swap(store[b][part])
+
+    keep_grid = reset_flags.reshape(local, STEPS).astype(F32)
+    position = lax.broadcasted_iota(jnp.int32, (local, STEPS), 1)
+    keep_ahead = jnp.where(position > 0, 1.0 - keep_grid, 0.0)
+    next_flags = jnp.concatenate([keep_grid[:, 1:], jnp.zeros((local, 1), F32)], axis=1)
+    keep_behind = jnp.where(position < STEPS - 1, 1.0 - next_flags, 0.0)
+    mine = lambda value: lax.dynamic_slice_in_dim(value, col * share, share, 0)
+    steps_first = lambda value: jnp.swapaxes(value, 0, 1)
+    x_mine = steps_first(mine(inputs.reshape(local, STEPS, model)))
+    g_mine = mine(grad_out.reshape(local, STEPS, 2, model))
+    g_dirs = (steps_first(g_mine[:, :, 0]), steps_first(g_mine[:, :, 1]))
+    keep_dirs = (steps_first(mine(keep_ahead)), steps_first(mine(keep_behind)))
+    keep_wide = [jnp.broadcast_to(k[..., None], (STEPS, share, LANES)).astype(BF16) for k in keep_dirs]
+    xk_here = jnp.concatenate([x_mine, by_dir(keep_wide)], axis=2)
+    xk_sent = jnp.concatenate([x_mine, by_other(keep_wide)], axis=2)
+    xk = in_run(jnp.concatenate([xk_here, half_swap(xk_sent)], axis=1))
+    x_run, keep_run = xk[..., :model], xk[..., model:].astype(F32)
+    g_run = in_run(jnp.concatenate([by_dir(g_dirs), half_swap(after(by_other(g_dirs), xk))], axis=1))
+    x_flat = x_run.reshape(STEPS * rows, model)
+
+    bias_own = lax.dynamic_index_in_dim(gate_bias, direction, 0, keepdims=False)
+    bias_near = over_chips(bias_own, True)
+    bias_all = (bias_own, bias_near, over_chips(bias_own, False), over_chips(bias_near, False))
+
+    def bias_block(b):
+        tiled = bias_all[b].reshape(4, cells // LANES, LANES)
+        tiled = jnp.swapaxes(tiled, 0, 1).reshape(1, 4 * cells)
+        parts = [lax.dynamic_slice(tiled, (0, 4 * cell_of(part)), (1, width)) for part in range(PARTS)]
+        return jnp.concatenate(parts, axis=1)
+
+    px = [input_gates(x_flat, w_in[b], bias_block(b)).reshape(STEPS, rows, PARTS * width) for b in range(BLOCKS)]
+    ordered = lambda store: [store[b][part] for b in range(BLOCKS) for part in range(PARTS)]
+    turned = lambda store: [jnp.swapaxes(w, 0, 1) for w in ordered(store)]
+    pre, cell, emit_own, emit_far, raw, kept, hid = run_forward(px, keep_run, ordered(w_rec), ordered(w_proj))
+
+    hid_time = in_run(hid)
+    hid_here, hid_there = hid_time[:, :share], half_swap(hid_time[:, share:])
+    hid_both = (by_dir((hid_here, hid_there)), by_other((hid_here, hid_there)))
+    x_wide = x_mine.astype(F32)
+    out_mine = jnp.stack([(x_wide + h.astype(F32)).astype(BF16) for h in hid_both], axis=2)
+    out_mine = jnp.swapaxes(out_mine, 0, 1).reshape(share * STEPS, 2 * model)
+    out_near = over_chips(out_mine, True)
+    out_parts = (out_mine, out_near, over_chips(out_mine, False), over_chips(out_near, False))
+
+    def by_column(parts):
+        whole_rows = jnp.zeros((BLOCKS * parts[0].shape[0], parts[0].shape[1]), parts[0].dtype)
+        for b, value in enumerate(parts):
+            whole_rows = lax.dynamic_update_slice(whole_rows, value, (block_at[b] * value.shape[0], 0))
+        return whole_rows
+
+    block_out = by_column(out_parts).reshape(local * STEPS, 2, model)
+
+    flat = lambda value: value.reshape(STEPS * rows, value.shape[-1])
+    row_at = [
+        (((half ^ direction) * 2 + (layer_of ^ pair)) * 2 + (side ^ core))
+        for layer_of in range(2)
+        for half in range(2)
+        for side in range(2)
+    ]
+
+    def turned_rows(value):
+        both = jnp.concatenate([value, core_swap(value)], axis=0)
+        blocked = jnp.swapaxes(both, 0, 1).reshape(8, value.shape[1] // 8, 2 * value.shape[0])
+        picked = [lax.dynamic_index_in_dim(blocked, at, 0, keepdims=False) for at in row_at]
+        return jnp.concatenate(picked, axis=0)
+
+    left = turned_rows(jnp.concatenate([x_flat, flat(kept)], axis=1))
+    emit_own, emit_far = flat(emit_own), core_swap(flat(emit_far))
+
+    slabs, draw, bias_sums = run_backward(pre, cell, raw, g_run, keep_run, turned(w_rec), turned(w_proj))
+
+    slabs = [[[flat(value) for value in side] for side in block] for block in slabs]
+    draw_turned = turned_rows(flat(draw))
+    moved = [[core_swap(slabs[b][1][u]) for u in range(2)] for b in range(BLOCKS)]
+
+    def grads(b, u, split):
+        return slab_grads(split, left, draw_turned, slabs[b][0][u], moved[b][u], emit_own, emit_far, b, u)
+
+    def add(first, *others):
+        total = first.astype(F32)
+        for other in others:
+            total = total + other.astype(F32)
+        return total.astype(BF16)
+
+    def pair_sums(mine_a, sent_a, mine_b, sent_b, met=None):
+        met = (mine_a, sent_a, mine_b, sent_b) if met is None else met
+        return add(mine_a, pair_swap(met[3])), add(mine_b, pair_swap(met[1]))
+
+    def chip_sums(opposite, near, other, own):
+        relay_a = over_chips(opposite[0], True)
+        relay_b = over_chips(opposite[1], False)
+        near_a = over_chips(near[0], True)
+        other_a = over_chips(add(other[0], relay_a), False)
+        near_b = over_chips(add(near[1], relay_b), True)
+        other_b = over_chips(other[1], False)
+        return (own[0], near_a, other_a), (own[1], near_b, other_b)
+
+    tile0 = [grads(b, 0, False) for b in (3, 1, 2, 0)]
+    sums0 = [add(*parts) for parts in chip_sums(*tile0)]
+    count = sums0[0].shape[0] // 2
+    sums0 = pair_sums(sums0[0][:count], sums0[0][count:], sums0[1][:count], sums0[1][count:])
+    opposite, near, other, own = [grads(b, 1, True) for b in (3, 1, 2, 0)]
+    tile1 = [pair_sums(*opposite), pair_sums(*near, met=other), pair_sums(*other, met=near), pair_sums(*own)]
+    sums1 = [add(*parts) for parts in chip_sums(*tile1)]
+
+    final = [[None] * 2 for _ in range(2)]
+    for u, sums in enumerate((sums0, sums1)):
+        for quarter in range(2):
+            value = sums[quarter]
+            here, there = value[:2], half_swap(value[2:])
+            both = jnp.stack([by_dir((here, there)), by_other((here, there))], axis=1)
+            kept_part, got_part = both[0], core_swap(both[1])
+            sides = [jnp.where(core == which, kept_part, got_part) for which in range(2)]
+            final[quarter][u] = jnp.stack(sides, axis=2)
+    depth = 2 * model // 8
+    quarters = [jnp.stack(final[quarter], axis=3) for quarter in range(2)]
+    ordered_quarters = (
+        jnp.where(pair == 0, quarters[0], quarters[1]),
+        jnp.where(pair == 0, quarters[1], quarters[0]),
+    )
+    full = jnp.stack(ordered_quarters, axis=3).reshape(2, -1, 2, 2, 2, 4, LANES)
+    weight_share = jnp.transpose(full[:, :depth], (0, 1, 5, 2, 3, 4, 6)).reshape(2, depth, 4, cells).astype(F32)
+    proj_share = jnp.transpose(full[:, depth:], (0, 2, 3, 4, 6, 5, 1)).reshape(2, cells, model // 8).astype(F32)
+
+    bias_parts = jnp.sum(bias_sums, axis=0).reshape(BLOCKS, 4, 2, 2 * piece)
+    bias_half = bias_parts[:, :, 0] + core_swap(bias_parts[:, :, 1])
+    bias_near = over_chips(bias_half[1], True)
+    bias_other = over_chips(bias_half[2], False)
+    bias_far = lax.ppermute(bias_half[3], "cols", [(j, j ^ 3) for j in range(4)])
+    bias_half = bias_half[0] + bias_near + bias_other + bias_far
+    bias_half = jnp.where(pair == 0, bias_half, jnp.concatenate([bias_half[:, piece:], bias_half[:, :piece]], axis=1))
+    bias_half = bias_half + pair_swap(bias_half)
+    bias_there = half_swap(bias_half)
+    bias_half = jnp.stack([by_dir((bias_half, bias_there)), by_other((bias_half, bias_there))])
+    bias_side = core_swap(bias_half)
+    bias_total = jnp.concatenate(
+        [jnp.where(core == which, bias_half, bias_side) for which in range(2)], axis=2
+    )
+
+    wide = None
+    for b in range(BLOCKS):
+        wide = add_input_grad([slabs[b][side][u] for side in range(2) for u in range(2)], w_in[b], wide)
+    dx = in_run(wide.reshape(STEPS, rows, model))
+    dx = dx[:, :share] + half_swap(dx[:, share:].astype(BF16)).astype(F32)
+    dx = (dx + g_dirs[0].astype(F32) + g_dirs[1].astype(F32)).astype(BF16)
+    dx = jnp.swapaxes(dx, 0, 1).reshape(share * STEPS, model)
+    slice_for = lambda at: lax.dynamic_slice_in_dim(dx, at * (model // 4), model // 4, 1)
+    dx_parts = (
+        slice_for(block_at[0]),
+        over_chips(slice_for(block_at[1]), True),
+        over_chips(slice_for(block_at[2]), False),
+        lax.ppermute(slice_for(block_at[3]), "cols", [(j, j ^ 3) for j in range(4)]),
+    )
+    input_grad = by_column(dx_parts)
+    return (block_out, input_grad, weight_share, bias_total, proj_share)
+
+
 def solution(mesh):
     placed = (
         P("rows", None),
@@ -170,8 +709,9 @@
         P(None, "cols", None),
         P("rows", None, None),
     )
+    plan = one_direction if (mesh.shape["rows"], mesh.shape["cols"]) == (8, 4) else shared_cells
     return jax.shard_map(
-        per_device,
+        plan,
         mesh=mesh,
         in_specs=placed,
         out_specs=(

time: 2820 us -> 857 us (0.30)
  waiting for transfers between devices: 1820 us -> 282 us
  matrix products: 455 us -> 0 us
  Pallas kernels: 0 us -> 284 us
  other arithmetic: 243 us -> 35 us
  starting transfers between devices: 0.18 us -> 68.7 us
  local copies, waits for them, and re-layouts: 243 us -> 178 us
  blocking collectives: 30.9 us -> 0 us
    psum x40 -> x0, waiting for transfers between devices: 1710 us -> none  [the longest x20 878 us: backward_step(): recur_sum = lax.psum(recur_part, 'cols')]
    dot_general x85 -> x0, matrix products: 455 us -> none  [the longest x20 139 us: forward_step(): jnp.einsum('dwh,dhg->dwg', kept_hidden, w_recur, preferred_element_type=j...]
    pallas_call x0 -> x18, Pallas kernels: none -> 284 us  [the longest x1 97.5 us: run_backward(): pl.pallas_call(backward_kernel, grid=(steps,), out_shape=tuple([shape(wid...]
    ppermute x0 -> x97, waiting for transfers between devices: none -> 282 us  [the longest x61 204 us: over_rows(): return lax.ppermute(value, 'rows', [(r, r ^ mask) for r in range(8)])]
    dynamic_update_slice x120 -> x0, other arithmetic: 152 us -> none  [the longest x100 131 us: per_device(): _, fwd_saved = lax.scan(forward_step, init_state, (input_gates, keep_stack))]
    unnamed x5 -> x0, waiting for transfers between devices: 113 us -> none
    ppermute x0 -> x97, starting transfers between devices: none -> 68.7 us  [the longest x34 38.7 us: over_chips(): return lax.ppermute(value, ('rows', 'cols'), pairs)]
    ppermute x0 -> x24, local copies, waits for them, and re-layouts: none -> 43.2 us  [the longest x16 29.7 us: over_rows(): return lax.ppermute(value, 'rows', [(r, r ^ mask) for r in range(8)])]
  transfers between devices with their start and end apart: 43 -> 97, of which waited for: 41 -> 37; matrix products, arithmetic and copies ran while one was open for 9% -> 18% of each run, Pallas kernels for 0% -> 11%
where the time goes in v1:
time: 857 us; the launch traced here: 851 us
  Pallas kernels  284 us (33%)
  waiting for transfers between devices  282 us (33%)
  local copies, waits for them, and re-layouts  178 us (21%)
  starting transfers between devices  68.7 us (8%)
  other arithmetic  35 us (4%)
    ppermute x61, waiting for transfers between devices, over_rows(): return lax.ppermute(value, 'rows', [(r, r ^ mask) for r in range(8)])  204 us
    pallas_call x1, Pallas kernels, run_backward(): pl.pallas_call(backward_kernel, grid=(steps,), out_shape=tuple([shape(wid...  97.5 us
    pallas_call x1, Pallas kernels, run_forward(): pl.pallas_call(forward_kernel, grid=(steps,), out_shape=tuple((jax.ShapeD...  85.5 us
    ppermute x34, waiting for transfers between devices, over_chips(): return lax.ppermute(value, ('rows', 'cols'), pairs)  73.3 us
    unnamed x269, local copies, waits for them, and re-layouts  50.4 us
    pallas_call x8, Pallas kernels, slab_grads(): pl.pallas_call(functools.partial(slab_kernel, split), grid=(1,), out_shap...  47.5 us
    ppermute x34, starting transfers between devices, over_chips(): return lax.ppermute(value, ('rows', 'cols'), pairs)  38.7 us
    pallas_call x4, Pallas kernels, add_input_grad(): pl.pallas_call(functools.partial(input_grad_kernel, total is not None), g...  32.8 us
  transfers between devices with their start and end apart: 97, of which 37 were waited for; matrix products, arithmetic and copies ran while one was open for 18% of the time, Pallas kernels for 11%

profile of v1, /device:TPU:0, one launch (start us, length us, event | category | flops | bytes accessed | tf_op | source)
XLA Modules:
  0.0 850.9 jit_solution(1182625994817439588)
XLA Ops:
  5.2 7.1 constant_dynamic-slice_fusion.9
  44.0 11.6 %collective-permute-done.15 = f32[4,1024]{1,0:T(4,128)S(1)} collective-permute-done((f32[4,1024]{1,0:T(4,128)S(1)}, f32[4,1024]{1,0:T(4,128)S(1)}, u32[]{:S(2)}, u32[]{:S(2)}) %collective-permute-start.15) | collective-permute-done | bytes 16416 | tf_op jit(solution)/shard_map/ppermute | solution.py:505
  64.9 11.9 %collective-permute-done.44 = bf16[20,16,512]{2,1,0:T(8,128)(2,1)S(1)} collective-permute-done((bf16[20,16,512]{2,1,0:T(8,128)(2,1)S(1)}, bf16[20,16,512]{2,1,0:T(8,128)(2,1)S(1)}, u32[]{:S(2)}, u32[]{:S(2)}) %collective-permute-start.44) | collective-permute-done | bytes 327712 | tf_op jit(solution)/shard_map/ppermute | solution.py:508
  100.5 7.3 collective-permute-done.7.w1.refs_5_
  135.9 9.4 %collective-permute-done.2.w1.refs_5_ = bf16[512,1024]{1,0:T(8,128)(2,1)} collective-permute-done((bf16[512,1024]{1,0:T(8,128)(2,1)S(1)}, bf16[512,1024]{1,0:T(8,128)(2,1)}, u32[]{:S(2)}, u32[]{:S(2)}) %collective-permute-start.2) | collective-permute-done | bytes 1048608 | tf_op jit(solution)/shard_map/ppermute | solution.py:505
  148.5 13.0 %collective-permute-done.12.w1.refs_5_ = bf16[512,1024]{1,0:T(8,128)(2,1)} collective-permute-done((bf16[512,1024]{1,0:T(8,128)(2,1)}, bf16[512,1024]{1,0:T(8,128)(2,1)}, u32[]{:S(2)}, u32[]{:S(2)}) %collective-permute-start.12) | collective-permute-done | bytes 1048608 | tf_op jit(solution)/shard_map/ppermute | solution.py:508
  174.2 9.4 %collective-permute-done.25 = bf16[512,1024]{0,1:T(8,128)(2,1)} collective-permute-done((bf16[512,1024]{0,1:T(8,128)(2,1)}, bf16[512,1024]{0,1:T(8,128)(2,1)}, u32[]{:S(2)}, u32[]{:S(2)}) %collective-permute-start.25) | collective-permute-done | bytes 1048608 | tf_op jit(solution)/shard_map/ppermute | solution.py:508
  255.8 85.5 %forward_chain.1 = (bf16[20,32,16384]{2,1,0:T(8,128)(2,1)}, f32[20,32,4096]{2,1,0:T(8,128)}, bf16[20,32,2048]{2,1,0:T(8,128)(2,1)}, bf16[20,32,2048]{2,1,0:T(8,1...) custom-call(bf16[20,32,4096]{2,1,0:T(8,128)(2,1)} %bitcast.338, ...), custom_call_target="tpu_custom_call" | custom-call | flops 107374182400 | bytes 83886080 | tf_op jit(solution)/shard_map/forward_chain/pallas_call | solution.py:275
  342.2 97.5 %backward_chain.1 = (bf16[20,32,1024]{2,1,0:T(8,128)(2,1)}, bf16[20,32,1024]{2,1,0:T(8,128)(2,1)}, bf16[20,32,1024]{2,1,0:T(8,128)(2,1)}, bf16[20,32,1024]{2,1,0...) custom-call(bf16[20,32,16384]{2,1,0:T(8,128)(2,1)} %get-tuple-elemen, ...), custom_call_target="tpu_custom_call" | custom-call | flops 107374182400 | bytes 83886080 | tf_op jit(solution)/shard_map/backward_chain/pallas_call | solution.py:375
  450.7 7.3 input_gradient.4.refs_8_
  458.1 8.5 %input_gradient.5.refs_8_ = f32[640,512]{1,0:T(8,128)S(1)} custom-call(bf16[640,1024]{1,0:T(8,128)(2,1)S(1)} %bitcast.332, bf16[640,1024]{1,0:T(8,128)(2,1)S(1)} %bitcast.322, bf16[640,1024]{1,0:T(8,128)(2,1)S(1)} %bitcast.348, bf16[640,1024]{1,0:T(8,128)(2,1)S(1)} %bitcast.346, bf16[512,1024]{1,0:T(8,128)(2,1)} %collective-permute-done.1.w0.refs_4_, ...), custom_call_target="tpu_custom_call" | custom-call | flops 2684354560 | bytes 5242880 | tf_op jit(solution)/shard_map/input_gradient/pallas_call | solution.py:466
  466.7 8.3 input_gradient.6.refs_8_
  483.3 8.6 %input_gradient.7 = f32[640,512]{1,0:T(8,128)S(1)} custom-call(bf16[640,1024]{1,0:T(8,128)(2,1)S(1)} %bitcast.330, bf16[640,1024]{1,0:T(8,128)(2,1)S(1)} %bitcast.326, bf16[640,1024]{1,0:T(8,128)(2,1)} %bitcast.99.refs_2_, bf16[640,1024]{1,0:T(8,128)(2,1)} %bitcast.100.refs_3_, bf16[512,1024]{1,0:T(8,128)(2,1)} %collective-permute-done.11.w0.refs_4_, ...), custom_call_target="tpu_custom_call" | custom-call | flops 2684354560 | bytes 5242880 | tf_op jit(solution)/shard_map/input_gradient/pallas_call | solution.py:466
  498.5 16.8 %collective-permute-done.45 = bf16[20,16,512]{2,1,0:T(8,128)(2,1)S(1)} collective-permute-done((bf16[20,16,512]{2,1,0:T(8,128)(2,1)S(1)}, bf16[20,16,512]{2,1,0:T(8,128)(2,1)S(1)}, u32[]{:S(2)}, u32[]{:S(2)}) %collective-permute-start.45) | collective-permute-done | bytes 327712 | tf_op jit(solution)/shard_map/ppermute | solution.py:508
  516.1 14.1 %collective-permute-done.40 = bf16[20,16,512]{2,1,0:T(8,128)(2,1)} collective-permute-done((bf16[20,16,512]{2,1,0:T(8,128)(2,1)S(1)}, bf16[20,16,512]{2,1,0:T(8,128)(2,1)}, u32[]{:S(2)}, u32[]{:S(2)}) %collective-permute-start.40) | collective-permute-done | bytes 327712 | tf_op jit(solution)/shard_map/ppermute | solution.py:508
  554.5 6.2 collective-permute-done.41
  600.7 6.3 weight_gradients.11
  613.6 6.3 weight_gradients.14
  621.6 6.4 weight_gradients.15
  656.5 6.9 collective-permute-done.83
  665.0 10.9 %collective-permute-done.86 = bf16[4,144,512]{2,1,0:T(8,128)(2,1)S(1)} collective-permute-done((bf16[4,144,512]{2,1,0:T(8,128)(2,1)}, bf16[4,144,512]{2,1,0:T(8,128)(2,1)S(1)}, u32[]{:S(2)}, u32[]{:S(2)}) %collective-permute-start.86) | collective-permute-done | bytes 589856 | tf_op jit(solution)/shard_map/ppermute | solution.py:508
  677.3 11.2 %collective-permute-done.71 = bf16[4,144,512]{2,1,0:T(8,128)(2,1)S(1)} collective-permute-done((bf16[4,144,512]{2,1,0:T(8,128)(2,1)}, bf16[4,144,512]{2,1,0:T(8,128)(2,1)S(1)}, u32[]{:S(2)}, u32[]{:S(2)}) %collective-permute-start.71) | collective-permute-done | bytes 589856 | tf_op jit(solution)/shard_map/ppermute | solution.py:508
  690.3 10.9 %collective-permute-done.82 = bf16[4,144,512]{2,1,0:T(8,128)(2,1)S(1)} collective-permute-done((bf16[4,144,512]{2,1,0:T(8,128)(2,1)S(1)}, bf16[4,144,512]{2,1,0:T(8,128)(2,1)S(1)}, u32[]{:S(2)}, u32[]{:S(2)}) %collective-permute-start.82) | collective-permute-done | bytes 589856 | tf_op jit(solution)/shard_map/ppermute | solution.py:508
  720.2 7.4 collective-permute-done.81
  729.1 25.2 %collective-permute-done.87 = bf16[4,144,512]{2,1,0:T(8,128)(2,1)S(1)} collective-permute-done((bf16[4,144,512]{2,1,0:T(8,128)(2,1)S(1)}, bf16[4,144,512]{2,1,0:T(8,128)(2,1)S(1)}, u32[]{:S(2)}, u32[]{:S(2)}) %collective-permute-start.87) | collective-permute-done | bytes 589856 | tf_op jit(solution)/shard_map/ppermute | solution.py:505
  759.3 9.6 %collective-permute-done.76 = bf16[2,144,512]{2,1,0:T(8,128)(2,1)S(1)} collective-permute-done((bf16[2,144,512]{2,1,0:T(8,128)(2,1)S(1)}, bf16[2,144,512]{2,1,0:T(8,128)(2,1)S(1)}, u32[]{:S(2)}, u32[]{:S(2)}) %collective-permute-start.76) | collective-permute-done | bytes 294944 | tf_op jit(solution)/shard_map/ppermute | solution.py:508
  772.1 10.1 %collective-permute-done.88 = bf16[2,144,512]{2,1,0:T(8,128)(2,1)S(1)} collective-permute-done((bf16[2,144,512]{2,1,0:T(8,128)(2,1)S(1)}, bf16[2,144,512]{2,1,0:T(8,128)(2,1)S(1)}, u32[]{:S(2)}, u32[]{:S(2)}) %collective-permute-start.88) | collective-permute-done | bytes 294944 | tf_op jit(solution)/shard_map/ppermute | solution.py:508
  783.2 9.3 %collective-permute-done.62 = bf16[4,144,512]{2,1,0:T(8,128)(2,1)S(1)} collective-permute-done((bf16[4,144,512]{2,1,0:T(8,128)(2,1)S(1)}, bf16[4,144,512]{2,1,0:T(8,128)(2,1)S(1)}, u32[]{:S(2)}, u32[]{:S(2)}) %collective-permute-start.62) | collective-permute-done | bytes 589856 | tf_op jit(solution)/shard_map/ppermute | solution.py:508
  792.8 18.4 %collective-permute-done.78 = bf16[4,144,512]{2,1,0:T(8,128)(2,1)S(1)} collective-permute-done((bf16[4,144,512]{2,1,0:T(8,128)(2,1)S(1)}, bf16[4,144,512]{2,1,0:T(8,128)(2,1)S(1)}, u32[]{:S(2)}, u32[]{:S(2)}) %collective-permute-start.78) | collective-permute-done | bytes 589856 | tf_op jit(solution)/shard_map/ppermute | solution.py:508
  811.7 15.2 %collective-permute-done.79 = bf16[2,144,512]{2,1,0:T(8,128)(2,1)S(1)} collective-permute-done((bf16[2,144,512]{2,1,0:T(8,128)(2,1)S(1)}, bf16[2,144,512]{2,1,0:T(8,128)(2,1)S(1)}, u32[]{:S(2)}, u32[]{:S(2)}) %collective-permute-start.79) | collective-permute-done | bytes 294944 | tf_op jit(solution)/shard_map/ppermute | solution.py:508
  836.3 7.4 copy.125
  843.7 7.0 reshape.390
  (608 shorter events, 356.9 us)
Async XLA Ops:
  14.1 49.2 %collective-permute-start.1 = (bf16[512,1024]{1,0:T(8,128)(2,1)S(1)}, bf16[512,1024]{1,0:T(8,128)(2,1)}, u32[]{:S(2)}, u32[]{:S(2)}) collective-permute-start(bf16[512,1024]{1,0:T(8,128)(2,1)S(1)} %reshape.335.w0.refs_4_), channel_id=1, source_target_pairs={{0,1},{1,0},{2,3},{3,2},{4,5},{5,4},{6,7},{7,6},{8,10},{9,11},{10,... | collective-permute-start | bytes 3145736 | tf_op jit(solution)/shard_map/ppermute | solution.py:505
  25.9 51.6 %collective-permute-start.6 = (bf16[512,1024]{1,0:T(8,128)(2,1)S(1)}, bf16[512,1024]{1,0:T(8,128)(2,1)}, u32[]{:S(2)}, u32[]{:S(2)}) collective-permute-start(bf16[512,1024]{1,0:T(8,128)(2,1)S(1)} %reshape.335.w0.refs_4_), channel_id=1, source_target_pairs={{0,2},{1,3},{2,0},{3,1},{4,6},{5,7},{6,4},{7,5},{8,9},{9,8},{10,11... | collective-permute-start | bytes 3145736 | tf_op jit(solution)/shard_map/ppermute | solution.py:505
  63.3 35.7 %collective-permute-start.11 = (bf16[512,1024]{1,0:T(8,128)(2,1)}, bf16[512,1024]{1,0:T(8,128)(2,1)}, u32[]{:S(2)}, u32[]{:S(2)}) collective-permute-start(bf16[512,1024]{1,0:T(8,128)(2,1)} %collective-permute-done.1.w0.refs_4_), channel_id=1, source_target_pairs={{0,2},{1,3},{2,0},{3,1},{4,6},{5,7},{6,4},{7,5},{8,9},{9,8},{10,11... | collective-permute-start | bytes 3145736 | tf_op jit(solution)/shard_map/ppermute | solution.py:505
  96.9 38.2 %collective-permute-start.17 = (bf16[512,1024]{0,1:T(8,128)(2,1)}, bf16[512,1024]{0,1:T(8,128)(2,1)}, u32[]{:S(2)}, u32[]{:S(2)}) collective-permute-start(bf16[512,1024]{0,1:T(8,128)(2,1)} %bitcast.391), channel_id=1, source_target_pairs={{0,1},{1,0},{2,3},{3,2},{4,5},{5,4},{6,7},{7,6},{8,10},{9,11},{10,... | collective-permute-start | bytes 3145736 | tf_op jit(solution)/shard_map/ppermute | solution.py:505
  98.7 36.5 %collective-permute-start.20 = (bf16[512,1024]{0,1:T(8,128)(2,1)}, bf16[512,1024]{0,1:T(8,128)(2,1)}, u32[]{:S(2)}, u32[]{:S(2)}) collective-permute-start(bf16[512,1024]{0,1:T(8,128)(2,1)} %bitcast.388), channel_id=1, source_target_pairs={{0,2},{1,3},{2,0},{3,1},{4,6},{5,7},{6,4},{7,5},{8,9},{9,8},{10,11... | collective-permute-start | bytes 3145736 | tf_op jit(solution)/shard_map/ppermute | solution.py:505
  99.0 46.3 %collective-permute-start.2 = (bf16[512,1024]{1,0:T(8,128)(2,1)S(1)}, bf16[512,1024]{1,0:T(8,128)(2,1)}, u32[]{:S(2)}, u32[]{:S(2)}) collective-permute-start(bf16[512,1024]{1,0:T(8,128)(2,1)S(1)} %reshape.337.w1.refs_5_), channel_id=1, source_target_pairs={{0,1},{1,0},{2,3},{3,2},{4,5},{5,4},{6,7},{7,6},{8,10},{9,11},{10,... | collective-permute-start | bytes 3145736 | tf_op jit(solution)/shard_map/ppermute | solution.py:505
  107.8 38.9 %collective-permute-start.24 = (bf16[512,1024]{0,1:T(8,128)(2,1)}, bf16[512,1024]{0,1:T(8,128)(2,1)}, u32[]{:S(2)}, u32[]{:S(2)}) collective-permute-start(bf16[512,1024]{0,1:T(8,128)(2,1)} %copy-done.119), channel_id=1, source_target_pairs={{0,2},{1,3},{2,0},{3,1},{4,6},{5,7},{6,4},{7,5},{8,9},{9,8},{10,11... | collective-permute-start | bytes 3145736 | tf_op jit(solution)/shard_map/ppermute | solution.py:505
  108.3 38.4 %collective-permute-start.21 = (bf16[512,1024]{0,1:T(8,128)(2,1)}, bf16[512,1024]{0,1:T(8,128)(2,1)}, u32[]{:S(2)}, u32[]{:S(2)}) collective-permute-start(bf16[512,1024]{0,1:T(8,128)(2,1)} %copy-done.119), channel_id=1, source_target_pairs={{0,8},{4,12},{8,0},{12,4},{16,24},{20,28},{24,16},{28,20},{1,9},{5... | collective-permute-start | bytes 3145736 | tf_op jit(solution)/shard_map/ppermute | solution.py:508
  147.3 36.3 %collective-permute-start.25 = (bf16[512,1024]{0,1:T(8,128)(2,1)}, bf16[512,1024]{0,1:T(8,128)(2,1)}, u32[]{:S(2)}, u32[]{:S(2)}) collective-permute-start(bf16[512,1024]{0,1:T(8,128)(2,1)} %collective-permute-done.24), channel_id=1, source_target_pairs={{0,8},{4,12},{8,0},{12,4},{16,24},{20,28},{24,16},{28,20},{1,9},{5... | collective-permute-start | bytes 3145736 | tf_op jit(solution)/shard_map/ppermute | solution.py:508
  165.1 71.9 %collective-permute-start.3 = (bf16[512,1024]{1,0:T(8,128)(2,1)}, bf16[512,1024]{1,0:T(8,128)(2,1)}, u32[]{:S(2)}, u32[]{:S(2)}) collective-permute-start(bf16[512,1024]{1,0:T(8,128)(2,1)} %collective-permute-done.1.w0.refs_4_), channel_id=1, source_target_pairs={{0,4},{4,0},{8,12},{12,8},{16,20},{20,16},{24,28},{28,24},{1,5},{5... | collective-permute-start | bytes 3145736 | tf_op jit(solution)/shard_map/ppermute | solution.py:508
  165.2 71.8 %collective-permute-start.4 = (bf16[512,1024]{1,0:T(8,128)(2,1)}, bf16[512,1024]{1,0:T(8,128)(2,1)}, u32[]{:S(2)}, u32[]{:S(2)}) collective-permute-start(bf16[512,1024]{1,0:T(8,128)(2,1)} %collective-permute-done.2.w1.refs_5_), channel_id=1, source_target_pairs={{0,4},{4,0},{8,12},{12,8},{16,20},{20,16},{24,28},{28,24},{1,5},{5... | collective-permute-start | bytes 3145736 | tf_op jit(solution)/shard_map/ppermute | solution.py:508
  183.6 63.8 %collective-permute-start.13 = (bf16[512,1024]{1,0:T(8,128)(2,1)}, bf16[512,1024]{1,0:T(8,128)(2,1)}, u32[]{:S(2)}, u32[]{:S(2)}) collective-permute-start(bf16[512,1024]{1,0:T(8,128)(2,1)} %collective-permute-done.11.w0.refs_4_), channel_id=1, source_target_pairs={{0,4},{4,0},{8,12},{12,8},{16,20},{20,16},{24,28},{28,24},{1,5},{5... | collective-permute-start | bytes 3145736 | tf_op jit(solution)/shard_map/ppermute | solution.py:508
  183.6 63.8 %collective-permute-start.14 = (bf16[512,1024]{1,0:T(8,128)(2,1)}, bf16[512,1024]{1,0:T(8,128)(2,1)}, u32[]{:S(2)}, u32[]{:S(2)}) collective-permute-start(bf16[512,1024]{1,0:T(8,128)(2,1)} %collective-permute-done.12.w1.refs_5_), channel_id=1, source_target_pairs={{0,4},{4,0},{8,12},{12,8},{16,20},{20,16},{24,28},{28,24},{1,5},{5... | collective-permute-start | bytes 3145736 | tf_op jit(solution)/shard_map/ppermute | solution.py:508
  184.1 60.8 %collective-permute-start.27 = (bf16[512,1024]{0,1:T(8,128)(2,1)}, bf16[512,1024]{0,1:T(8,128)(2,1)}, u32[]{:S(2)}, u32[]{:S(2)}) collective-permute-start(bf16[512,1024]{0,1:T(8,128)(2,1)} %collective-permute-done.25), channel_id=1, source_target_pairs={{0,4},{4,0},{8,12},{12,8},{16,20},{20,16},{24,28},{28,24},{1,5},{5... | collective-permute-start | bytes 3145736 | tf_op jit(solution)/shard_map/ppermute | solution.py:508
  440.5 106.2 %collective-permute-start.50 = (bf16[640,512]{1,0:T(8,128)(2,1)}, bf16[640,512]{1,0:T(8,128)(2,1)}, u32[]{:S(2)}, u32[]{:S(2)}) collective-permute-start(bf16[640,512]{1,0:T(8,128)(2,1)} %bitcast.130), channel_id=1, source_target_pairs={{0,4},{4,0},{8,12},{12,8},{16,20},{20,16},{24,28},{28,24},{1,5},{5... | collective-permute-start | bytes 1966088 | tf_op jit(solution)/shard_map/ppermute | solution.py:508
  441.0 136.6 %collective-permute-start.53 = (bf16[640,1024]{1,0:T(8,128)(2,1)}, bf16[640,1024]{1,0:T(8,128)(2,1)}, u32[]{:S(2)}, u32[]{:S(2)}) collective-permute-start(bf16[640,1024]{1,0:T(8,128)(2,1)} %bitcast.347), channel_id=1, source_target_pairs={{0,4},{4,0},{8,12},{12,8},{16,20},{20,16},{24,28},{28,24},{1,5},{5... | collective-permute-start | bytes 3932168 | tf_op jit(solution)/shard_map/ppermute | solution.py:508
  479.9 85.3 %collective-permute-start.49 = (bf16[640,1024]{1,0:T(8,128)(2,1)}, bf16[640,1024]{1,0:T(8,128)(2,1)}, u32[]{:S(2)}, u32[]{:S(2)}) collective-permute-start(bf16[640,1024]{1,0:T(8,128)(2,1)} %pad_maximum_fusion), channel_id=1, source_target_pairs={{0,4},{4,0},{8,12},{12,8},{16,20},{20,16},{24,28},{28,24},{1,5},{5... | collective-permute-start | bytes 3932168 | tf_op jit(solution)/shard_map/ppermute | solution.py:508
  480.4 108.5 %collective-permute-start.52 = (bf16[640,2048]{1,0:T(8,128)(2,1)}, bf16[640,2048]{1,0:T(8,128)(2,1)}, u32[]{:S(2)}, u32[]{:S(2)}) collective-permute-start(bf16[640,2048]{1,0:T(8,128)(2,1)} %bitcast.142), channel_id=1, source_target_pairs={{0,4},{4,0},{8,12},{12,8},{16,20},{20,16},{24,28},{28,24},{1,5},{5... | collective-permute-start | bytes 7864328 | tf_op jit(solution)/shard_map/ppermute | solution.py:508
  562.7 37.9 %collective-permute-start.51 = (bf16[640,1024]{1,0:T(8,128)(2,1)}, bf16[640,1024]{1,0:T(8,128)(2,1)}, u32[]{:S(2)}, u32[]{:S(2)}) collective-permute-start(bf16[640,1024]{1,0:T(8,128)(2,1)} %bitcast.111.refs_2_), channel_id=1, source_target_pairs={{0,4},{4,0},{8,12},{12,8},{16,20},{20,16},{24,28},{28,24},{1,5},{5... | collective-permute-start | bytes 3932168 | tf_op jit(solution)/shard_map/ppermute | solution.py:508
  578.8 42.9 %collective-permute-start.72 = (bf16[640,1024]{1,0:T(8,128)(2,1)}, bf16[640,1024]{1,0:T(8,128)(2,1)}, u32[]{:S(2)}, u32[]{:S(2)}) collective-permute-start(bf16[640,1024]{1,0:T(8,128)(2,1)} %bitcast.100.refs_3_), channel_id=1, source_target_pairs={{0,4},{4,0},{8,12},{12,8},{16,20},{20,16},{24,28},{28,24},{1,5},{5... | collective-permute-start | bytes 3932168 | tf_op jit(solution)/shard_map/ppermute | solution.py:508
  582.1 47.7 %collective-permute-start.55 = (bf16[640,1024]{1,0:T(8,128)(2,1)}, bf16[640,1024]{1,0:T(8,128)(2,1)}, u32[]{:S(2)}, u32[]{:S(2)}) collective-permute-start(bf16[640,1024]{1,0:T(8,128)(2,1)} %bitcast.103.refs_2_), channel_id=1, source_target_pairs={{0,4},{4,0},{8,12},{12,8},{16,20},{20,16},{24,28},{28,24},{1,5},{5... | collective-permute-start | bytes 3932168 | tf_op jit(solution)/shard_map/ppermute | solution.py:508
  589.0 49.5 %collective-permute-start.67 = (bf16[640,1024]{1,0:T(8,128)(2,1)}, bf16[640,1024]{1,0:T(8,128)(2,1)S(1)}, u32[]{:S(2)}, u32[]{:S(2)}) collective-permute-start(bf16[640,1024]{1,0:T(8,128)(2,1)} %bitcast.345), channel_id=1, source_target_pairs={{0,4},{4,0},{8,12},{12,8},{16,20},{20,16},{24,28},{28,24},{1,5},{5... | collective-permute-start | bytes 3932168 | tf_op jit(solution)/shard_map/ppermute | solution.py:508
  600.6 44.3 %collective-permute-start.65 = (bf16[640,1024]{1,0:T(8,128)(2,1)S(1)}, bf16[640,1024]{1,0:T(8,128)(2,1)S(1)}, u32[]{:S(2)}, u32[]{:S(2)}) collective-permute-start(bf16[640,1024]{1,0:T(8,128)(2,1)S(1)} %bitcast.350), channel_id=1, source_target_pairs={{0,4},{4,0},{8,12},{12,8},{16,20},{20,16},{24,28},{28,24},{1,5},{5... | collective-permute-start | bytes 3932168 | tf_op jit(solution)/shard_map/ppermute | solution.py:508
  613.0 89.9 %collective-permute-start.59 = (bf16[8,144,512]{2,1,0:T(8,128)(2,1)}, bf16[8,144,512]{2,1,0:T(8,128)(2,1)}, u32[]{:S(2)}, u32[]{:S(2)}) collective-permute-start(bf16[8,144,512]{2,1,0:T(8,128)(2,1)} %get-tuple-element.96), channel_id=1, source_target_pairs={{0,2},{1,3},{2,0},{3,1},{4,6},{5,7},{6,4},{7,5},{8,9},{9,8},{10,11... | collective-permute-start | bytes 3538952 | tf_op jit(solution)/shard_map/ppermute | solution.py:505
  651.8 36.8 %collective-permute-start.71 = (bf16[4,144,512]{2,1,0:T(8,128)(2,1)}, bf16[4,144,512]{2,1,0:T(8,128)(2,1)S(1)}, u32[]{:S(2)}, u32[]{:S(2)}) collective-permute-start(bf16[4,144,512]{2,1,0:T(8,128)(2,1)} %get-tuple-element.103), channel_id=1, source_target_pairs={{0,8},{4,12},{8,0},{12,4},{16,24},{20,28},{24,16},{28,20},{1,9},{5... | collective-permute-start | bytes 1769480 | tf_op jit(solution)/shard_map/ppermute | solution.py:508
  663.4 49.9 %collective-permute-start.57 = (bf16[8,144,512]{2,1,0:T(8,128)(2,1)S(1)}, bf16[8,144,512]{2,1,0:T(8,128)(2,1)S(1)}, u32[]{:S(2)}, u32[]{:S(2)}) collective-permute-start(bf16[8,144,512]{2,1,0:T(8,128)(2,1)S(1)} %copy-done.104), channel_id=1, source_target_pairs={{0,1},{1,0},{2,3},{3,2},{4,5},{5,4},{6,7},{7,6},{8,10},{9,11},{10,... | collective-permute-start | bytes 3538952 | tf_op jit(solution)/shard_map/ppermute | solution.py:505
  705.1 64.0 %collective-permute-start.61 = (bf16[8,144,512]{2,1,0:T(8,128)(2,1)S(1)}, bf16[8,144,512]{2,1,0:T(8,128)(2,1)S(1)}, u32[]{:S(2)}, u32[]{:S(2)}) collective-permute-start(bf16[8,144,512]{2,1,0:T(8,128)(2,1)S(1)} %copy-done.102), channel_id=1, source_target_pairs={{0,2},{1,3},{2,0},{3,1},{4,6},{5,7},{6,4},{7,5},{8,9},{9,8},{10,11... | collective-permute-start | bytes 3538952 | tf_op jit(solution)/shard_map/ppermute | solution.py:505
  713.3 40.9 %collective-permute-start.87 = (bf16[4,144,512]{2,1,0:T(8,128)(2,1)S(1)}, bf16[4,144,512]{2,1,0:T(8,128)(2,1)S(1)}, u32[]{:S(2)}, u32[]{:S(2)}) collective-permute-start(bf16[4,144,512]{2,1,0:T(8,128)(2,1)S(1)} %add_convert_fusion.5), channel_id=1, source_target_pairs={{0,2},{1,3},{2,0},{3,1},{4,6},{5,7},{6,4},{7,5},{8,9},{9,8},{10,11... | collective-permute-start | bytes 1769480 | tf_op jit(solution)/shard_map/ppermute | solution.py:505
  714.9 54.2 %collective-permute-start.60 = (bf16[8,144,512]{2,1,0:T(8,128)(2,1)S(1)}, bf16[8,144,512]{2,1,0:T(8,128)(2,1)S(1)}, u32[]{:S(2)}, u32[]{:S(2)}) collective-permute-start(bf16[8,144,512]{2,1,0:T(8,128)(2,1)S(1)} %add_convert_fusion.1), channel_id=1, source_target_pairs={{0,1},{1,0},{2,3},{3,2},{4,5},{5,4},{6,7},{7,6},{8,10},{9,11},{10,... | collective-permute-start | bytes 3538952 | tf_op jit(solution)/shard_map/ppermute | solution.py:505
  719.1 37.4 %collective-permute-start.85 = (bf16[4,144,512]{2,1,0:T(8,128)(2,1)S(1)}, bf16[4,144,512]{2,1,0:T(8,128)(2,1)S(1)}, u32[]{:S(2)}, u32[]{:S(2)}) collective-permute-start(bf16[4,144,512]{2,1,0:T(8,128)(2,1)S(1)} %add_convert_fusion.6), channel_id=1, source_target_pairs={{0,1},{1,0},{2,3},{3,2},{4,5},{5,4},{6,7},{7,6},{8,10},{9,11},{10,... | collective-permute-start | bytes 1769480 | tf_op jit(solution)/shard_map/ppermute | solution.py:505
  727.6 54.7 %collective-permute-start.54 = (bf16[8,144,512]{2,1,0:T(8,128)(2,1)S(1)}, bf16[8,144,512]{2,1,0:T(8,128)(2,1)S(1)}, u32[]{:S(2)}, u32[]{:S(2)}) collective-permute-start(bf16[8,144,512]{2,1,0:T(8,128)(2,1)S(1)} %copy-done.100), channel_id=1, source_target_pairs={{0,1},{1,0},{2,3},{3,2},{4,5},{5,4},{6,7},{7,6},{8,10},{9,11},{10,... | collective-permute-start | bytes 3538952 | tf_op jit(solution)/shard_map/ppermute | solution.py:505
  783.1 44.5 %collective-permute-start.89 = (bf16[2,144,512]{2,1,0:T(8,128)(2,1)S(1)}, bf16[2,144,512]{2,1,0:T(8,128)(2,1)S(1)}, u32[]{:S(2)}, u32[]{:S(2)}) collective-permute-start(bf16[2,144,512]{2,1,0:T(8,128)(2,1)S(1)} %fusion.17), channel_id=1, source_target_pairs={{0,4},{4,0},{8,12},{12,8},{16,20},{20,16},{24,28},{28,24},{1,5},{5... | collective-permute-start | bytes 884744 | tf_op jit(solution)/shard_map/ppermute | solution.py:508
  (189 other events, 3560.0 us)

commit v2 on v1

v2 whole, which is shorter than its diff:
```python
import functools

import jax
import jax.numpy as jnp
from jax import lax
from jax.experimental import pallas as pl
from jax.experimental.pallas import tpu as pltpu
from jax.sharding import PartitionSpec as P

STEPS = 20
BF16 = jnp.bfloat16
F32 = jnp.float32
THIRD = 1.0 / 3.0
LANES = 128
BLOCKS = 4
LIGHT = pl.CostEstimate(flops=1, bytes_accessed=1, transcendentals=0)
PARTS = 4


def soft_clip(amount):
    return 3.0 * jnp.tanh(amount / 3.0)


def clip_slope(amount):
    tangent = jnp.tanh(amount / 3.0)
    return 1.0 - tangent * tangent


def shared_cells(inputs, reset_flags, gate_weight, gate_bias, proj_weight, grad_out):
    tok_rows, model_width = inputs.shape
    windows = tok_rows // STEPS
    cell_cols = gate_weight.shape[3]
    gate_width = 4 * cell_cols
    share_width = model_width // lax.axis_size("cols")
    column = lax.axis_index("cols") * share_width
    weight = gate_weight.reshape(2, 2 * model_width, gate_width)
    w_input = weight[:, :model_width]
    w_recur = weight[:, model_width:]
    bias_row = gate_bias.reshape(2, 1, gate_width)
    sequence = jnp.swapaxes(inputs.reshape(windows, STEPS, model_width), 0, 1)
    x_stack = jnp.stack([sequence, sequence[::-1]], axis=1)
    flag_grid = jnp.swapaxes(reset_flags.reshape(windows, STEPS), 0, 1).astype(jnp.float32)
    position = lax.broadcasted_iota(jnp.int32, (STEPS, windows), 0)
    keep_ahead = jnp.where(position > 0, 1.0 - flag_grid, 0.0)
    next_flags = jnp.concatenate([flag_grid[1:], jnp.zeros((1, windows), jnp.float32)], axis=0)
    keep_behind = jnp.where(position < STEPS - 1, 1.0 - next_flags, 0.0)
    keep_stack = jnp.stack([keep_ahead, keep_behind[::-1]], axis=1)[..., None]
    input_gates = jnp.einsum("sdwh,dhg->sdwg", x_stack, w_input, preferred_element_type=jnp.float32)

    def forward_step(state_pair, pieces):
        hidden, cell_prev = state_pair
        gates_in, keep_step = pieces
        kept_hidden = hidden * keep_step.astype(jnp.bfloat16)
        gate_pre = (
            gates_in
            + jnp.einsum("dwh,dhg->dwg", kept_hidden, w_recur, preferred_element_type=jnp.float32)
            + bias_row
        )
        in_gate = jax.nn.sigmoid(gate_pre[..., :cell_cols])
        forget = jax.nn.sigmoid(gate_pre[..., cell_cols : 2 * cell_cols])
        update = jnp.tanh(gate_pre[..., 2 * cell_cols : 3 * cell_cols])
        out_gate = jax.nn.sigmoid(gate_pre[..., 3 * cell_cols :])
        kept_cell = cell_prev * keep_step
        cell_new = soft_clip(forget * kept_cell + in_gate * update)
        cell_output = (out_gate * jnp.tanh(cell_new)).astype(jnp.bfloat16)
        partial_raw = jnp.einsum(
            "dwc,dch->dwh", cell_output, proj_weight, preferred_element_type=jnp.float32
        )
        proj_raw = lax.psum(partial_raw, "cols")
        new_hidden = soft_clip(proj_raw).astype(jnp.bfloat16)
        return (
            (new_hidden, cell_new),
            (kept_hidden, gate_pre, kept_cell, cell_new, cell_output, proj_raw, new_hidden),
        )

    init_state = (
        jnp.zeros((2, windows, model_width), jnp.bfloat16),
        jnp.zeros((2, windows, cell_cols), jnp.float32),
    )
    _, fwd_saved = lax.scan(forward_step, init_state, (input_gates, keep_stack))
    kept_all, pre_all, kept_cells, cell_states, cell_outputs, proj_raws, hiddens = fwd_saved
    ahead_hidden = hiddens[:, 0]
    behind_hidden = hiddens[::-1, 1]
    both_outputs = jnp.stack([ahead_hidden, behind_hidden], axis=2).astype(jnp.float32) + sequence[
        :, :, None, :
    ].astype(jnp.float32)
    block_out = (
        jnp.swapaxes(both_outputs, 0, 1).reshape(tok_rows, 2, model_width).astype(jnp.bfloat16)
    )
    out_grid = jnp.transpose(grad_out.reshape(windows, STEPS, 2, model_width), (1, 2, 0, 3))
    grad_stack = jnp.stack([out_grid[:, 0], out_grid[::-1, 1]], axis=1)

    def backward_step(state_pair, pieces):
        recur_part, cell_grad = state_pair
        gate_pre, kept_cell, cell_new, cell_output, proj_raw, grad_step, keep_step = pieces
        recur_sum = lax.psum(recur_part, "cols")
        hidden_grad = grad_step.astype(jnp.float32) + recur_sum
        raw_grad = (hidden_grad * clip_slope(proj_raw)).astype(jnp.bfloat16)
        emit_grad = jnp.einsum(
            "dwh,dch->dwc", raw_grad, proj_weight, preferred_element_type=jnp.float32
        )
        in_gate = jax.nn.sigmoid(gate_pre[..., :cell_cols])
        forget = jax.nn.sigmoid(gate_pre[..., cell_cols : 2 * cell_cols])
        update = jnp.tanh(gate_pre[..., 2 * cell_cols : 3 * cell_cols])
        out_gate = jax.nn.sigmoid(gate_pre[..., 3 * cell_cols :])
        tanh_cell = jnp.tanh(cell_new)
        cell_total = cell_grad + emit_grad * out_gate * (1.0 - tanh_cell * tanh_cell)
        cell_third = cell_new / 3.0
        cell_raw_grad = cell_total * (1.0 - cell_third * cell_third)
        pre_grad = jnp.concatenate(
            [
                cell_raw_grad * update * in_gate * (1.0 - in_gate),
                cell_raw_grad * kept_cell * forget * (1.0 - forget),
                cell_raw_grad * in_gate * (1.0 - update * update),
                emit_grad * tanh_cell * out_gate * (1.0 - out_gate),
            ],
            axis=-1,
        ).astype(jnp.bfloat16)
        recur_next = (
            jnp.einsum("dwg,dhg->dwh", pre_grad, w_recur, preferred_element_type=jnp.float32)
            * keep_step
        )
        cell_next = cell_raw_grad * forget * keep_step
        return ((recur_next, cell_next), (pre_grad, raw_grad))

    zero_state = (
        jnp.zeros((2, windows, model_width), jnp.float32),
        jnp.zeros((2, windows, cell_cols), jnp.float32),
    )
    _, back_saved = lax.scan(
        backward_step,
        zero_state,
        (pre_all, kept_cells, cell_states, cell_outputs, proj_raws, grad_stack, keep_stack),
        reverse=True,
    )
    pre_grads, raw_grads = back_saved
    input_part = jnp.einsum(
        "sdwg,dhg->sdwh", pre_grads, w_input, preferred_element_type=jnp.float32
    )
    input_sum = jnp.swapaxes(input_part[:, 0] + input_part[::-1, 1], 0, 1).reshape(
        tok_rows, model_width
    )
    input_share = lax.psum_scatter(
        input_sum.astype(jnp.bfloat16), "cols", scatter_dimension=1, tiled=True
    ).astype(jnp.float32)
    residual_grad = grad_out[:, 0].astype(jnp.float32) + grad_out[:, 1].astype(jnp.float32)
    input_grad = (
        input_share + lax.dynamic_slice_in_dim(residual_grad, column, share_width, 1)
    ).astype(jnp.bfloat16)
    input_weight_grad = jnp.einsum(
        "sdwh,sdwg->dhg", x_stack, pre_grads, preferred_element_type=jnp.float32
    )
    recur_weight_grad = jnp.einsum(
        "sdwh,sdwg->dhg", kept_all, pre_grads, preferred_element_type=jnp.float32
    )
    weight_grad = jnp.concatenate([input_weight_grad, recur_weight_grad], axis=1).reshape(
        2, 2 * model_width, 4, cell_cols
    )
    proj_grad = jnp.einsum(
        "sdwc,sdwh->dch", cell_outputs, raw_grads, preferred_element_type=jnp.float32
    )
    bias_grad = jnp.sum(pre_grads, axis=(0, 2), dtype=jnp.float32).reshape(2, 4, cell_cols)
    weight_share, proj_share = (
        lax.psum_scatter(
            weight_grad.astype(jnp.bfloat16), "rows", scatter_dimension=1, tiled=True
        ).astype(jnp.float32),
        lax.psum_scatter(
            proj_grad.astype(jnp.bfloat16), "rows", scatter_dimension=2, tiled=True
        ).astype(jnp.float32),
    )
    bias_total = lax.psum(bias_grad, "rows")
    return (block_out, input_grad, weight_share, bias_total, proj_share)


def sigmoid(amount):
    return 0.5 * jnp.tanh(0.5 * amount) + 0.5


def whole(shape):
    return pl.BlockSpec(shape, lambda *_: (0,) * len(shape), pipeline_mode=pl.Buffered(1))


def matmul(a, b):
    return jnp.dot(a, b, preferred_element_type=F32)


def own_piece_kernel(order_ref, w_ref, extra_ref, out_ref):
    step = pl.program_id(0)
    lines = w_ref.shape[1]
    model, width = extra_ref.shape[-1] if extra_ref.shape[1] > 4 else None, out_ref.shape[1]
    for u in range(2):
        for q in range(4):
            to = (u * 4 + q) * LANES
            out_ref[pl.ds(step * lines, lines), to : to + LANES] = w_ref[0, :, q, u * LANES : (u + 1) * LANES]
    base = width // 2

    @pl.when(step == 0)
    def _():
        if model is None:
            rest = jnp.concatenate(
                [extra_ref[0, q : q + 1, u * LANES : (u + 1) * LANES] for u in range(2) for q in range(4)], axis=1
            )
            parts = []
            for _ in range(3):
                parts.append(rest.astype(BF16).astype(F32))
                rest = rest - parts[-1]
            parts.append(jnp.zeros((13, width), F32))
            out_ref[base:, :] = jnp.concatenate(parts, axis=0).astype(BF16)
        else:
            half = extra_ref.shape[1] // 2
            out_ref[base:, :model] = extra_ref[0, :half, :]
            out_ref[base:, model:] = extra_ref[0, half:, :]


def own_piece(place, gate_weight, extra, recurrent, memory=16):
    model, piece = gate_weight.shape[1] // 2, gate_weight.shape[3] // PARTS
    cut = model // 4
    first = 4 if recurrent else 0
    if recurrent:
        extra_spec = pl.BlockSpec((1, piece, model), lambda n, p: (p[0], p[1], 0))
    else:
        extra_spec = pl.BlockSpec((1, 4, piece), lambda n, p: (p[0], 0, p[1]))
    lines = model + (piece // 2 if recurrent else 16)
    return pl.pallas_call(
        own_piece_kernel,
        grid_spec=pltpu.PrefetchScalarGridSpec(
            num_scalar_prefetch=1,
            grid=(4,),
            in_specs=[pl.BlockSpec((1, cut, 4, piece), lambda n, p: (p[0], n + first, 0, p[1])), extra_spec],
            out_specs=pl.BlockSpec((lines, 4 * piece), lambda n, p: (0, 0)),
        ),
        out_shape=jax.ShapeDtypeStruct((lines, 4 * piece), BF16),
        compiler_params=pltpu.CompilerParams(vmem_limit_bytes=memory * 2**20, dimension_semantics=("arbitrary",)),
        cost_estimate=LIGHT,
        name="own_piece",
    )(place, gate_weight, extra)


def input_kernel(x_ref, w0, w1, w2, w3, out_ref):
    model, width = x_ref.shape[1], w0.shape[1]
    for n, w_ref in enumerate((w0, w1, w2, w3)):
        bias = jnp.sum(w_ref[model:, :].astype(F32), axis=0, keepdims=True)
        out_ref[:, n * width : (n + 1) * width] = (matmul(x_ref[...], w_ref[:model, :]) + bias).astype(BF16)


def input_gates(x, weights):
    rows, model = x.shape
    width = weights[0].shape[1]
    tile = rows // 2
    return pl.pallas_call(
        input_kernel,
        grid=(2,),
        out_shape=jax.ShapeDtypeStruct((rows, PARTS * width), BF16),
        in_specs=[pl.BlockSpec((tile, model), lambda n: (n, 0))] + [whole(w.shape) for w in weights],
        out_specs=pl.BlockSpec((tile, PARTS * width), lambda n: (n, 0)),
        compiler_params=pltpu.CompilerParams(vmem_limit_bytes=20 * 2**20),
        cost_estimate=LIGHT,
        name="input_gates",
    )(x, *weights)


def forward_kernel(*refs):
    px_refs, keep_ref = refs[:BLOCKS], refs[BLOCKS]
    w_refs = refs[BLOCKS + 1 : BLOCKS + 1 + BLOCKS * PARTS]
    pre_out, cell_out, emit_own, emit_far, raw_out, kept_out, hid_out, c_scr, h_scr = refs[BLOCKS + 1 + BLOCKS * PARTS :]
    step = pl.program_id(0)
    width = w_refs[0].shape[1]
    hidden = width // 2
    piece = width // 4
    cells = piece * PARTS
    tiles = piece // LANES
    half = cells // 2
    rows = keep_ref.shape[1]

    @pl.when(step == 0)
    def _():
        c_scr[...] = jnp.zeros_like(c_scr)
        h_scr[...] = jnp.zeros_like(h_scr)

    keep = keep_ref[0][:, :1]
    kept = (h_scr[...] * keep).astype(BF16)
    kept_out[0] = kept
    raw = jnp.zeros((rows, hidden), F32)
    for b in range(BLOCKS):
        parts, proj = [], []
        for s in range(PARTS):
            w_ref = w_refs[b * PARTS + s]
            pre = px_refs[b][0, :, s * width : (s + 1) * width].astype(F32) + matmul(kept, w_ref[:hidden, :])
            at = b * 4 * cells + s * width
            pre_out[0, :, at : at + width] = pre.astype(BF16)
            parts.append(pre)
            proj += [w_ref[hidden:, :hidden], w_ref[hidden:, hidden:]]
        gates = [
            jnp.concatenate(
                [part[:, (u * 4 + q) * LANES : (u * 4 + q + 1) * LANES] for part in parts for u in range(tiles)], axis=1
            )
            for q in range(4)
        ]
        i, f, u, o = sigmoid(gates[0]), sigmoid(gates[1]), jnp.tanh(gates[2]), sigmoid(gates[3])
        at = b * cells
        kept_cell = c_scr[:, at : at + cells] * keep
        cell = 3.0 * jnp.tanh((f * kept_cell + i * u) * THIRD)
        emit = (o * jnp.tanh(cell)).astype(BF16)
        c_scr[:, at : at + cells] = cell
        cell_out[0, :, at : at + cells] = cell
        emit_own[0, :, b * half : (b + 1) * half] = emit[:, :half]
        emit_far[0, :, b * half : (b + 1) * half] = emit[:, half:]
        raw = raw + matmul(emit, jnp.concatenate(proj, axis=0))
    raw_out[0] = raw
    hid = 3.0 * jnp.tanh(raw * THIRD)
    h_scr[...] = hid.astype(BF16).astype(F32)
    hid_out[0] = hid.astype(BF16)


def run_forward(px, keep, weights):
    steps, rows, wide = px[0].shape
    hidden = weights[0].shape[1] // 2
    total = BLOCKS * wide // 4
    block = lambda n: pl.BlockSpec((1, rows, n), lambda t: (t, 0, 0))
    sizes = (4 * total, total, total // 2, total // 2, hidden, hidden, hidden)
    kinds = (BF16, F32, BF16, BF16, F32, BF16, BF16)
    return pl.pallas_call(
        forward_kernel,
        grid=(steps,),
        out_shape=tuple(jax.ShapeDtypeStruct((steps, rows, n), kind) for n, kind in zip(sizes, kinds)),
        in_specs=[block(wide)] * BLOCKS + [block(LANES)] + [whole(w.shape) for w in weights],
        out_specs=tuple(block(n) for n in sizes),
        scratch_shapes=[pltpu.VMEM((rows, total), F32), pltpu.VMEM((rows, hidden), F32)],
        compiler_params=pltpu.CompilerParams(vmem_limit_bytes=48 * 2**20, dimension_semantics=("arbitrary",)),
        cost_estimate=pl.CostEstimate(
            flops=2 * steps * rows * hidden * 5 * total * 8,
            bytes_accessed=steps * rows * total * 24 + 10 * total * hidden,
            transcendentals=steps * rows * total * 6,
        ),
        name="forward_chain",
    )(*px, keep, *weights)


def backward_kernel(*refs):
    pre_ref, cell_ref, before_ref, raw_ref, grad_ref, keep_ref = refs[:6]
    wt_refs, pt_refs = refs[6 : 6 + BLOCKS * PARTS], refs[6 + BLOCKS * PARTS : 6 + 2 * BLOCKS * PARTS]
    outs = refs[6 + 2 * BLOCKS * PARTS :]
    slabs, draw_out, bias_out, dc_scr, dk_scr = outs[: 2 * BLOCKS], *outs[2 * BLOCKS :]
    step = pl.program_id(0)
    hidden, piece = pt_refs[0].shape
    cells = piece * PARTS
    tiles = piece // LANES
    width = 4 * piece
    chunk = 4 * LANES
    rows = keep_ref.shape[1]

    @pl.when(step == 0)
    def _():
        dc_scr[...] = jnp.zeros_like(dc_scr)
        dk_scr[...] = jnp.zeros_like(dk_scr)
        bias_out[...] = jnp.zeros_like(bias_out)

    keep = keep_ref[0][:, :1]
    tangent = jnp.tanh(raw_ref[0] * THIRD)
    draw = ((grad_ref[0].astype(F32) + dk_scr[...]) * (1.0 - tangent * tangent)).astype(BF16)
    draw_out[0] = draw
    dk = jnp.zeros((rows, hidden), F32)
    for b in range(BLOCKS):
        at = b * cells
        demit = matmul(draw, jnp.concatenate([pt_refs[b * PARTS + s][...] for s in range(PARTS)], axis=1))
        gates = [
            jnp.concatenate(
                [
                    pre_ref[0, :, 4 * at + s * width + (u * 4 + q) * LANES : 4 * at + s * width + (u * 4 + q + 1) * LANES]
                    for s in range(PARTS)
                    for u in range(tiles)
                ],
                axis=1,
            ).astype(F32)
            for q in range(4)
        ]
        i, f, u, o = sigmoid(gates[0]), sigmoid(gates[1]), jnp.tanh(gates[2]), sigmoid(gates[3])
        cell = cell_ref[0, :, at : at + cells]
        kept_cell = before_ref[0, :, at : at + cells] * keep
        tanh_cell = jnp.tanh(cell)
        third = cell * THIRD
        dcell = (dc_scr[:, at : at + cells] + demit * o * (1.0 - tanh_cell * tanh_cell)) * (1.0 - third * third)
        dgates = (
            dcell * u * i * (1.0 - i),
            dcell * kept_cell * f * (1.0 - f),
            dcell * i * (1.0 - u * u),
            demit * tanh_cell * o * (1.0 - o),
        )
        dc_scr[:, at : at + cells] = dcell * f * keep
        for q in range(4):
            folded = dgates[q][:8]
            for r in range(8, rows, 8):
                folded = folded + dgates[q][r : r + 8]
            bias_out[:, (b * 4 + q) * cells : (b * 4 + q + 1) * cells] += folded
        dgates = [dgate.astype(BF16) for dgate in dgates]
        for s in range(PARTS):
            part = jnp.concatenate(
                [
                    dgates[q][:, s * piece + u * LANES : s * piece + (u + 1) * LANES]
                    for u in range(tiles)
                    for q in range(4)
                ],
                axis=1,
            )
            side, quarter = s // 2, s % 2
            for u in range(tiles):
                to = (u * 2 + quarter) * chunk
                slabs[b * 2 + side][0, :, to : to + chunk] = part[:, u * chunk : (u + 1) * chunk]
            dk = dk + matmul(part, wt_refs[b * PARTS + s][...])
    dk_scr[...] = dk * keep


def run_backward(pre, cell, raw, grad, keep, weights, projs):
    steps, rows, gates = pre.shape
    total = gates // 4
    hidden, piece = projs[0].shape
    half = PARTS * piece * 2
    block = lambda n: pl.BlockSpec((1, rows, n), lambda s: (steps - 1 - s, 0, 0))
    before = pl.BlockSpec((1, rows, total), lambda s: (jnp.maximum(steps - 2 - s, 0), 0, 0))
    shape = lambda n: jax.ShapeDtypeStruct((steps, rows, n), BF16)
    out = pl.pallas_call(
        backward_kernel,
        grid=(steps,),
        out_shape=tuple([shape(half)] * (2 * BLOCKS) + [shape(hidden), jax.ShapeDtypeStruct((8, gates), F32)]),
        in_specs=[block(gates), block(total), before, block(hidden), block(hidden), block(LANES)]
        + [whole(w.shape) for w in [*weights, *projs]],
        out_specs=tuple([block(half)] * (2 * BLOCKS) + [block(hidden), pl.BlockSpec((8, gates), lambda s: (0, 0))]),
        scratch_shapes=[pltpu.VMEM((rows, total), F32), pltpu.VMEM((rows, hidden), F32)],
        compiler_params=pltpu.CompilerParams(vmem_limit_bytes=48 * 2**20, dimension_semantics=("arbitrary",)),
        cost_estimate=pl.CostEstimate(
            flops=2 * steps * rows * hidden * 5 * total * 8,
            bytes_accessed=steps * rows * total * 24 + 10 * total * hidden,
            transcendentals=steps * rows * total * 6,
        ),
        name="backward_chain",
    )(pre, cell, cell, raw, grad, keep, *weights, *projs)
    return [out[b * 2 : b * 2 + 2] for b in range(BLOCKS)], out[2 * BLOCKS], out[2 * BLOCKS + 1]


def block_kernel(order_ref, x_ref, kept_ref, draw_ref, own_ref, far_ref, own_emit, far_emit, *refs):
    first_a, first_b, second_here, second_there, right, emit = refs
    rows = own_ref.shape[0]
    tile, step = pl.program_id(0), pl.program_id(1)
    depth, lines = x_ref.shape[0] // 4, draw_ref.shape[0] // 8
    group = lines // 4
    chunk = 4 * LANES
    first = order_ref[1]
    here, half = (step // 2) ^ order_ref[2], (step % 2) ^ order_ref[0]

    @pl.when(step == 0)
    def _():
        right[:rows, :], right[rows:, :] = own_ref[...], far_ref[...]
        for u in range(2):

            @pl.when(tile == u)
            def _():
                for quarter in range(2):
                    to, at = quarter * LANES, (quarter * 2 + u) * LANES
                    emit[:rows, to : to + LANES] = own_emit[:, at : at + LANES]
                    emit[rows:, to : to + LANES] = far_emit[:, at : at + LANES]

    def body(left_ref):
        left = left_ref[pl.ds(here * (2 * depth), 2 * depth), :]
        dp = matmul(draw_ref[pl.ds((half * 2 + here) * (2 * lines), 2 * lines), :], emit[...]).astype(BF16)
        for quarter in range(2):
            dw = matmul(left, right[:, quarter * chunk : (quarter + 1) * chunk]).astype(BF16)

            def store(out):
                for side in range(2):
                    to = side ^ first
                    out[to, :depth, :] = dw[side * depth : (side + 1) * depth]
                    for g in range(4):
                        at = side * lines + g * group
                        out[to, depth : depth + group, g * LANES : (g + 1) * LANES] = dp[
                            at : at + group, quarter * LANES : (quarter + 1) * LANES
                        ]

            pl.when(tile == 0)(lambda: store((first_a, first_b)[quarter]))
            pl.when((tile == 1) & (step < 2))(lambda: store(second_here.at[quarter]))
            pl.when((tile == 1) & (step >= 2))(lambda: store(second_there.at[quarter]))

    pl.when(half == 0)(lambda: body(x_ref))
    pl.when(half == 1)(lambda: body(kept_ref))


def block_grads(order, x_turned, kept_turned, draw_turned, own, far, emit_own, emit_far, b):
    rows = own.shape[0]
    chunk = 4 * LANES
    depth, lines = x_turned.shape[0] // 4, draw_turned.shape[0] // 8
    high = depth + lines // 4
    emit = pl.BlockSpec((rows, 4 * LANES), lambda u, n, o: (0, b))
    slab = pl.BlockSpec((rows, 2 * chunk), lambda u, n, o: (0, u))
    left = pl.BlockSpec(memory_space=pltpu.VMEM)
    first = pl.BlockSpec((2, high, chunk), lambda u, n, o: (jnp.where(u == 0, n, 3), 0, 0))
    here = pl.BlockSpec((2, 2, high, chunk), lambda u, n, o: (0, jnp.where(u == 0, 0, jnp.minimum(n, 1)), 0, 0))
    there = pl.BlockSpec((2, 2, high, chunk), lambda u, n, o: (0, jnp.where(u == 0, 0, jnp.maximum(n - 2, 0)), 0, 0))
    return pl.pallas_call(
        block_kernel,
        grid_spec=pltpu.PrefetchScalarGridSpec(
            num_scalar_prefetch=1,
            grid=(2, 4),
            in_specs=[left, left, left, slab, slab, emit, emit],
            out_specs=[first, first, here, there],
            scratch_shapes=[pltpu.VMEM((2 * rows, 2 * chunk), BF16), pltpu.VMEM((2 * rows, 2 * LANES), BF16)],
        ),
        out_shape=[jax.ShapeDtypeStruct((8, high, chunk), BF16)] * 2
        + [jax.ShapeDtypeStruct((2, 4, high, chunk), BF16)] * 2,
        compiler_params=pltpu.CompilerParams(vmem_limit_bytes=28 * 2**20, dimension_semantics=("arbitrary",) * 2),
        cost_estimate=LIGHT,
        name="weight_gradients",
    )(order, x_turned, kept_turned, draw_turned, own, far, emit_own, emit_far)


def layer_kernel(col_ref, x_ref, *refs):
    hid_refs, out_ref = refs[:4], refs[4]
    model = x_ref.shape[1]
    mask = pl.program_id(0) ^ col_ref[0]
    x = x_ref[...].astype(F32)

    def body(hid_ref):
        for d in range(2):
            out_ref[:, d, :] = (x + hid_ref[:, d * model : (d + 1) * model].astype(F32)).astype(BF16)

    for n in range(4):
        pl.when(mask == n)(functools.partial(body, hid_refs[n]))


def layer_sum(col, x, hiddens):
    rows, wide = hiddens[0].shape
    model = x.shape[1]
    return pl.pallas_call(
        layer_kernel,
        grid_spec=pltpu.PrefetchScalarGridSpec(
            num_scalar_prefetch=1,
            grid=(4,),
            in_specs=[pl.BlockSpec((rows, model), lambda n, c: (n, 0))] + [whole((rows, wide))] * 4,
            out_specs=pl.BlockSpec((rows, 2, model), lambda n, c: (n, 0, 0)),
        ),
        out_shape=jax.ShapeDtypeStruct((x.shape[0], 2, model), BF16),
        compiler_params=pltpu.CompilerParams(vmem_limit_bytes=16 * 2**20),
        cost_estimate=LIGHT,
        name="layer_sum",
    )(col.reshape(1).astype(jnp.int32), x, *hiddens)


def turn_rows_kernel(own_ref, met_ref, out_ref):
    rows = own_ref.shape[0]
    out_ref[:, :rows] = jnp.swapaxes(own_ref[...], 0, 1)
    out_ref[:, rows:] = jnp.swapaxes(met_ref[...], 0, 1)


def turn_rows(own, met):
    rows, wide = own.shape
    return pl.pallas_call(
        turn_rows_kernel,
        grid=(2,),
        out_shape=jax.ShapeDtypeStruct((wide, 2 * rows), BF16),
        in_specs=[pl.BlockSpec((rows, wide // 2), lambda n: (0, n))] * 2,
        out_specs=pl.BlockSpec((wide // 2, 2 * rows), lambda n: (n, 0)),
        compiler_params=pltpu.CompilerParams(vmem_limit_bytes=16 * 2**20),
        cost_estimate=LIGHT,
        name="turn_rows",
    )(own, met)


def turn_kernel(*refs):
    w_refs, p_refs, wt_refs, pt_refs = (refs[n * PARTS : (n + 1) * PARTS] for n in range(4))
    for source, target in zip(w_refs, wt_refs):
        target[...] = jnp.swapaxes(source[...], 0, 1)

    @pl.when(pl.program_id(0) == 0)
    def _():
        for source, target in zip(p_refs, pt_refs):
            lines, hidden = source.shape[0], source.shape[1] // 2
            target[:, :lines] = jnp.swapaxes(source[:, :hidden], 0, 1)
            target[:, lines:] = jnp.swapaxes(source[:, hidden:], 0, 1)


def turn(pieces):
    width = pieces[0].shape[1]
    hidden, piece = width // 2, width // 4
    cut = width // 4
    results = pl.pallas_call(
        turn_kernel,
        grid=(4,),
        out_shape=[jax.ShapeDtypeStruct((width, hidden), BF16)] * PARTS
        + [jax.ShapeDtypeStruct((hidden, piece), BF16)] * PARTS,
        in_specs=[pl.BlockSpec((hidden, cut), lambda n: (0, n))] * PARTS
        + [pl.BlockSpec((piece // 2, width), lambda n: (2 * hidden // piece, 0))] * PARTS,
        out_specs=[pl.BlockSpec((cut, hidden), lambda n: (n, 0))] * PARTS
        + [pl.BlockSpec((hidden, piece), lambda n: (0, 0))] * PARTS,
        compiler_params=pltpu.CompilerParams(vmem_limit_bytes=20 * 2**20, dimension_semantics=("arbitrary",)),
        cost_estimate=LIGHT,
        name="turn_pieces",
    )(*pieces, *pieces)
    return results[:PARTS], results[PARTS:]


def assemble_kernel(order_ref, *refs):
    weight_out, proj_out = refs[4:]
    depth = weight_out.shape[1]
    group = refs[0].shape[-2] - depth

    def body(tiles):
        for u, tile_ref in enumerate(tiles):
            value = tile_ref[0, 0].astype(F32)
            lanes = slice(u * LANES, (u + 1) * LANES)
            for q in range(4):
                columns = slice(q * LANES, (q + 1) * LANES)
                weight_out[0, :, q, lanes] = value[:depth, columns]
                proj_out[0, q * group : (q + 1) * group, lanes] = value[depth:, columns]

    far = (pl.program_id(1) // 2) ^ order_ref[1]
    pl.when(far == 0)(lambda: body(refs[:2]))
    pl.when(far == 1)(lambda: body(refs[2:4]))


def assemble(order, own0, own1, far0, far1, depth):
    lines = own0.shape[2]
    group = lines - depth
    cells = 8 * LANES
    piece = pl.BlockSpec((1, 1, lines, 4 * LANES), lambda d, n, o: (d ^ o[0], (n % 2) ^ o[2], 0, 0))
    return pl.pallas_call(
        assemble_kernel,
        grid_spec=pltpu.PrefetchScalarGridSpec(
            num_scalar_prefetch=1,
            grid=(2, 4),
            in_specs=[piece] * 4,
            out_specs=[
                pl.BlockSpec((1, depth, 4, 2 * LANES), lambda d, n, o: (d, 0, 0, n)),
                pl.BlockSpec((1, 4 * group, 2 * LANES), lambda d, n, o: (d, 0, n)),
            ],
        ),
        out_shape=[
            jax.ShapeDtypeStruct((2, depth, 4, cells), F32),
            jax.ShapeDtypeStruct((2, 4 * group, cells), F32),
        ],
        compiler_params=pltpu.CompilerParams(vmem_limit_bytes=16 * 2**20),
        cost_estimate=LIGHT,
        name="assemble_gradients",
    )(order, own0, own1, far0, far1)


def input_grad_kernel(has_sum, *refs):
    slab_refs, w_refs, out_ref = refs[:2], refs[2:6], refs[-1]
    chunk = 4 * LANES
    model = out_ref.shape[1]
    total = refs[6][...] if has_sum else None
    for side in range(2):
        for u in range(2):
            for quarter in range(2):
                at = (u * 2 + quarter) * chunk
                part = lax.dot_general(
                    slab_refs[side][:, at : at + chunk],
                    w_refs[side * 2 + quarter][:model, u * chunk : (u + 1) * chunk],
                    (((1,), (1,)), ((), ())),
                    preferred_element_type=F32,
                )
                total = part if total is None else total + part
    out_ref[...] = total


def add_input_grad(slabs, weights, total):
    rows, half = slabs[0].shape
    model = weights[0].shape[1] // 2
    tile = rows // 2
    operands = [*slabs, *weights] + ([] if total is None else [total])
    lines = lambda n: pl.BlockSpec((tile, n), lambda s: (s, 0))
    return pl.pallas_call(
        functools.partial(input_grad_kernel, total is not None),
        grid=(2,),
        out_shape=jax.ShapeDtypeStruct((rows, model), F32),
        in_specs=[lines(half)] * 2
        + [whole(w.shape) for w in weights]
        + ([] if total is None else [lines(model)]),
        out_specs=lines(model),
        compiler_params=pltpu.CompilerParams(vmem_limit_bytes=24 * 2**20),
        cost_estimate=LIGHT,
        name="input_gradient",
    )(*operands)


def after(values):
    return lax.optimization_barrier(values)


def one_direction(inputs, reset_flags, gate_weight, gate_bias, proj_weight, grad_out):
    row, col = lax.axis_index("rows"), lax.axis_index("cols")
    layer, core = row // 2, row % 2
    direction, pair = layer // 2, layer % 2
    model = inputs.shape[1]
    local = inputs.shape[0] // STEPS
    share = local // 4
    rows = 2 * share
    cells = gate_weight.shape[3]
    piece = cells // PARTS
    width = 4 * piece
    tiles = piece // LANES

    def mask_of(r, near):
        odd = (r // 2) % 2
        return (2 if odd else 1) if near else (1 if odd else 2)

    def over_chips(value, near):
        pairs = [(r * 4 + j, r * 4 + (j ^ mask_of(r, near))) for r in range(8) for j in range(4)]
        return lax.ppermute(value, ("rows", "cols"), pairs)

    def over_rows(value, mask):
        return lax.ppermute(value, "rows", [(r, r ^ mask) for r in range(8)])

    core_swap = functools.partial(over_rows, mask=1)
    pair_swap = functools.partial(over_rows, mask=2)
    half_swap = functools.partial(over_rows, mask=4)
    near_mask = jnp.where(pair == 0, 1, 2)
    block_at = [col, col ^ near_mask, col ^ (3 - near_mask), col ^ 3]
    by_dir = lambda pair_of: jnp.where(direction == 0, pair_of[0], pair_of[1])
    by_other = lambda pair_of: jnp.where(direction == 0, pair_of[1], pair_of[0])
    in_run = lambda value: jnp.where(direction == 0, value, value[::-1])

    order = jnp.stack([direction, core, pair]).astype(jnp.int32)

    def place_of(part):
        return jnp.stack([direction, (core ^ (part // 2)) * 2 + (pair ^ (part % 2))]).astype(jnp.int32)

    places = [place_of(part) for part in range(PARTS)]
    input_piece = lambda part: own_piece(places[part], gate_weight, gate_bias, False)
    recurrent_piece = lambda part: own_piece(places[part], gate_weight, proj_weight, True)

    local_windows = lambda value: lax.dynamic_slice_in_dim(value, col * share, share, 0)
    steps_first = lambda value: jnp.swapaxes(value, 0, 1)
    by_side = lambda k, there: [jnp.where(core == which, k, there) for which in range(2)]

    w_in = {(0, 0): own_piece(places[0], gate_weight, gate_bias, False, memory=60)}
    w_rec = {}
    w_in[1, 0] = over_chips(w_in[0, 0], True)
    w_in[2, 0] = over_chips(w_in[0, 0], False)
    w_rec[0, 0] = recurrent_piece(0)

    keep_grid = local_windows(reset_flags.reshape(local, STEPS)).astype(F32)
    position = lax.broadcasted_iota(jnp.int32, (share, STEPS), 1)
    keep_ahead = jnp.where(position > 0, 1.0 - keep_grid, 0.0)
    next_flags = jnp.concatenate([keep_grid[:, 1:], jnp.zeros((share, 1), F32)], axis=1)
    keep_behind = jnp.where(position < STEPS - 1, 1.0 - next_flags, 0.0)
    own_tokens = share * STEPS
    x_mine = lax.dynamic_slice_in_dim(inputs, col * own_tokens, own_tokens, 0).reshape(share, STEPS, model)
    x_mine = steps_first(x_mine)
    keep_dirs = (steps_first(keep_ahead), steps_first(keep_behind))
    keep_wide = [jnp.broadcast_to(k[..., None], (STEPS, share, LANES)).astype(BF16) for k in keep_dirs]
    xk_here = jnp.concatenate([x_mine, by_dir(keep_wide)], axis=2)
    xk_sent = jnp.concatenate([x_mine, by_other(keep_wide)], axis=2)
    xk_met = half_swap(xk_sent)
    w_in[0, 1] = input_piece(1)
    g_mine = lax.dynamic_slice_in_dim(grad_out, col * own_tokens, own_tokens, 0).reshape(share, STEPS, 2, model)
    g_dirs = (steps_first(g_mine[:, :, 0]), steps_first(g_mine[:, :, 1]))
    w_in, w_rec, xk_here, xk_met, g_dirs, places = after((w_in, w_rec, xk_here, xk_met, g_dirs, places))

    w_rec[1, 0] = over_chips(w_rec[0, 0], True)
    w_in[3, 0] = over_chips(w_in[1, 0], False)
    w_in[2, 1] = pair_swap(w_in[1, 0])
    for b in (1, 2):
        w_in[b, 2] = core_swap(w_in[b, 0])
    w_rec[0, 1], w_in[0, 2], w_in[0, 3] = recurrent_piece(1), input_piece(2), input_piece(3)
    xk = in_run(jnp.concatenate([xk_here, xk_met], axis=1))
    x_run, keep_run = xk[..., :model], xk[..., model:].astype(F32)
    x_flat = x_run.reshape(STEPS * rows, model)
    w_in, w_rec, x_flat, keep_run, g_dirs, places = after((w_in, w_rec, x_flat, keep_run, g_dirs, places))

    gates_of = lambda b: input_gates(x_flat, [w_in[b, part] for part in range(PARTS)])
    turn_of = lambda b: turn([w_rec[b, part] for part in range(PARTS)])
    w_in[1, 1] = over_chips(w_in[0, 1], True)
    w_rec[3, 0] = over_chips(w_rec[1, 0], False)
    w_in[3, 1] = pair_swap(w_in[3, 0])
    w_rec[1, 2], w_in[3, 2] = core_swap(w_rec[1, 0]), core_swap(w_in[3, 0])
    w_rec[0, 2], w_rec[0, 3] = recurrent_piece(2), recurrent_piece(3)
    px, turned = {0: gates_of(0)}, {}
    w_in, w_rec, px, x_flat = after((w_in, w_rec, px, x_flat))

    w_rec[1, 1] = over_chips(w_rec[0, 1], True)
    w_rec[2, 0] = over_chips(w_rec[0, 0], False)
    w_rec[2, 1] = pair_swap(w_rec[1, 0])
    for b in (1, 2, 3):
        w_in[b, 3] = core_swap(w_in[b, 1])
    turned[0] = turn_of(0)
    for b in (1, 2, 3):
        px[b] = gates_of(b)
    w_in, w_rec, px, turned, x_flat = after((w_in, w_rec, px, turned, x_flat))

    last_half = w_rec[3, 0].shape[0] // 2
    last_piece = [pair_swap(w_rec[3, 0][:last_half]), over_chips(w_rec[1, 1][last_half:], False)]
    w_rec[1, 3], w_rec[2, 2] = core_swap(w_rec[1, 1]), core_swap(w_rec[2, 0])
    w_rec[2, 3], w_rec[3, 2] = core_swap(w_rec[2, 1]), core_swap(w_rec[3, 0])
    x_met = core_swap(x_flat)
    turned[1], turned[2] = turn_of(1), turn_of(2)
    w_rec, turned, last_piece, x_met = after((w_rec, turned, last_piece, x_met))

    w_rec[3, 1] = jnp.concatenate(last_piece, axis=0)
    w_rec[3, 3] = core_swap(w_rec[3, 1])
    x_turned = turn_rows(x_flat, x_met)
    g_sent = by_other(g_dirs)
    w_rec, turned, x_turned, g_sent = after((w_rec, turned, x_turned, g_sent))

    g_met = half_swap(g_sent)
    px = [px[b].reshape(STEPS, rows, PARTS * width) for b in range(BLOCKS)]
    pre, cell, emit_own, emit_far, raw, kept, hid = run_forward(
        px, keep_run, [w_rec[b, part] for b in range(BLOCKS) for part in range(PARTS)]
    )

    pre, cell, emit_own, emit_far, raw, kept, hid, g_met = after((pre, cell, emit_own, emit_far, raw, kept, hid, g_met))
    g_run = in_run(jnp.concatenate([by_dir(g_dirs), g_met], axis=1))

    flat = lambda value: value.reshape(STEPS * rows, value.shape[-1])
    hid_time = in_run(hid)
    hid_here, hid_there = hid_time[:, :share], half_swap(hid_time[:, share:])
    emit_met = core_swap(flat(emit_far))
    kept = flat(kept)
    kept_met = core_swap(kept)
    turned[3] = turn_of(3)
    hid_here, hid_there, kept, kept_met, emit_met, turned, chain = after(
        (hid_here, hid_there, kept, kept_met, emit_met, turned, (pre, cell, raw))
    )

    def over_cols(value, mask):
        return lax.ppermute(value, "cols", [(j, j ^ mask) for j in range(4)])

    hid_both = jnp.concatenate([by_dir((hid_here, hid_there)), by_other((hid_here, hid_there))], axis=2)
    hid_parts = [hid_both] + [over_cols(hid_both, mask) for mask in (1, 2, 3)]

    kept_turned = turn_rows(kept, kept_met)
    slabs, draw, bias_sums = run_backward(
        *chain,
        g_run,
        keep_run,
        [w for b in range(BLOCKS) for w in turned[b][0]],
        [p for b in range(BLOCKS) for p in turned[b][1]],
    )
    hid_parts, kept_turned, slabs, draw, bias_sums, emit_own, emit_met = after(
        (hid_parts, kept_turned, slabs, draw, bias_sums, emit_own, emit_met)
    )

    slabs = [[flat(value) for value in block] for block in slabs]
    emit_own, draw = flat(emit_own), flat(draw)
    far = {3: core_swap(slabs[3][1])}
    draw_met = core_swap(draw)
    bias_parts = jnp.sum(bias_sums, axis=0).reshape(BLOCKS, 4, 2, 2 * piece)
    bias_half = bias_parts[:, :, 0] + core_swap(bias_parts[:, :, 1])
    far, draw_met, slabs, bias_half = after((far, draw_met, slabs, bias_half))

    def grads(b):
        left = (x_turned, kept_turned, draw_turned)
        return block_grads(order, *left, slabs[b][0], far[b], emit_own, emit_met, b)

    def add(first, *others):
        total = first.astype(F32)
        for other in others:
            total = total + other.astype(F32)
        return total.astype(BF16)

    def flip(value):
        return jnp.concatenate([value[1:], value[:1]], axis=0)

    draw_turned = turn_rows(draw, draw_met)
    opposite = grads(3)
    for b in (1, 2):
        far[b] = core_swap(slabs[b][1])
    bias_met = [over_chips(bias_half[1], True), over_chips(bias_half[2], False), over_cols(bias_half[3], 3)]
    far, opposite, draw_turned, slabs, bias_half, bias_met = after(
        (far, opposite, draw_turned, slabs, bias_half, bias_met)
    )

    relay_a, relay_b = over_chips(opposite[0], True), over_chips(opposite[1], False)
    met = pair_swap(opposite[3])
    far[0] = core_swap(slabs[0][1])
    bias_half = bias_half[0] + bias_met[0] + bias_met[1] + bias_met[2]
    bias_half = jnp.where(pair == 0, bias_half, jnp.concatenate([bias_half[:, piece:], bias_half[:, :piece]], axis=1))
    bias_half = bias_half + pair_swap(bias_half)
    near, other = grads(1), grads(2)
    far, relay_a, relay_b, met, near, other, slabs, bias_half = after(
        (far, relay_a, relay_b, met, near, other, slabs, bias_half)
    )

    near_a, other_b = over_chips(near[0], True), over_chips(other[1], False)
    other_met = pair_swap(near[3])
    opposite1 = add(opposite[2], flip(met))
    near_b, other_a = add(near[1], relay_b), add(other[0], relay_a)
    own = grads(0)
    near1, other1, own0, own1 = near[2:], other[2:], own[:2], own[2:]
    bias_there = half_swap(bias_half)
    bias_half = jnp.stack([by_dir((bias_half, bias_there)), by_other((bias_half, bias_there))])
    near_a, other_b, other_met, opposite1, near_b, other_a, other1, own0, own1, slabs, bias_half, hid_parts = after(
        (near_a, other_b, other_met, opposite1, near_b, other_a, other1, own0, own1, slabs, bias_half, hid_parts)
    )

    near_b, other_a = over_chips(near_b, True), over_chips(other_a, False)
    near_met = pair_swap(other1[1])
    wide = None
    for b in range(BLOCKS):
        wide = add_input_grad(slabs[b], [w_in[b, part] for part in range(PARTS)], wide)
    bias_total = jnp.concatenate(by_side(bias_half, core_swap(bias_half)), axis=2)
    near_b, other_a, near_met, wide, own1, bias_total, hid_parts = after(
        (near_b, other_a, near_met, wide, own1, bias_total, hid_parts)
    )

    relay_a, relay_b = over_chips(opposite1[0], True), over_chips(opposite1[1], False)
    sums0 = jnp.stack([add(own0[0], near_a, other_a), add(own0[1], near_b, other_b)])
    count = sums0.shape[1] // 2
    sums0_met = pair_swap(sums0[:, count:])
    dx = in_run(wide.reshape(STEPS, rows, model))
    dx, dx_met = dx[:, :share], half_swap(dx[:, share:].astype(BF16))
    hid_parts = [steps_first(value).reshape(own_tokens, 2 * model) for value in hid_parts]
    relay_a, relay_b, sums0, sums0_met, dx, dx_met, own1, hid_parts = after(
        (relay_a, relay_b, sums0, sums0_met, dx, dx_met, own1, hid_parts)
    )

    near1 = add(near1[0], flip(near_met), jnp.stack([jnp.zeros_like(relay_b), relay_b]))
    other1 = add(other1[0], flip(other_met), jnp.stack([relay_a, jnp.zeros_like(relay_a)]))
    near_met, other_met = over_chips(near1, True), over_chips(other1, False)
    own_met = pair_swap(own1[1])
    by_half = lambda value: value.reshape(2, 2, 2, *value.shape[2:])
    sums0 = by_half(add(sums0[:, :count], flip(sums0_met)))
    sums0_met = half_swap(sums0[:, 1])
    dx = dx + dx_met.astype(F32) + g_dirs[0].astype(F32) + g_dirs[1].astype(F32)
    dx = steps_first(dx.astype(BF16)).reshape(own_tokens, model)
    def by_column(parts):
        whole_rows = jnp.zeros((BLOCKS * parts[0].shape[0], parts[0].shape[1]), parts[0].dtype)
        for mask, value in enumerate(parts):
            whole_rows = lax.dynamic_update_slice(whole_rows, value, ((col ^ mask) * value.shape[0], 0))
        return whole_rows

    block_out = layer_sum(col, inputs, hid_parts)
    near_met, other_met, own_met, sums0, sums0_met, dx, own1, block_out = after(
        (near_met, other_met, own_met, sums0, sums0_met, dx, own1, block_out)
    )

    sums1 = by_half(add(own1[0], flip(own_met), near_met, other_met))
    sums1_met = half_swap(sums1[:, 1])

    def two_directions(here, there):
        both = jnp.stack([here, there])
        return both[:, :, 0], both[:, :, 1]

    kept0, sent0 = two_directions(sums0[:, 0], sums0_met)
    met0 = core_swap(sent0)
    slice_for = lambda at: lax.dynamic_slice_in_dim(dx, at * (model // 4), model // 4, 1)
    dx_parts = [slice_for(col ^ mask) for mask in range(4)]
    dx_parts = [dx_parts[0]] + [over_cols(dx_parts[mask], mask) for mask in (1, 2, 3)]

    sums1, sums1_met, kept0, met0, dx_parts = after((sums1, sums1_met, kept0, met0, dx_parts))

    kept1, sent1 = two_directions(sums1[:, 0], sums1_met)
    met1 = core_swap(sent1)
    weight_share, proj_share = assemble(order, kept0, kept1, met0, met1, 2 * model // 8)
    proj_share = jnp.swapaxes(proj_share, 1, 2)
    input_grad = by_column(dx_parts)
    return (block_out, input_grad, weight_share, bias_total, proj_share)


def solution(mesh):
    placed = (
        P("rows", None),
        P("rows"),
        P(None, None, None, "cols"),
        P(None, None, "cols"),
        P(None, "cols", None),
        P("rows", None, None),
    )
    plan = one_direction if (mesh.shape["rows"], mesh.shape["cols"]) == (8, 4) else shared_cells
    return jax.shard_map(
        plan,
        mesh=mesh,
        in_specs=placed,
        out_specs=(
            P("rows", None, None),
            P("rows", "cols"),
            P(None, "rows", None, "cols"),
            P(None, None, "cols"),
            P(None, "cols", "rows"),
        ),
        check_vma=False,
    )
```

time: 857 us -> 644 us (0.75)
  waiting for transfers between devices: 282 us -> 127 us
  local copies, waits for them, and re-layouts: 178 us -> 104 us
  Pallas kernels: 284 us -> 309 us
  starting transfers between devices: 68.7 us -> 58 us
    ppermute x61 -> x41, waiting for transfers between devices: 204 us -> 95.9 us  [over_rows(): return lax.ppermute(value, 'rows', [(r, r ^ mask) for r in range(8)])]
    ppermute x34 -> x21, waiting for transfers between devices: 73.3 us -> 26.5 us  [over_chips(): return lax.ppermute(value, ('rows', 'cols'), pairs)]
    ppermute x24 -> x0, local copies, waits for them, and re-layouts: 43.2 us -> none  [the longest x16 29.7 us: over_rows(): return lax.ppermute(value, 'rows', [(r, r ^ mask) for r in range(8)])]
    pallas_call x13 -> x26, Pallas kernels: 166 us -> 206 us  [the longest x1 86.9 us: run_backward(): pl.pallas_call(backward_kernel, grid=(steps,), out_shape=tuple([shape(hal...]
    reshape x12 -> x8, local copies, waits for them, and re-layouts: 31.7 us -> 1.98 us  [the longest x4 1.64 us: one_direction(): steps_first(value).reshape(own_tokens, 2 * model)]
    unnamed x269 -> x319, local copies, waits for them, and re-layouts: 50.4 us -> 78.1 us
    ppermute x34 -> x21, starting transfers between devices: 38.7 us -> 22.1 us  [over_chips(): return lax.ppermute(value, ('rows', 'cols'), pairs)]
    convert_element_type x5 -> x2, local copies, waits for them, and re-layouts: 16.1 us -> 0.18 us  [add(): return total.astype(BF16)]
  transfers between devices with their start and end apart: 97 -> 69, of which waited for: 37 -> 29; matrix products, arithmetic and copies ran while one was open for 18% -> 7% of each run, Pallas kernels for 11% -> 47%
where the time goes in v2:
time: 644 us; the launch traced here: 634 us
  Pallas kernels  309 us (48%)
  waiting for transfers between devices  127 us (20%)
  local copies, waits for them, and re-layouts  104 us (16%)
  starting transfers between devices  58 us (9%)
  other arithmetic  33.7 us (5%)
    ppermute x41, waiting for transfers between devices, over_rows(): return lax.ppermute(value, 'rows', [(r, r ^ mask) for r in range(8)])  95.9 us
    pallas_call x1, Pallas kernels, run_backward(): pl.pallas_call(backward_kernel, grid=(steps,), out_shape=tuple([shape(hal...  86.9 us
    pallas_call x1, Pallas kernels, run_forward(): pl.pallas_call(forward_kernel, grid=(steps,), out_shape=tuple((jax.ShapeD...  85.7 us
    unnamed x319, local copies, waits for them, and re-layouts  78.1 us
    pallas_call x4, Pallas kernels, block_grads(): pl.pallas_call(block_kernel, grid_spec=pltpu.PrefetchScalarGridSpec(num_s...  52.5 us
    pallas_call x8, Pallas kernels, own_piece(): pl.pallas_call(own_piece_kernel, grid_spec=pltpu.PrefetchScalarGridSpec(n...  28.7 us
    ppermute x41, starting transfers between devices, over_rows(): return lax.ppermute(value, 'rows', [(r, r ^ mask) for r in range(8)])  28.1 us
    ppermute x21, waiting for transfers between devices, over_chips(): return lax.ppermute(value, ('rows', 'cols'), pairs)  26.5 us
  transfers between devices with their start and end apart: 69, of which 29 were waited for; matrix products, arithmetic and copies ran while one was open for 7% of the time, Pallas kernels for 47%

profile of v2, /device:TPU:0, one launch (start us, length us, event | category | flops | bytes accessed | tf_op | source)
XLA Modules:
  0.0 634.2 jit_solution(10276893333058900261)
XLA Ops:
  1.3 5.6 own_piece.8.w0.refs_2_
  19.3 5.8 copy-done.2
  25.1 3.3 own_piece.10.refs_0_.refs_4_.refs_5_
  41.6 5.8 copy-done.4
  47.4 3.3 own_piece.13.refs_1_.refs_5_.refs_6_
  50.7 3.3 own_piece.11.w2.refs_4_
  54.0 3.3 own_piece.12.w3.refs_5_
  59.1 5.8 collective-permute-done.4.w1.refs_3_
  70.3 3.3 own_piece.14.refs_2_.refs_6_.refs_7_
  73.7 3.3 own_piece.15.refs_3_.refs_7_.refs_8_
  82.6 11.7 %collective-permute-done.8.w1.refs_3_ = bf16[528,1024]{1,0:T(8,128)(2,1)S(1)} collective-permute-done((bf16[528,1024]{1,0:T(8,128)(2,1)S(1)}, bf16[528,1024]{1,0:T(8,128)(2,1)S(1)}, u32[]{:S(2)}, u32[]{:S(2)}) %collective-permute-start.8) | collective-permute-done | bytes 1081376 | tf_op jit(solution)/shard_map/ppermute | solution.py:706
  94.6 4.1 collective-permute-done.12.refs_17_.refs_0_.refs_4_
  110.9 4.8 input_gates.6
  117.9 4.8 input_gates.5
  125.0 4.9 collective-permute-done.16.refs_1_.refs_5_.refs_10_
  144.4 3.7 collective-permute-done.23
  155.9 85.7 %forward_chain.1 = (bf16[20,32,16384]{2,1,0:T(8,128)(2,1)}, f32[20,32,4096]{2,1,0:T(8,128)}, bf16[20,32,2048]{2,1,0:T(8,128)(2,1)}, bf16[20,32,2048]{2,1,0:T(8,1...) custom-call(bf16[20,32,4096]{2,1,0:T(8,128)(2,1)} %bitcast.128, ...), custom_call_target="tpu_custom_call" | custom-call | flops 107374182400 | bytes 83886080 | tf_op jit(solution)/shard_map/forward_chain/pallas_call | solution.py:322
  252.6 15.4 %collective-permute-done.28 = bf16[20,16,512]{2,1,0:T(8,128)(2,1)S(1)} collective-permute-done((bf16[20,16,512]{2,1,0:T(8,128)(2,1)S(1)}, bf16[20,16,512]{2,1,0:T(8,128)(2,1)S(1)}, u32[]{:S(2)}, u32[]{:S(2)}) %collective-permute-start.28) | collective-permute-done | bytes 327712 | tf_op jit(solution)/shard_map/ppermute | solution.py:709
  273.0 86.9 %backward_chain.1 = (bf16[20,32,2048]{2,1,0:T(8,128)(2,1)}, bf16[20,32,2048]{2,1,0:T(8,128)(2,1)}, bf16[20,32,2048]{2,1,0:T(8,128)(2,1)}, bf16[20,32,2048]{2,1,0...) custom-call(bf16[20,32,16384]{2,1,0:T(8,128)(2,1)} %get-tuple-elemen, ...), custom_call_target="tpu_custom_call" | custom-call | flops 107374182400 | bytes 83886080 | tf_op jit(solution)/shard_map/backward_chain/pallas_call | solution.py:421
  380.6 14.1 %weight_gradients.4 = (bf16[8,144,512]{2,1,0:T(8,128)(2,1)}, bf16[8,144,512]{2,1,0:T(8,128)(2,1)}, bf16[2,4,144,512]{3,2,1,0:T(8,128)(2,1)S(1)}, bf16[2,4,144,512]{3,2,1,0:T(8,128)(2,1)}) custom-call(s32[3]{0:T(128)S(1)} %pad_add_fusion.4.order_ref, bf16[512,1280]{1,0:T(8,128)(2,1)S(1)} %copy-done.11, bf16[512,1280]{1,0:T(8,128)(2,1)S(1)} %copy-done.14, ...), custom_call_target="tpu_custom_call" | custom-call | flops 1 | bytes 1 | tf_op jit(solution)/shard_map/weight_gradients/pallas_call | solution.py:497
  412.8 12.7 %weight_gradients.6 = (bf16[8,144,512]{2,1,0:T(8,128)(2,1)S(1)}, bf16[8,144,512]{2,1,0:T(8,128)(2,1)S(1)}, bf16[2,4,144,512]{3,2,1,0:T(8,128)(2,1)S(1)}, bf16[2,4,144,512]{3,2,1,0:T(8,128)(2,1)}) custom-call(s32[3]{0:T(128)S(1)} %pad_add_fusion.4.order_ref, bf16[512,1280]{1,0:T(8,128)(2,1)S(1)} %copy-done.12, bf16[512,1280]{1,0:T(8,128)(2,1)S(1)} %copy-done.15, ...), custom_call_target="tpu_custom_call" | custom-call | flops 1 | bytes 1 | tf_op jit(solution)/shard_map/weight_gradients/pallas_call | solution.py:497
  426.5 12.1 %weight_gradients.5 = (bf16[8,144,512]{2,1,0:T(8,128)(2,1)S(1)}, bf16[8,144,512]{2,1,0:T(8,128)(2,1)S(1)}, bf16[2,4,144,512]{3,2,1,0:T(8,128)(2,1)S(1)}, bf16[2,4,144,512]{3,2,1,0:T(8,128)(2,1)S(1)}) custom-call(s32[3]{0:T(128)S(1)} %pad_add_fusion.4.order_ref, bf16[512,1280]{1,0:T(8,128)(2,1)S(1)} %copy-done.12, bf16[512,1280]{1,0:T(8,128)(2,1)S(1)} %copy-done.15, ...), custom_call_target="tpu_custom_call" | custom-call | flops 1 | bytes 1 | tf_op jit(solution)/shard_map/weight_gradients/pallas_call | solution.py:497
  452.0 13.7 %weight_gradients.7 = (bf16[8,144,512]{2,1,0:T(8,128)(2,1)S(1)}, bf16[8,144,512]{2,1,0:T(8,128)(2,1)S(1)}, bf16[2,4,144,512]{3,2,1,0:T(8,128)(2,1)S(1)}, bf16[2,4,144,512]{3,2,1,0:T(8,128)(2,1)}) custom-call(s32[3]{0:T(128)S(1)} %pad_add_fusion.4.order_ref, bf16[512,1280]{1,0:T(8,128)(2,1)S(1)} %copy-done.12, bf16[512,1280]{1,0:T(8,128)(2,1)S(1)} %copy-done.15, ...), custom_call_target="tpu_custom_call" | custom-call | flops 1 | bytes 1 | tf_op jit(solution)/shard_map/weight_gradients/pallas_call | solution.py:497
  480.3 4.6 input_gradient.4.refs_6_
  485.0 4.5 input_gradient.5.refs_6_
  489.7 4.5 input_gradient.6.refs_6_
  494.3 3.3 input_gradient.7
  522.1 16.1 %collective-permute-done.58 = bf16[20,16,512]{2,1,0:T(8,128)(2,1)} collective-permute-done((bf16[20,16,512]{2,1,0:T(8,128)(2,1)}, bf16[20,16,512]{2,1,0:T(8,128)(2,1)}, u32[]{:S(2)}, u32[]{:S(2)}) %collective-permute-start.58) | collective-permute-done | bytes 327712 | tf_op jit(solution)/shard_map/ppermute | solution.py:709
  550.6 4.5 layer_sum.1
  556.8 27.5 %collective-permute-done.62 = bf16[2,2,144,512]{3,2,0,1:T(8,128)(2,1)} collective-permute-done((bf16[2,2,144,512]{3,2,0,1:T(8,128)(2,1)}, bf16[2,2,144,512]{3,2,0,1:T(8,128)(2,1)}, u32[]{:S(2)}, u32[]{:S(2)}) %collective-permute-start.62) | collective-permute-done | bytes 589856 | tf_op jit(solution)/shard_map/ppermute | solution.py:709
  602.7 18.6 %collective-permute-done.63 = bf16[2,2,144,512]{3,2,0,1:T(8,128)(2,1)} collective-permute-done((bf16[2,2,144,512]{3,2,0,1:T(8,128)(2,1)}, bf16[2,2,144,512]{3,2,0,1:T(8,128)(2,1)}, u32[]{:S(2)}, u32[]{:S(2)}) %collective-permute-start.63) | collective-permute-done | bytes 589856 | tf_op jit(solution)/shard_map/ppermute | solution.py:709
  628.5 5.3 assemble_gradients.1
  (549 shorter events, 225.0 us)
Async XLA Ops:
  7.0 30.8 %collective-permute-start = (bf16[528,1024]{1,0:T(8,128)(2,1)}, bf16[528,1024]{1,0:T(8,128)(2,1)}, u32[]{:S(2)}, u32[]{:S(2)}) collective-permute-start(bf16[528,1024]{1,0:T(8,128)(2,1)} %own_piece.8.w0.refs_2_), channel_id=1, source_target_pairs={{0,1},{1,0},{2,3},{3,2},{4,5},{5,4},{6,7},{7,6},{8,10},{9,11},{10,... | collective-permute-start | bytes 3244040 | tf_op jit(solution)/shard_map/ppermute | solution.py:706
  9.9 27.8 %collective-permute-start.1 = (bf16[528,1024]{1,0:T(8,128)(2,1)}, bf16[528,1024]{1,0:T(8,128)(2,1)}, u32[]{:S(2)}, u32[]{:S(2)}) collective-permute-start(bf16[528,1024]{1,0:T(8,128)(2,1)} %own_piece.8.w0.refs_2_), channel_id=1, source_target_pairs={{0,2},{1,3},{2,0},{3,1},{4,6},{5,7},{6,4},{7,5},{8,9},{9,8},{10,11... | collective-permute-start | bytes 3244040 | tf_op jit(solution)/shard_map/ppermute | solution.py:706
  37.7 29.7 %collective-permute-start.7 = (bf16[640,1024]{1,0:T(8,128)(2,1)S(1)}, bf16[640,1024]{1,0:T(8,128)(2,1)S(1)}, u32[]{:S(2)}, u32[]{:S(2)}) collective-permute-start(bf16[640,1024]{1,0:T(8,128)(2,1)S(1)} %own_piece.10.refs_0_.refs_4_.refs_5_), channel_id=1, source_target_pairs={{0,1},{1,0},{2,3},{3,2},{4,5},{5,4},{6,7},{7,6},{8,10},{9,11},{10,... | collective-permute-start | bytes 3932168 | tf_op jit(solution)/shard_map/ppermute | solution.py:706
  67.5 27.1 %collective-permute-start.11 = (bf16[640,1024]{1,0:T(8,128)(2,1)S(1)}, bf16[640,1024]{1,0:T(8,128)(2,1)S(1)}, u32[]{:S(2)}, u32[]{:S(2)}) collective-permute-start(bf16[640,1024]{1,0:T(8,128)(2,1)S(1)} %collective-permute-done.7.refs_0_.refs_4_.refs_9_), channel_id=1, source_target_pairs={{0,4},{4,0},{8,12},{12,8},{16,20},{20,16},{24,28},{28,24},{1,5},{5... | collective-permute-start | bytes 3932168 | tf_op jit(solution)/shard_map/ppermute | solution.py:709
  67.5 31.2 %collective-permute-start.12 = (bf16[640,1024]{1,0:T(8,128)(2,1)S(1)}, bf16[640,1024]{1,0:T(8,128)(2,1)S(1)}, u32[]{:S(2)}, u32[]{:S(2)}) collective-permute-start(bf16[640,1024]{1,0:T(8,128)(2,1)S(1)} %collective-permute-done.7.refs_0_.refs_4_.refs_9_), channel_id=1, source_target_pairs={{0,2},{1,3},{2,0},{3,1},{4,6},{5,7},{6,4},{7,5},{8,9},{9,8},{10,11... | collective-permute-start | bytes 3932168 | tf_op jit(solution)/shard_map/ppermute | solution.py:706
  98.7 31.2 %collective-permute-start.16 = (bf16[640,1024]{1,0:T(8,128)(2,1)S(1)}, bf16[640,1024]{1,0:T(8,128)(2,1)S(1)}, u32[]{:S(2)}, u32[]{:S(2)}) collective-permute-start(bf16[640,1024]{1,0:T(8,128)(2,1)S(1)} %own_piece.13.refs_1_.refs_5_.refs_6_), channel_id=1, source_target_pairs={{0,1},{1,0},{2,3},{3,2},{4,5},{5,4},{6,7},{7,6},{8,10},{9,11},{10,... | collective-permute-start | bytes 3932168 | tf_op jit(solution)/shard_map/ppermute | solution.py:706
  99.2 30.9 %collective-permute-start.17 = (bf16[640,1024]{1,0:T(8,128)(2,1)S(1)}, bf16[640,1024]{1,0:T(8,128)(2,1)S(1)}, u32[]{:S(2)}, u32[]{:S(2)}) collective-permute-start(bf16[640,1024]{1,0:T(8,128)(2,1)S(1)} %own_piece.10.refs_0_.refs_4_.refs_5_), channel_id=1, source_target_pairs={{0,2},{1,3},{2,0},{3,1},{4,6},{5,7},{6,4},{7,5},{8,9},{9,8},{10,11... | collective-permute-start | bytes 3932168 | tf_op jit(solution)/shard_map/ppermute | solution.py:706
  99.7 30.6 %collective-permute-start.18 = (bf16[640,1024]{1,0:T(8,128)(2,1)S(1)}, bf16[640,1024]{1,0:T(8,128)(2,1)S(1)}, u32[]{:S(2)}, u32[]{:S(2)}) collective-permute-start(bf16[640,1024]{1,0:T(8,128)(2,1)S(1)} %collective-permute-done.7.refs_0_.refs_4_.refs_9_), channel_id=1, source_target_pairs={{0,8},{4,12},{8,0},{12,4},{16,24},{20,28},{24,16},{28,20},{1,9},{5... | collective-permute-start | bytes 3932168 | tf_op jit(solution)/shard_map/ppermute | solution.py:709
  154.5 88.1 %collective-permute-start.27 = (bf16[20,16,512]{2,1,0:T(8,128)(2,1)S(1)}, bf16[20,16,512]{2,1,0:T(8,128)(2,1)S(1)}, u32[]{:S(2)}, u32[]{:S(2)}) collective-permute-start(bf16[20,16,512]{2,1,0:T(8,128)(2,1)S(1)} %get-tuple-element.591), channel_id=1, source_target_pairs={{0,16},{4,20},{8,24},{12,28},{16,0},{20,4},{24,8},{28,12},{1,17},{... | collective-permute-start | bytes 983048 | tf_op jit(solution)/shard_map/ppermute | solution.py:709
  269.5 92.3 %collective-permute-start.31 = (bf16[20,16,1024]{2,1,0:T(8,128)(2,1)S(1)}, bf16[20,16,1024]{2,1,0:T(8,128)(2,1)S(1)}, u32[]{:S(2)}, u32[]{:S(2)}) collective-permute-start(bf16[20,16,1024]{2,1,0:T(8,128)(2,1)S(1)} %pad_maximum_fusion.1), channel_id=1, source_target_pairs={{0,1},{1,0},{2,3},{3,2},{4,5},{5,4},{6,7},{7,6},{8,9},{9,8},{10,11... | collective-permute-start | bytes 1966088 | tf_op jit(solution)/shard_map/ppermute | solution.py:823
  270.7 91.0 %collective-permute-start.32 = (bf16[20,16,1024]{2,1,0:T(8,128)(2,1)S(1)}, bf16[20,16,1024]{2,1,0:T(8,128)(2,1)S(1)}, u32[]{:S(2)}, u32[]{:S(2)}) collective-permute-start(bf16[20,16,1024]{2,1,0:T(8,128)(2,1)S(1)} %pad_maximum_fusion.1), channel_id=1, source_target_pairs={{0,2},{1,3},{2,0},{3,1},{4,6},{5,7},{6,4},{7,5},{8,10},{9,11},{10,... | collective-permute-start | bytes 1966088 | tf_op jit(solution)/shard_map/ppermute | solution.py:823
  272.2 89.5 %collective-permute-start.33 = (bf16[20,16,1024]{2,1,0:T(8,128)(2,1)S(1)}, bf16[20,16,1024]{2,1,0:T(8,128)(2,1)S(1)}, u32[]{:S(2)}, u32[]{:S(2)}) collective-permute-start(bf16[20,16,1024]{2,1,0:T(8,128)(2,1)S(1)} %pad_maximum_fusion.1), channel_id=1, source_target_pairs={{0,3},{1,2},{2,1},{3,0},{4,7},{5,6},{6,5},{7,4},{8,11},{9,10},{10,... | collective-permute-start | bytes 1966088 | tf_op jit(solution)/shard_map/ppermute | solution.py:823
  368.3 27.4 %collective-permute-start.37 = (bf16[640,2048]{1,0:T(8,128)(2,1)}, bf16[640,2048]{1,0:T(8,128)(2,1)S(1)}, u32[]{:S(2)}, u32[]{:S(2)}) collective-permute-start(bf16[640,2048]{1,0:T(8,128)(2,1)} %bitcast.137), channel_id=1, source_target_pairs={{0,4},{4,0},{8,12},{12,8},{16,20},{20,16},{24,28},{28,24},{1,5},{5... | collective-permute-start | bytes 7864328 | tf_op jit(solution)/shard_map/ppermute | solution.py:709
  368.4 28.8 %collective-permute-start.38 = (bf16[640,2048]{1,0:T(8,128)(2,1)}, bf16[640,2048]{1,0:T(8,128)(2,1)S(1)}, u32[]{:S(2)}, u32[]{:S(2)}) collective-permute-start(bf16[640,2048]{1,0:T(8,128)(2,1)} %bitcast.135), channel_id=1, source_target_pairs={{0,4},{4,0},{8,12},{12,8},{16,20},{20,16},{24,28},{28,24},{1,5},{5... | collective-permute-start | bytes 7864328 | tf_op jit(solution)/shard_map/ppermute | solution.py:709
  398.7 39.9 %collective-permute-start.42 = (bf16[640,2048]{1,0:T(8,128)(2,1)}, bf16[640,2048]{1,0:T(8,128)(2,1)}, u32[]{:S(2)}, u32[]{:S(2)}) collective-permute-start(bf16[640,2048]{1,0:T(8,128)(2,1)} %bitcast.23.refs_1_), channel_id=1, source_target_pairs={{0,4},{4,0},{8,12},{12,8},{16,20},{20,16},{24,28},{28,24},{1,5},{5... | collective-permute-start | bytes 7864328 | tf_op jit(solution)/shard_map/ppermute | solution.py:709
  398.7 39.9 %collective-permute-start.43 = (bf16[8,144,512]{2,1,0:T(8,128)(2,1)}, bf16[8,144,512]{2,1,0:T(8,128)(2,1)}, u32[]{:S(2)}, u32[]{:S(2)}) collective-permute-start(bf16[8,144,512]{2,1,0:T(8,128)(2,1)} %get-tuple-element.714), channel_id=1, source_target_pairs={{0,1},{1,0},{2,3},{3,2},{4,5},{5,4},{6,7},{7,6},{8,10},{9,11},{10,... | collective-permute-start | bytes 3538952 | tf_op jit(solution)/shard_map/ppermute | solution.py:706
  400.0 38.6 %collective-permute-start.44 = (bf16[8,144,512]{2,1,0:T(8,128)(2,1)}, bf16[8,144,512]{2,1,0:T(8,128)(2,1)}, u32[]{:S(2)}, u32[]{:S(2)}) collective-permute-start(bf16[8,144,512]{2,1,0:T(8,128)(2,1)} %get-tuple-element.715), channel_id=1, source_target_pairs={{0,2},{1,3},{2,0},{3,1},{4,6},{5,7},{6,4},{7,5},{8,9},{9,8},{10,11... | collective-permute-start | bytes 3538952 | tf_op jit(solution)/shard_map/ppermute | solution.py:706
  401.5 37.1 %collective-permute-start.45 = (bf16[2,4,144,512]{3,2,1,0:T(8,128)(2,1)}, bf16[2,4,144,512]{3,2,1,0:T(8,128)(2,1)}, u32[]{:S(2)}, u32[]{:S(2)}) collective-permute-start(bf16[2,4,144,512]{3,2,1,0:T(8,128)(2,1)} %get-tuple-element.716), channel_id=1, source_target_pairs={{0,8},{4,12},{8,0},{12,4},{16,24},{20,28},{24,16},{28,20},{1,9},{5... | collective-permute-start | bytes 3538952 | tf_op jit(solution)/shard_map/ppermute | solution.py:709
  401.5 37.0 %collective-permute-start.46 = (f32[4,512]{1,0:T(4,128)S(1)}, f32[4,512]{1,0:T(4,128)S(1)}, u32[]{:S(2)}, u32[]{:S(2)}) collective-permute-start(f32[4,512]{1,0:T(4,128)S(1)} %maximum_select_fusion), channel_id=1, source_target_pairs={{0,8},{4,12},{8,0},{12,4},{16,24},{20,28},{24,16},{28,20},{1,9},{5... | collective-permute-start | bytes 24584 | tf_op jit(solution)/shard_map/ppermute | solution.py:709
  438.6 30.1 %collective-permute-start.50 = (f32[4,512]{1,0:T(4,128)S(1)}, f32[4,512]{1,0:T(4,128)S(1)}, u32[]{:S(2)}, u32[]{:S(2)}) collective-permute-start(f32[4,512]{1,0:T(4,128)S(1)} %add.137), channel_id=1, source_target_pairs={{0,16},{4,20},{8,24},{12,28},{16,0},{20,4},{24,8},{28,12},{1,17},{... | collective-permute-start | bytes 24584 | tf_op jit(solution)/shard_map/ppermute | solution.py:709
  440.0 28.8 %collective-permute-start.47 = (bf16[8,144,512]{2,1,0:T(8,128)(2,1)S(1)}, bf16[8,144,512]{2,1,0:T(8,128)(2,1)S(1)}, u32[]{:S(2)}, u32[]{:S(2)}) collective-permute-start(bf16[8,144,512]{2,1,0:T(8,128)(2,1)S(1)} %get-tuple-element.738), channel_id=1, source_target_pairs={{0,1},{1,0},{2,3},{3,2},{4,5},{5,4},{6,7},{7,6},{8,10},{9,11},{10,... | collective-permute-start | bytes 3538952 | tf_op jit(solution)/shard_map/ppermute | solution.py:706
  440.5 28.3 %collective-permute-start.48 = (bf16[8,144,512]{2,1,0:T(8,128)(2,1)S(1)}, bf16[8,144,512]{2,1,0:T(8,128)(2,1)S(1)}, u32[]{:S(2)}, u32[]{:S(2)}) collective-permute-start(bf16[8,144,512]{2,1,0:T(8,128)(2,1)S(1)} %get-tuple-element.739), channel_id=1, source_target_pairs={{0,2},{1,3},{2,0},{3,1},{4,6},{5,7},{6,4},{7,5},{8,9},{9,8},{10,11... | collective-permute-start | bytes 3538952 | tf_op jit(solution)/shard_map/ppermute | solution.py:706
  441.0 27.8 %collective-permute-start.49 = (bf16[2,4,144,512]{3,2,1,0:T(8,128)(2,1)S(1)}, bf16[2,4,144,512]{3,2,1,0:T(8,128)(2,1)S(1)}, u32[]{:S(2)}, u32[]{:S(2)}) collective-permute-start(bf16[2,4,144,512]{3,2,1,0:T(8,128)(2,1)S(1)} %get-tuple-element.740), channel_id=1, source_target_pairs={{0,8},{4,12},{8,0},{12,4},{16,24},{20,28},{24,16},{28,20},{1,9},{5... | collective-permute-start | bytes 3538952 | tf_op jit(solution)/shard_map/ppermute | solution.py:709
  469.9 28.4 %collective-permute-start.51 = (bf16[8,144,512]{2,1,0:T(8,128)(2,1)}, bf16[8,144,512]{2,1,0:T(8,128)(2,1)}, u32[]{:S(2)}, u32[]{:S(2)}) collective-permute-start(bf16[8,144,512]{2,1,0:T(8,128)(2,1)} %add_convert_fusion.7), channel_id=1, source_target_pairs={{0,1},{1,0},{2,3},{3,2},{4,5},{5,4},{6,7},{7,6},{8,10},{9,11},{10,... | collective-permute-start | bytes 3538952 | tf_op jit(solution)/shard_map/ppermute | solution.py:706
  471.4 26.9 %collective-permute-start.52 = (bf16[8,144,512]{2,1,0:T(8,128)(2,1)}, bf16[8,144,512]{2,1,0:T(8,128)(2,1)}, u32[]{:S(2)}, u32[]{:S(2)}) collective-permute-start(bf16[8,144,512]{2,1,0:T(8,128)(2,1)} %add_convert_fusion.6), channel_id=1, source_target_pairs={{0,2},{1,3},{2,0},{3,1},{4,6},{5,7},{6,4},{7,5},{8,9},{9,8},{10,11... | collective-permute-start | bytes 3538952 | tf_op jit(solution)/shard_map/ppermute | solution.py:706
  504.1 35.2 %collective-permute-start.57 = (bf16[2,4,144,512]{3,2,1,0:T(8,128)(2,1)}, bf16[2,4,144,512]{3,2,1,0:T(8,128)(2,1)}, u32[]{:S(2)}, u32[]{:S(2)}) collective-permute-start(bf16[2,4,144,512]{3,2,1,0:T(8,128)(2,1)} %fusion.2), channel_id=1, source_target_pairs={{0,8},{4,12},{8,0},{12,4},{16,24},{20,28},{24,16},{28,20},{1,9},{5... | collective-permute-start | bytes 3538952 | tf_op jit(solution)/shard_map/ppermute | solution.py:709
  509.2 29.0 %collective-permute-start.58 = (bf16[20,16,512]{2,1,0:T(8,128)(2,1)}, bf16[20,16,512]{2,1,0:T(8,128)(2,1)}, u32[]{:S(2)}, u32[]{:S(2)}) collective-permute-start(bf16[20,16,512]{2,1,0:T(8,128)(2,1)} %slice.221), channel_id=1, source_target_pairs={{0,16},{4,20},{8,24},{12,28},{16,0},{20,4},{24,8},{28,12},{1,17},{... | collective-permute-start | bytes 983048 | tf_op jit(solution)/shard_map/ppermute | solution.py:709
  541.9 42.3 %collective-permute-start.60 = (bf16[2,4,144,512]{3,2,1,0:T(8,128)(2,1)}, bf16[2,4,144,512]{3,2,1,0:T(8,128)(2,1)}, u32[]{:S(2)}, u32[]{:S(2)}) collective-permute-start(bf16[2,4,144,512]{3,2,1,0:T(8,128)(2,1)} %add_convert_fusion.2), channel_id=1, source_target_pairs={{0,2},{1,3},{2,0},{3,1},{4,6},{5,7},{6,4},{7,5},{8,9},{9,8},{10,11... | collective-permute-start | bytes 3538952 | tf_op jit(solution)/shard_map/ppermute | solution.py:706
  544.9 39.3 %collective-permute-start.59 = (bf16[2,4,144,512]{3,2,1,0:T(8,128)(2,1)}, bf16[2,4,144,512]{3,2,1,0:T(8,128)(2,1)}, u32[]{:S(2)}, u32[]{:S(2)}) collective-permute-start(bf16[2,4,144,512]{3,2,1,0:T(8,128)(2,1)} %add_convert_fusion.3), channel_id=1, source_target_pairs={{0,1},{1,0},{2,3},{3,2},{4,5},{5,4},{6,7},{7,6},{8,10},{9,11},{10,... | collective-permute-start | bytes 3538952 | tf_op jit(solution)/shard_map/ppermute | solution.py:706
  545.7 39.5 %collective-permute-start.61 = (bf16[2,4,144,512]{3,2,1,0:T(8,128)(2,1)}, bf16[2,4,144,512]{3,2,1,0:T(8,128)(2,1)}, u32[]{:S(2)}, u32[]{:S(2)}) collective-permute-start(bf16[2,4,144,512]{3,2,1,0:T(8,128)(2,1)} %get-tuple-element.820), channel_id=1, source_target_pairs={{0,8},{4,12},{8,0},{12,4},{16,24},{20,28},{24,16},{28,20},{1,9},{5... | collective-permute-start | bytes 3538952 | tf_op jit(solution)/shard_map/ppermute | solution.py:709
  549.4 34.8 %collective-permute-start.62 = (bf16[2,2,144,512]{3,2,0,1:T(8,128)(2,1)}, bf16[2,2,144,512]{3,2,0,1:T(8,128)(2,1)}, u32[]{:S(2)}, u32[]{:S(2)}) collective-permute-start(bf16[2,2,144,512]{3,2,0,1:T(8,128)(2,1)} %slice_bitcast_fusion.1), channel_id=1, source_target_pairs={{0,16},{4,20},{8,24},{12,28},{16,0},{20,4},{24,8},{28,12},{1,17},{... | collective-permute-start | bytes 1769480 | tf_op jit(solution)/shard_map/ppermute | solution.py:709
  592.0 29.3 %collective-permute-start.63 = (bf16[2,2,144,512]{3,2,0,1:T(8,128)(2,1)}, bf16[2,2,144,512]{3,2,0,1:T(8,128)(2,1)}, u32[]{:S(2)}, u32[]{:S(2)}) collective-permute-start(bf16[2,2,144,512]{3,2,0,1:T(8,128)(2,1)} %slice_bitcast_fusion), channel_id=1, source_target_pairs={{0,16},{4,20},{8,24},{12,28},{16,0},{20,4},{24,8},{28,12},{1,17},{... | collective-permute-start | bytes 1769480 | tf_op jit(solution)/shard_map/ppermute | solution.py:709
  (196 other events, 2069.9 us)

commit v3 on v2

--- a/solution.py
+++ b/solution.py
@@ -505,7 +505,7 @@
         ),
         out_shape=[jax.ShapeDtypeStruct((8, high, chunk), BF16)] * 2
         + [jax.ShapeDtypeStruct((2, 4, high, chunk), BF16)] * 2,
-        compiler_params=pltpu.CompilerParams(vmem_limit_bytes=28 * 2**20, dimension_semantics=("arbitrary",) * 2),
+        compiler_params=pltpu.CompilerParams(vmem_limit_bytes=54 * 2**20, dimension_semantics=("arbitrary",) * 2),
         cost_estimate=LIGHT,
         name="weight_gradients",
     )(order, x_turned, kept_turned, draw_turned, own, far, emit_own, emit_far)
@@ -795,6 +795,7 @@
 
     w_rec[3, 1] = jnp.concatenate(last_piece, axis=0)
     w_rec[3, 3] = core_swap(w_rec[3, 1])
+    turned[3] = turn_of(3)
     x_turned = turn_rows(x_flat, x_met)
     g_sent = by_other(g_dirs)
     w_rec, turned, x_turned, g_sent = after((w_rec, turned, x_turned, g_sent))
@@ -814,36 +815,30 @@
     emit_met = core_swap(flat(emit_far))
     kept = flat(kept)
     kept_met = core_swap(kept)
-    turned[3] = turn_of(3)
-    hid_here, hid_there, kept, kept_met, emit_met, turned, chain = after(
-        (hid_here, hid_there, kept, kept_met, emit_met, turned, (pre, cell, raw))
-    )
 
     def over_cols(value, mask):
         return lax.ppermute(value, "cols", [(j, j ^ mask) for j in range(4)])
 
-    hid_both = jnp.concatenate([by_dir((hid_here, hid_there)), by_other((hid_here, hid_there))], axis=2)
-    hid_parts = [hid_both] + [over_cols(hid_both, mask) for mask in (1, 2, 3)]
-
-    kept_turned = turn_rows(kept, kept_met)
     slabs, draw, bias_sums = run_backward(
-        *chain,
+        pre,
+        cell,
+        raw,
         g_run,
         keep_run,
         [w for b in range(BLOCKS) for w in turned[b][0]],
         [p for b in range(BLOCKS) for p in turned[b][1]],
     )
-    hid_parts, kept_turned, slabs, draw, bias_sums, emit_own, emit_met = after(
-        (hid_parts, kept_turned, slabs, draw, bias_sums, emit_own, emit_met)
+    hid_here, hid_there, kept, kept_met, slabs, draw, bias_sums, emit_own, emit_met = after(
+        (hid_here, hid_there, kept, kept_met, slabs, draw, bias_sums, emit_own, emit_met)
     )
 
     slabs = [[flat(value) for value in block] for block in slabs]
     emit_own, draw = flat(emit_own), flat(draw)
-    far = {3: core_swap(slabs[3][1])}
-    draw_met = core_swap(draw)
     bias_parts = jnp.sum(bias_sums, axis=0).reshape(BLOCKS, 4, 2, 2 * piece)
     bias_half = bias_parts[:, :, 0] + core_swap(bias_parts[:, :, 1])
-    far, draw_met, slabs, bias_half = after((far, draw_met, slabs, bias_half))
+    draw_met, far = core_swap(draw), {3: core_swap(slabs[3][1])}
+    far[1] = core_swap(after((slabs[1][1], draw_met))[0])
+    kept_turned, draw_turned = turn_rows(kept, kept_met), turn_rows(draw, draw_met)
 
     def grads(b):
         left = (x_turned, kept_turned, draw_turned)
@@ -858,36 +853,33 @@
     def flip(value):
         return jnp.concatenate([value[1:], value[:1]], axis=0)
 
-    draw_turned = turn_rows(draw, draw_met)
     opposite = grads(3)
-    for b in (1, 2):
-        far[b] = core_swap(slabs[b][1])
-    bias_met = [over_chips(bias_half[1], True), over_chips(bias_half[2], False), over_cols(bias_half[3], 3)]
-    far, opposite, draw_turned, slabs, bias_half, bias_met = after(
-        (far, opposite, draw_turned, slabs, bias_half, bias_met)
+    far, opposite, kept_turned, draw_turned, slabs, bias_half = after(
+        (far, opposite, kept_turned, draw_turned, slabs, bias_half)
     )
 
     relay_a, relay_b = over_chips(opposite[0], True), over_chips(opposite[1], False)
     met = pair_swap(opposite[3])
-    far[0] = core_swap(slabs[0][1])
-    bias_half = bias_half[0] + bias_met[0] + bias_met[1] + bias_met[2]
-    bias_half = jnp.where(pair == 0, bias_half, jnp.concatenate([bias_half[:, piece:], bias_half[:, :piece]], axis=1))
-    bias_half = bias_half + pair_swap(bias_half)
-    near, other = grads(1), grads(2)
-    far, relay_a, relay_b, met, near, other, slabs, bias_half = after(
-        (far, relay_a, relay_b, met, near, other, slabs, bias_half)
+    far[2] = core_swap(slabs[2][1])
+    bias_met = [over_chips(bias_half[1], True), over_chips(bias_half[2], False)]
+    near = grads(1)
+    other = grads(2)
+    hid_both = jnp.concatenate([by_dir((hid_here, hid_there)), by_other((hid_here, hid_there))], axis=2)
+    hid_both = steps_first(hid_both).reshape(own_tokens, 2 * model)
+    far, relay_a, relay_b, met, near, other, slabs, bias_met, hid_both = after(
+        (far, relay_a, relay_b, met, near, other, slabs, bias_met, hid_both)
     )
 
     near_a, other_b = over_chips(near[0], True), over_chips(other[1], False)
     other_met = pair_swap(near[3])
+    far[0] = core_swap(slabs[0][1])
+    bias_met = bias_met + [over_cols(bias_half[3], 3)]
+    near_b, other_a = add(near[1], relay_b), add(other[0], relay_a)
     opposite1 = add(opposite[2], flip(met))
-    near_b, other_a = add(near[1], relay_b), add(other[0], relay_a)
     own = grads(0)
     near1, other1, own0, own1 = near[2:], other[2:], own[:2], own[2:]
-    bias_there = half_swap(bias_half)
-    bias_half = jnp.stack([by_dir((bias_half, bias_there)), by_other((bias_half, bias_there))])
-    near_a, other_b, other_met, opposite1, near_b, other_a, other1, own0, own1, slabs, bias_half, hid_parts = after(
-        (near_a, other_b, other_met, opposite1, near_b, other_a, other1, own0, own1, slabs, bias_half, hid_parts)
+    near_a, other_b, other_met, opposite1, near_b, other_a, other1, own0, own1, slabs, bias_met = after(
+        (near_a, other_b, other_met, opposite1, near_b, other_a, other1, own0, own1, slabs, bias_met)
     )
 
     near_b, other_a = over_chips(near_b, True), over_chips(other_a, False)
@@ -895,62 +887,78 @@
     wide = None
     for b in range(BLOCKS):
         wide = add_input_grad(slabs[b], [w_in[b, part] for part in range(PARTS)], wide)
-    bias_total = jnp.concatenate(by_side(bias_half, core_swap(bias_half)), axis=2)
-    near_b, other_a, near_met, wide, own1, bias_total, hid_parts = after(
-        (near_b, other_a, near_met, wide, own1, bias_total, hid_parts)
+    bias_half = bias_half[0] + bias_met[0] + bias_met[1] + bias_met[2]
+    bias_half = jnp.where(pair == 0, bias_half, jnp.concatenate([bias_half[:, piece:], bias_half[:, :piece]], axis=1))
+    bias_met = pair_swap(bias_half)
+    own0 = [add(own0[0], near_a), add(own0[1], other_b)]
+    other_a1, other_b1 = add(other1[0][0], other_met[1]), add(other1[0][1], other_met[0])
+    dx = in_run(wide.reshape(STEPS, rows, model))
+    dx, dx_sent = dx[:, :share], dx[:, share:].astype(BF16)
+    near_b, other_a, near_met, dx, dx_sent, own0, own1, bias_met, other_a1, other_b1 = after(
+        (near_b, other_a, near_met, dx, dx_sent, own0, own1, bias_met, other_a1, other_b1)
     )
 
     relay_a, relay_b = over_chips(opposite1[0], True), over_chips(opposite1[1], False)
-    sums0 = jnp.stack([add(own0[0], near_a, other_a), add(own0[1], near_b, other_b)])
-    count = sums0.shape[1] // 2
-    sums0_met = pair_swap(sums0[:, count:])
-    dx = in_run(wide.reshape(STEPS, rows, model))
-    dx, dx_met = dx[:, :share], half_swap(dx[:, share:].astype(BF16))
-    hid_parts = [steps_first(value).reshape(own_tokens, 2 * model) for value in hid_parts]
-    relay_a, relay_b, sums0, sums0_met, dx, dx_met, own1, hid_parts = after(
-        (relay_a, relay_b, sums0, sums0_met, dx, dx_met, own1, hid_parts)
-    )
-
-    near1 = add(near1[0], flip(near_met), jnp.stack([jnp.zeros_like(relay_b), relay_b]))
-    other1 = add(other1[0], flip(other_met), jnp.stack([relay_a, jnp.zeros_like(relay_a)]))
-    near_met, other_met = over_chips(near1, True), over_chips(other1, False)
+    near_a1, near_b1 = add(near1[0][0], near_met[1]), add(near1[0][1], near_met[0])
+    near_a1, other_b1 = over_chips(near_a1, True), over_chips(other_b1, False)
+    count = own0[0].shape[0] // 2
+    sums0_met = pair_swap(jnp.stack([add(own0[0][count:], other_a[count:]), add(own0[1][count:], near_b[count:])]))
+    sums0 = [add(own0[0][:count], other_a[:count]), add(own0[1][:count], near_b[:count])]
+    bias_half = bias_half + bias_met
+    lines, rest = [], bias_half
+    for _ in range(3):
+        lines.append(lax.reduce_precision(rest, 8, 7))
+        rest = rest - lines[-1]
+    lines = jnp.concatenate(lines + [jnp.zeros_like(rest)], axis=0).astype(BF16)
+    dx_met = half_swap(jnp.concatenate([dx_sent.reshape(own_tokens, model), lines], axis=0))
+    near_a1, near_b1, other_a1, other_b1, relay_a, relay_b, sums0, sums0_met, dx, dx_met, own1, bias_half = after(
+        (near_a1, near_b1, other_a1, other_b1, relay_a, relay_b, sums0, sums0_met, dx, dx_met, own1, bias_half)
+    )
+
+    near_b1, other_a1 = over_chips(add(near_b1, relay_b), True), over_chips(add(other_a1, relay_a), False)
     own_met = pair_swap(own1[1])
-    by_half = lambda value: value.reshape(2, 2, 2, *value.shape[2:])
-    sums0 = by_half(add(sums0[:, :count], flip(sums0_met)))
-    sums0_met = half_swap(sums0[:, 1])
+    sums0_sent = jnp.stack([add(sums0[n][2:], sums0_met[1 - n][2:]) for n in range(2)])
+    there0 = half_swap(sums0_sent)
+    here0 = jnp.stack([add(sums0[n][:2], sums0_met[1 - n][:2]) for n in range(2)])
+    bias_there = dx_met[own_tokens:].astype(F32).reshape(4, 4, 2 * piece)
+    bias_there = bias_there[0] + bias_there[1] + bias_there[2]
+    bias_half = jnp.stack([by_dir((bias_half, bias_there)), by_other((bias_half, bias_there))])
+    dx_met = dx_met[:own_tokens].reshape(STEPS, share, model)
     dx = dx + dx_met.astype(F32) + g_dirs[0].astype(F32) + g_dirs[1].astype(F32)
     dx = steps_first(dx.astype(BF16)).reshape(own_tokens, model)
-    def by_column(parts):
-        whole_rows = jnp.zeros((BLOCKS * parts[0].shape[0], parts[0].shape[1]), parts[0].dtype)
-        for mask, value in enumerate(parts):
-            whole_rows = lax.dynamic_update_slice(whole_rows, value, ((col ^ mask) * value.shape[0], 0))
-        return whole_rows
-
-    block_out = layer_sum(col, inputs, hid_parts)
-    near_met, other_met, own_met, sums0, sums0_met, dx, own1, block_out = after(
-        (near_met, other_met, own_met, sums0, sums0_met, dx, own1, block_out)
-    )
-
-    sums1 = by_half(add(own1[0], flip(own_met), near_met, other_met))
-    sums1_met = half_swap(sums1[:, 1])
+    share_width = model // 4
+    slice_for = lambda mask: lax.dynamic_slice_in_dim(dx, (col ^ mask) * share_width, share_width, 1)
+    outgoing = [jnp.concatenate([hid_both, slice_for(mask)], axis=1) for mask in range(4)]
+    incoming = [outgoing[0], None, None, over_cols(outgoing[3], 3)]
+    own_a1, own_b1 = add(own1[0][0], near_a1), add(own1[0][1], other_b1)
+    near_b1, other_a1, own_met, here0, there0, own_a1, own_b1, incoming[0], incoming[3], outgoing, bias_half = after(
+        (near_b1, other_a1, own_met, here0, there0, own_a1, own_b1, incoming[0], incoming[3], outgoing, bias_half)
+    )
+
+    parts1 = ((own_a1, own_met[1], other_a1), (own_b1, own_met[0], near_b1))
+    there1 = half_swap(jnp.stack([add(*(value[2:] for value in parts)) for parts in parts1]))
+    here1 = jnp.stack([add(*(value[:2] for value in parts)) for parts in parts1])
 
     def two_directions(here, there):
         both = jnp.stack([here, there])
         return both[:, :, 0], both[:, :, 1]
 
-    kept0, sent0 = two_directions(sums0[:, 0], sums0_met)
+    kept0, sent0 = two_directions(here0, there0)
     met0 = core_swap(sent0)
-    slice_for = lambda at: lax.dynamic_slice_in_dim(dx, at * (model // 4), model // 4, 1)
-    dx_parts = [slice_for(col ^ mask) for mask in range(4)]
-    dx_parts = [dx_parts[0]] + [over_cols(dx_parts[mask], mask) for mask in (1, 2, 3)]
-
-    sums1, sums1_met, kept0, met0, dx_parts = after((sums1, sums1_met, kept0, met0, dx_parts))
-
-    kept1, sent1 = two_directions(sums1[:, 0], sums1_met)
+    incoming[1], incoming[2] = over_cols(outgoing[1], 1), over_cols(outgoing[2], 2)
+    block_out = layer_sum(col, inputs, [value[:, : 2 * model] for value in incoming])
+    input_grad = jnp.zeros((BLOCKS * own_tokens, share_width), BF16)
+    for mask, value in enumerate(incoming):
+        input_grad = lax.dynamic_update_slice(input_grad, value[:, 2 * model :], ((col ^ mask) * own_tokens, 0))
+    bias_total = jnp.concatenate(by_side(bias_half, core_swap(bias_half)), axis=2)
+    here1, there1, kept0, met0, block_out, input_grad, bias_total = after(
+        (here1, there1, kept0, met0, block_out, input_grad, bias_total)
+    )
+
+    kept1, sent1 = two_directions(here1, there1)
     met1 = core_swap(sent1)
     weight_share, proj_share = assemble(order, kept0, kept1, met0, met1, 2 * model // 8)
     proj_share = jnp.swapaxes(proj_share, 1, 2)
-    input_grad = by_column(dx_parts)
     return (block_out, input_grad, weight_share, bias_total, proj_share)
 
 

time: 644 us -> 592 us (0.919)
  local copies, waits for them, and re-layouts: 104 us -> 54.9 us
  Pallas kernels: 309 us -> 323 us
  waiting for transfers between devices: 127 us -> 113 us
    unnamed x319 -> x259, local copies, waits for them, and re-layouts: 78.1 us -> 37.7 us
    ppermute x41 -> x40, waiting for transfers between devices: 95.9 us -> 64.6 us  [over_rows(): return lax.ppermute(value, 'rows', [(r, r ^ mask) for r in range(8)])]
    pallas_call x4, Pallas kernels: 52.5 us -> 68.2 us  [block_grads(): pl.pallas_call(block_kernel, grid_spec=pltpu.PrefetchScalarGridSpec(num_s...]
    ppermute x7 -> x4, waiting for transfers between devices: 4.63 us -> 14.5 us  [over_cols(): return lax.ppermute(value, 'cols', [(j, j ^ mask) for j in range(4)])]
    ppermute x21 -> x23, waiting for transfers between devices: 26.5 us -> 34.2 us  [over_chips(): return lax.ppermute(value, ('rows', 'cols'), pairs)]
    convert_element_type x7 -> x10, other arithmetic: 14.6 us -> 18.4 us  [add(): return total.astype(BF16)]
    ppermute x21 -> x23, starting transfers between devices: 22.1 us -> 25.5 us  [over_chips(): return lax.ppermute(value, ('rows', 'cols'), pairs)]
    ppermute x41 -> x40, starting transfers between devices: 28.1 us -> 26.3 us  [over_rows(): return lax.ppermute(value, 'rows', [(r, r ^ mask) for r in range(8)])]
  transfers between devices with their start and end apart: 69 -> 67, of which waited for: 29 -> 27; matrix products, arithmetic and copies ran while one was open for 7% -> 7% of each run, Pallas kernels for 47% -> 53%
where the time goes in v3:
time: 592 us; the launch traced here: 583 us
  Pallas kernels  323 us (55%)
  waiting for transfers between devices  113 us (19%)
  starting transfers between devices  56.4 us (10%)
  local copies, waits for them, and re-layouts  54.9 us (9%)
  other arithmetic  31.5 us (5%)
    pallas_call x1, Pallas kernels, run_backward(): pl.pallas_call(backward_kernel, grid=(steps,), out_shape=tuple([shape(hal...  86.9 us
    pallas_call x1, Pallas kernels, run_forward(): pl.pallas_call(forward_kernel, grid=(steps,), out_shape=tuple((jax.ShapeD...  85.7 us
    pallas_call x4, Pallas kernels, block_grads(): pl.pallas_call(block_kernel, grid_spec=pltpu.PrefetchScalarGridSpec(num_s...  68.2 us
    ppermute x40, waiting for transfers between devices, over_rows(): return lax.ppermute(value, 'rows', [(r, r ^ mask) for r in range(8)])  64.6 us
    unnamed x259, local copies, waits for them, and re-layouts  37.7 us
    ppermute x23, waiting for transfers between devices, over_chips(): return lax.ppermute(value, ('rows', 'cols'), pairs)  34.2 us
    pallas_call x8, Pallas kernels, own_piece(): pl.pallas_call(own_piece_kernel, grid_spec=pltpu.PrefetchScalarGridSpec(n...  28.7 us
    ppermute x40, starting transfers between devices, over_rows(): return lax.ppermute(value, 'rows', [(r, r ^ mask) for r in range(8)])  26.3 us
  transfers between devices with their start and end apart: 67, of which 27 were waited for; matrix products, arithmetic and copies ran while one was open for 7% of the time, Pallas kernels for 53%

profile of v3, /device:TPU:0, one launch (start us, length us, event | category | flops | bytes accessed | tf_op | source)
XLA Modules:
  0.0 582.5 jit_solution(9484690108969033724)
XLA Ops:
  1.3 5.6 own_piece.8.w0.refs_2_
  19.3 5.8 copy-done.2
  25.1 3.3 own_piece.10.refs_0_.refs_4_.refs_5_
  41.6 5.8 copy-done.4
  47.4 3.3 own_piece.13.refs_1_.refs_5_.refs_6_
  50.7 3.3 own_piece.11.w2.refs_4_
  59.0 5.8 collective-permute-done.4.w1.refs_3_
  70.3 3.3 own_piece.14.refs_2_.refs_6_.refs_7_
  73.7 3.3 own_piece.15.refs_3_.refs_7_.refs_8_
  82.6 11.8 %collective-permute-done.8.w1.refs_3_ = bf16[528,1024]{1,0:T(8,128)(2,1)S(1)} collective-permute-done((bf16[528,1024]{1,0:T(8,128)(2,1)S(1)}, bf16[528,1024]{1,0:T(8,128)(2,1)S(1)}, u32[]{:S(2)}, u32[]{:S(2)}) %collective-permute-start.8) | collective-permute-done | bytes 1081376 | tf_op jit(solution)/shard_map/ppermute | solution.py:706
  94.6 4.1 collective-permute-done.12.refs_0_.refs_4_.refs_17_
  111.1 4.8 input_gates.6
  118.3 4.8 input_gates.5
  125.4 4.5 collective-permute-done.16.refs_1_.refs_5_.refs_10_
  157.5 85.7 %forward_chain.1 = (bf16[20,32,16384]{2,1,0:T(8,128)(2,1)}, f32[20,32,4096]{2,1,0:T(8,128)}, bf16[20,32,2048]{2,1,0:T(8,128)(2,1)}, bf16[20,32,2048]{2,1,0:T(8,1...) custom-call(bf16[20,32,4096]{2,1,0:T(8,128)(2,1)} %bitcast.175, ...), custom_call_target="tpu_custom_call" | custom-call | flops 107374182400 | bytes 83886080 | tf_op jit(solution)/shard_map/forward_chain/pallas_call | solution.py:322
  246.9 86.9 %backward_chain.1 = (bf16[20,32,2048]{2,1,0:T(8,128)(2,1)}, bf16[20,32,2048]{2,1,0:T(8,128)(2,1)}, bf16[20,32,2048]{2,1,0:T(8,128)(2,1)}, bf16[20,32,2048]{2,1,0...) custom-call(bf16[20,32,16384]{2,1,0:T(8,128)(2,1)} %get-tuple-elemen, ...), custom_call_target="tpu_custom_call" | custom-call | flops 107374182400 | bytes 83886080 | tf_op jit(solution)/shard_map/backward_chain/pallas_call | solution.py:421
  341.5 17.1 %weight_gradients.4 = (bf16[8,144,512]{2,1,0:T(8,128)(2,1)}, bf16[8,144,512]{2,1,0:T(8,128)(2,1)}, bf16[2,4,144,512]{3,2,1,0:T(8,128)(2,1)}, bf16[2,4,144,512]{3,2,1,0:T(8,128)(2,1)}) custom-call(s32[3]{0:T(128)} %pad_add_fusion.4.order_ref, bf16[512,1280]{1,0:T(8,128)(2,1)} %copy-done.6, bf16[512,1280]{1,0:T(8,128)(2,1)} %copy-done.7, ...), custom_call_target="tpu_custom_call" | custom-call | flops 1 | bytes 1 | tf_op jit(solution)/shard_map/weight_gradients/pallas_call | solution.py:497
  367.2 16.9 %weight_gradients.5 = (bf16[8,144,512]{2,1,0:T(8,128)(2,1)}, bf16[8,144,512]{2,1,0:T(8,128)(2,1)}, bf16[2,4,144,512]{3,2,1,0:T(8,128)(2,1)}, bf16[2,4,144,512]{3,2,1,0:T(8,128)(2,1)}) custom-call(s32[3]{0:T(128)} %pad_add_fusion.4.order_ref, bf16[512,1280]{1,0:T(8,128)(2,1)} %copy-done.6, bf16[512,1280]{1,0:T(8,128)(2,1)} %copy-done.7, ...), custom_call_target="tpu_custom_call" | custom-call | flops 1 | bytes 1 | tf_op jit(solution)/shard_map/weight_gradients/pallas_call | solution.py:497
  384.1 16.9 %weight_gradients.6 = (bf16[8,144,512]{2,1,0:T(8,128)(2,1)}, bf16[8,144,512]{2,1,0:T(8,128)(2,1)}, bf16[2,4,144,512]{3,2,1,0:T(8,128)(2,1)}, bf16[2,4,144,512]{3,2,1,0:T(8,128)(2,1)}) custom-call(s32[3]{0:T(128)} %pad_add_fusion.4.order_ref, bf16[512,1280]{1,0:T(8,128)(2,1)} %copy-done.6, bf16[512,1280]{1,0:T(8,128)(2,1)} %copy-done.7, ...), custom_call_target="tpu_custom_call" | custom-call | flops 1 | bytes 1 | tf_op jit(solution)/shard_map/weight_gradients/pallas_call | solution.py:497
  414.2 17.3 %weight_gradients.7 = (bf16[8,144,512]{2,1,0:T(8,128)(2,1)}, bf16[8,144,512]{2,1,0:T(8,128)(2,1)}, bf16[2,4,144,512]{3,2,1,0:T(8,128)(2,1)}, bf16[2,4,144,512]{3,2,1,0:T(8,128)(2,1)}) custom-call(s32[3]{0:T(128)} %pad_add_fusion.4.order_ref, bf16[512,1280]{1,0:T(8,128)(2,1)} %copy-done.6, bf16[512,1280]{1,0:T(8,128)(2,1)} %copy-done.7, ...), custom_call_target="tpu_custom_call" | custom-call | flops 1 | bytes 1 | tf_op jit(solution)/shard_map/weight_gradients/pallas_call | solution.py:497
  437.0 4.6 input_gradient.4.refs_6_
  441.7 4.5 input_gradient.5.refs_6_
  446.4 4.5 input_gradient.6.refs_6_
  451.0 3.4 input_gradient.7
  474.4 8.7 %collective-permute-done.52 = bf16[4,144,512]{2,1,0:T(8,128)(2,1)} collective-permute-done((bf16[4,144,512]{2,1,0:T(8,128)(2,1)}, bf16[4,144,512]{2,1,0:T(8,128)(2,1)}, u32[]{:S(2)}, u32[]{:S(2)}) %collective-permute-start.52) | collective-permute-done | bytes 589856 | tf_op jit(solution)/shard_map/ppermute | solution.py:706
  484.4 13.9 %collective-permute-done.55 = bf16[336,512]{1,0:T(8,128)(2,1)S(1)} collective-permute-done((bf16[336,512]{1,0:T(8,128)(2,1)}, bf16[336,512]{1,0:T(8,128)(2,1)S(1)}, u32[]{:S(2)}, u32[]{:S(2)}) %collective-permute-start.55) | collective-permute-done | bytes 344096 | tf_op jit(solution)/shard_map/ppermute | solution.py:709
  514.6 13.7 %collective-permute-done.59 = bf16[2,2,144,512]{3,2,0,1:T(8,128)(2,1)S(1)} collective-permute-done((bf16[2,2,144,512]{3,2,0,1:T(8,128)(2,1)S(1)}, bf16[2,2,144,512]{3,2,0,1:T(8,128)(2,1)S(1)}, u32[]{:S(2)}, u32[]{:S(2)}) %collective-permute-start.59) | collective-permute-done | bytes 589856 | tf_op jit(solution)/shard_map/ppermute | solution.py:709
  528.5 14.4 %collective-permute-done.58 = bf16[2,4,144,512]{3,2,1,0:T(8,128)(2,1)S(1)} collective-permute-done((bf16[2,4,144,512]{3,2,1,0:T(8,128)(2,1)S(1)}, bf16[2,4,144,512]{3,2,1,0:T(8,128)(2,1)S(1)}, u32[]{:S(2)}, u32[]{:S(2)}) %collective-permute-start.58) | collective-permute-done | bytes 1179680 | tf_op jit(solution)/shard_map/ppermute | solution.py:709
  547.3 14.5 %collective-permute-done.63 = bf16[320,1152]{1,0:T(8,128)(2,1)S(1)} collective-permute-done((bf16[320,1152]{1,0:T(8,128)(2,1)S(1)}, bf16[320,1152]{1,0:T(8,128)(2,1)S(1)}, u32[]{:S(2)}, u32[]{:S(2)}) %collective-permute-start.63) | collective-permute-done | bytes 737312 | tf_op jit(solution)/shard_map/ppermute | solution.py:820
  562.0 4.3 layer_sum.1
  566.4 8.2 %collective-permute-done.61 = bf16[2,2,144,512]{3,2,0,1:T(8,128)(2,1)S(1)} collective-permute-done((bf16[2,2,144,512]{3,2,0,1:T(8,128)(2,1)S(1)}, bf16[2,2,144,512]{3,2,0,1:T(8,128)(2,1)S(1)}, u32[]{:S(2)}, u32[]{:S(2)}) %collective-permute-start.61) | collective-permute-done | bytes 589856 | tf_op jit(solution)/shard_map/ppermute | solution.py:709
  576.8 5.3 assemble_gradients.1
  (487 shorter events, 169.2 us)
Async XLA Ops:
  7.0 30.7 %collective-permute-start = (bf16[528,1024]{1,0:T(8,128)(2,1)}, bf16[528,1024]{1,0:T(8,128)(2,1)}, u32[]{:S(2)}, u32[]{:S(2)}) collective-permute-start(bf16[528,1024]{1,0:T(8,128)(2,1)} %own_piece.8.w0.refs_2_), channel_id=1, source_target_pairs={{0,1},{1,0},{2,3},{3,2},{4,5},{5,4},{6,7},{7,6},{8,10},{9,11},{10,... | collective-permute-start | bytes 3244040 | tf_op jit(solution)/shard_map/ppermute | solution.py:706
  9.9 27.8 %collective-permute-start.1 = (bf16[528,1024]{1,0:T(8,128)(2,1)}, bf16[528,1024]{1,0:T(8,128)(2,1)}, u32[]{:S(2)}, u32[]{:S(2)}) collective-permute-start(bf16[528,1024]{1,0:T(8,128)(2,1)} %own_piece.8.w0.refs_2_), channel_id=1, source_target_pairs={{0,2},{1,3},{2,0},{3,1},{4,6},{5,7},{6,4},{7,5},{8,9},{9,8},{10,11... | collective-permute-start | bytes 3244040 | tf_op jit(solution)/shard_map/ppermute | solution.py:706
  37.7 29.7 %collective-permute-start.7 = (bf16[640,1024]{1,0:T(8,128)(2,1)S(1)}, bf16[640,1024]{1,0:T(8,128)(2,1)S(1)}, u32[]{:S(2)}, u32[]{:S(2)}) collective-permute-start(bf16[640,1024]{1,0:T(8,128)(2,1)S(1)} %own_piece.10.refs_0_.refs_4_.refs_5_), channel_id=1, source_target_pairs={{0,1},{1,0},{2,3},{3,2},{4,5},{5,4},{6,7},{7,6},{8,10},{9,11},{10,... | collective-permute-start | bytes 3932168 | tf_op jit(solution)/shard_map/ppermute | solution.py:706
  38.3 26.5 %collective-permute-start.4 = (bf16[528,1024]{1,0:T(8,128)(2,1)}, bf16[528,1024]{1,0:T(8,128)(2,1)S(1)}, u32[]{:S(2)}, u32[]{:S(2)}) collective-permute-start(bf16[528,1024]{1,0:T(8,128)(2,1)} %collective-permute-done.w0.refs_2_), channel_id=1, source_target_pairs={{0,8},{4,12},{8,0},{12,4},{16,24},{20,28},{24,16},{28,20},{1,9},{5... | collective-permute-start | bytes 3244040 | tf_op jit(solution)/shard_map/ppermute | solution.py:709
  40.1 26.3 %collective-permute-start.6 = (bf16[528,1024]{1,0:T(8,128)(2,1)}, bf16[528,1024]{1,0:T(8,128)(2,1)S(1)}, u32[]{:S(2)}, u32[]{:S(2)}) collective-permute-start(bf16[528,1024]{1,0:T(8,128)(2,1)} %collective-permute-done.w0.refs_2_), channel_id=1, source_target_pairs={{0,2},{1,3},{2,0},{3,1},{4,6},{5,7},{6,4},{7,5},{8,9},{9,8},{10,11... | collective-permute-start | bytes 3244040 | tf_op jit(solution)/shard_map/ppermute | solution.py:706
  67.5 27.1 %collective-permute-start.11 = (bf16[640,1024]{1,0:T(8,128)(2,1)S(1)}, bf16[640,1024]{1,0:T(8,128)(2,1)S(1)}, u32[]{:S(2)}, u32[]{:S(2)}) collective-permute-start(bf16[640,1024]{1,0:T(8,128)(2,1)S(1)} %collective-permute-done.7.refs_0_.refs_4_.refs_9_), channel_id=1, source_target_pairs={{0,4},{4,0},{8,12},{12,8},{16,20},{20,16},{24,28},{28,24},{1,5},{5... | collective-permute-start | bytes 3932168 | tf_op jit(solution)/shard_map/ppermute | solution.py:709
  67.5 31.2 %collective-permute-start.12 = (bf16[640,1024]{1,0:T(8,128)(2,1)S(1)}, bf16[640,1024]{1,0:T(8,128)(2,1)S(1)}, u32[]{:S(2)}, u32[]{:S(2)}) collective-permute-start(bf16[640,1024]{1,0:T(8,128)(2,1)S(1)} %collective-permute-done.7.refs_0_.refs_4_.refs_9_), channel_id=1, source_target_pairs={{0,2},{1,3},{2,0},{3,1},{4,6},{5,7},{6,4},{7,5},{8,9},{9,8},{10,11... | collective-permute-start | bytes 3932168 | tf_op jit(solution)/shard_map/ppermute | solution.py:706
  68.2 26.1 %collective-permute-start.8 = (bf16[528,1024]{1,0:T(8,128)(2,1)S(1)}, bf16[528,1024]{1,0:T(8,128)(2,1)S(1)}, u32[]{:S(2)}, u32[]{:S(2)}) collective-permute-start(bf16[528,1024]{1,0:T(8,128)(2,1)S(1)} %copy-done.18), channel_id=1, source_target_pairs={{0,1},{1,0},{2,3},{3,2},{4,5},{5,4},{6,7},{7,6},{8,10},{9,11},{10,... | collective-permute-start | bytes 3244040 | tf_op jit(solution)/shard_map/ppermute | solution.py:706
  98.7 31.2 %collective-permute-start.16 = (bf16[640,1024]{1,0:T(8,128)(2,1)S(1)}, bf16[640,1024]{1,0:T(8,128)(2,1)S(1)}, u32[]{:S(2)}, u32[]{:S(2)}) collective-permute-start(bf16[640,1024]{1,0:T(8,128)(2,1)S(1)} %own_piece.13.refs_1_.refs_5_.refs_6_), channel_id=1, source_target_pairs={{0,1},{1,0},{2,3},{3,2},{4,5},{5,4},{6,7},{7,6},{8,10},{9,11},{10,... | collective-permute-start | bytes 3932168 | tf_op jit(solution)/shard_map/ppermute | solution.py:706
  99.2 30.9 %collective-permute-start.17 = (bf16[640,1024]{1,0:T(8,128)(2,1)S(1)}, bf16[640,1024]{1,0:T(8,128)(2,1)S(1)}, u32[]{:S(2)}, u32[]{:S(2)}) collective-permute-start(bf16[640,1024]{1,0:T(8,128)(2,1)S(1)} %own_piece.10.refs_0_.refs_4_.refs_5_), channel_id=1, source_target_pairs={{0,2},{1,3},{2,0},{3,1},{4,6},{5,7},{6,4},{7,5},{8,9},{9,8},{10,11... | collective-permute-start | bytes 3932168 | tf_op jit(solution)/shard_map/ppermute | solution.py:706
  99.7 30.6 %collective-permute-start.18 = (bf16[640,1024]{1,0:T(8,128)(2,1)S(1)}, bf16[640,1024]{1,0:T(8,128)(2,1)S(1)}, u32[]{:S(2)}, u32[]{:S(2)}) collective-permute-start(bf16[640,1024]{1,0:T(8,128)(2,1)S(1)} %collective-permute-done.7.refs_0_.refs_4_.refs_9_), channel_id=1, source_target_pairs={{0,8},{4,12},{8,0},{12,4},{16,24},{20,28},{24,16},{28,20},{1,9},{5... | collective-permute-start | bytes 3932168 | tf_op jit(solution)/shard_map/ppermute | solution.py:709
  156.1 87.2 %collective-permute-start.27 = (bf16[20,16,512]{2,1,0:T(8,128)(2,1)S(1)}, bf16[20,16,512]{2,1,0:T(8,128)(2,1)S(1)}, u32[]{:S(2)}, u32[]{:S(2)}) collective-permute-start(bf16[20,16,512]{2,1,0:T(8,128)(2,1)S(1)} %get-tuple-element.558), channel_id=1, source_target_pairs={{0,16},{4,20},{8,24},{12,28},{16,0},{20,4},{24,8},{28,12},{1,17},{... | collective-permute-start | bytes 983048 | tf_op jit(solution)/shard_map/ppermute | solution.py:709
  244.6 89.2 %collective-permute-start.30 = (bf16[640,2048]{1,0:T(8,128)(2,1)}, bf16[640,2048]{1,0:T(8,128)(2,1)S(1)}, u32[]{:S(2)}, u32[]{:S(2)}) collective-permute-start(bf16[640,2048]{1,0:T(8,128)(2,1)} %bitcast.205), channel_id=1, source_target_pairs={{0,4},{4,0},{8,12},{12,8},{16,20},{20,16},{24,28},{28,24},{1,5},{5... | collective-permute-start | bytes 7864328 | tf_op jit(solution)/shard_map/ppermute | solution.py:709
  244.9 88.9 %collective-permute-start.28 = (bf16[20,16,512]{2,1,0:T(8,128)(2,1)S(1)}, bf16[20,16,512]{2,1,0:T(8,128)(2,1)S(1)}, u32[]{:S(2)}, u32[]{:S(2)}) collective-permute-start(bf16[20,16,512]{2,1,0:T(8,128)(2,1)S(1)} %get-tuple-element.807), channel_id=1, source_target_pairs={{0,16},{4,20},{8,24},{12,28},{16,0},{20,4},{24,8},{28,12},{1,17},{... | collective-permute-start | bytes 983048 | tf_op jit(solution)/shard_map/ppermute | solution.py:709
  246.5 87.2 %collective-permute-start.29 = (bf16[640,512]{1,0:T(8,128)(2,1)S(1)}, bf16[640,512]{1,0:T(8,128)(2,1)S(1)}, u32[]{:S(2)}, u32[]{:S(2)}) collective-permute-start(bf16[640,512]{1,0:T(8,128)(2,1)S(1)} %bitcast.186), channel_id=1, source_target_pairs={{0,4},{4,0},{8,12},{12,8},{16,20},{20,16},{24,28},{28,24},{1,5},{5... | collective-permute-start | bytes 1966088 | tf_op jit(solution)/shard_map/ppermute | solution.py:709
  358.9 42.1 %collective-permute-start.36 = (bf16[8,144,512]{2,1,0:T(8,128)(2,1)}, bf16[8,144,512]{2,1,0:T(8,128)(2,1)}, u32[]{:S(2)}, u32[]{:S(2)}) collective-permute-start(bf16[8,144,512]{2,1,0:T(8,128)(2,1)} %get-tuple-element.631), channel_id=1, source_target_pairs={{0,1},{1,0},{2,3},{3,2},{4,5},{5,4},{6,7},{7,6},{8,10},{9,11},{10,... | collective-permute-start | bytes 3538952 | tf_op jit(solution)/shard_map/ppermute | solution.py:706
  360.4 40.6 %collective-permute-start.37 = (bf16[8,144,512]{2,1,0:T(8,128)(2,1)}, bf16[8,144,512]{2,1,0:T(8,128)(2,1)}, u32[]{:S(2)}, u32[]{:S(2)}) collective-permute-start(bf16[8,144,512]{2,1,0:T(8,128)(2,1)} %get-tuple-element.632), channel_id=1, source_target_pairs={{0,2},{1,3},{2,0},{3,1},{4,6},{5,7},{6,4},{7,5},{8,9},{9,8},{10,11... | collective-permute-start | bytes 3538952 | tf_op jit(solution)/shard_map/ppermute | solution.py:706
  361.9 39.1 %collective-permute-start.38 = (bf16[2,4,144,512]{3,2,1,0:T(8,128)(2,1)}, bf16[2,4,144,512]{3,2,1,0:T(8,128)(2,1)}, u32[]{:S(2)}, u32[]{:S(2)}) collective-permute-start(bf16[2,4,144,512]{3,2,1,0:T(8,128)(2,1)} %get-tuple-element.633), channel_id=1, source_target_pairs={{0,8},{4,12},{8,0},{12,4},{16,24},{20,28},{24,16},{28,20},{1,9},{5... | collective-permute-start | bytes 3538952 | tf_op jit(solution)/shard_map/ppermute | solution.py:709
  363.6 37.4 %collective-permute-start.39 = (f32[4,512]{1,0:T(4,128)S(1)}, f32[4,512]{1,0:T(4,128)S(1)}, u32[]{:S(2)}, u32[]{:S(2)}) collective-permute-start(f32[4,512]{1,0:T(4,128)S(1)} %get-tuple-element.825), channel_id=1, source_target_pairs={{0,1},{1,0},{2,3},{3,2},{4,5},{5,4},{6,7},{7,6},{8,10},{9,11},{10,... | collective-permute-start | bytes 24584 | tf_op jit(solution)/shard_map/ppermute | solution.py:706
  364.2 36.8 %collective-permute-start.40 = (f32[4,512]{1,0:T(4,128)S(1)}, f32[4,512]{1,0:T(4,128)S(1)}, u32[]{:S(2)}, u32[]{:S(2)}) collective-permute-start(f32[4,512]{1,0:T(4,128)S(1)} %get-tuple-element.824), channel_id=1, source_target_pairs={{0,2},{1,3},{2,0},{3,1},{4,6},{5,7},{6,4},{7,5},{8,9},{9,8},{10,11... | collective-permute-start | bytes 24584 | tf_op jit(solution)/shard_map/ppermute | solution.py:706
  401.1 30.3 %collective-permute-start.45 = (f32[4,512]{1,0:T(4,128)S(1)}, f32[4,512]{1,0:T(4,128)S(1)}, u32[]{:S(2)}, u32[]{:S(2)}) collective-permute-start(f32[4,512]{1,0:T(4,128)S(1)} %get-tuple-element.823), channel_id=1, source_target_pairs={{0,3},{1,2},{2,1},{3,0},{4,7},{5,6},{6,5},{7,4},{8,11},{9,10},{10,... | collective-permute-start | bytes 24584 | tf_op jit(solution)/shard_map/ppermute | solution.py:820
  403.2 28.3 %collective-permute-start.41 = (bf16[8,144,512]{2,1,0:T(8,128)(2,1)}, bf16[8,144,512]{2,1,0:T(8,128)(2,1)}, u32[]{:S(2)}, u32[]{:S(2)}) collective-permute-start(bf16[8,144,512]{2,1,0:T(8,128)(2,1)} %get-tuple-element.655), channel_id=1, source_target_pairs={{0,1},{1,0},{2,3},{3,2},{4,5},{5,4},{6,7},{7,6},{8,10},{9,11},{10,... | collective-permute-start | bytes 3538952 | tf_op jit(solution)/shard_map/ppermute | solution.py:706
  403.8 27.8 %collective-permute-start.42 = (bf16[8,144,512]{2,1,0:T(8,128)(2,1)}, bf16[8,144,512]{2,1,0:T(8,128)(2,1)}, u32[]{:S(2)}, u32[]{:S(2)}) collective-permute-start(bf16[8,144,512]{2,1,0:T(8,128)(2,1)} %get-tuple-element.656), channel_id=1, source_target_pairs={{0,2},{1,3},{2,0},{3,1},{4,6},{5,7},{6,4},{7,5},{8,9},{9,8},{10,11... | collective-permute-start | bytes 3538952 | tf_op jit(solution)/shard_map/ppermute | solution.py:706
  404.7 27.8 %collective-permute-start.43 = (bf16[2,4,144,512]{3,2,1,0:T(8,128)(2,1)}, bf16[2,4,144,512]{3,2,1,0:T(8,128)(2,1)}, u32[]{:S(2)}, u32[]{:S(2)}) collective-permute-start(bf16[2,4,144,512]{3,2,1,0:T(8,128)(2,1)} %get-tuple-element.657), channel_id=1, source_target_pairs={{0,8},{4,12},{8,0},{12,4},{16,24},{20,28},{24,16},{28,20},{1,9},{5... | collective-permute-start | bytes 3538952 | tf_op jit(solution)/shard_map/ppermute | solution.py:709
  432.5 29.4 %collective-permute-start.49 = (f32[4,512]{1,0:T(4,128)S(1)}, f32[4,512]{1,0:T(4,128)S(1)}, u32[]{:S(2)}, u32[]{:S(2)}) collective-permute-start(f32[4,512]{1,0:T(4,128)S(1)} %maximum_select_fusion), channel_id=1, source_target_pairs={{0,8},{4,12},{8,0},{12,4},{16,24},{20,28},{24,16},{28,20},{1,9},{5... | collective-permute-start | bytes 24584 | tf_op jit(solution)/shard_map/ppermute | solution.py:709
  433.5 28.4 %collective-permute-start.46 = (bf16[8,144,512]{2,1,0:T(8,128)(2,1)}, bf16[8,144,512]{2,1,0:T(8,128)(2,1)S(1)}, u32[]{:S(2)}, u32[]{:S(2)}) collective-permute-start(bf16[8,144,512]{2,1,0:T(8,128)(2,1)} %add_convert_fusion.3), channel_id=1, source_target_pairs={{0,1},{1,0},{2,3},{3,2},{4,5},{5,4},{6,7},{7,6},{8,10},{9,11},{10,... | collective-permute-start | bytes 3538952 | tf_op jit(solution)/shard_map/ppermute | solution.py:706
  435.0 26.9 %collective-permute-start.47 = (bf16[8,144,512]{2,1,0:T(8,128)(2,1)}, bf16[8,144,512]{2,1,0:T(8,128)(2,1)S(1)}, u32[]{:S(2)}, u32[]{:S(2)}) collective-permute-start(bf16[8,144,512]{2,1,0:T(8,128)(2,1)} %add_convert_fusion.2), channel_id=1, source_target_pairs={{0,2},{1,3},{2,0},{3,1},{4,6},{5,7},{6,4},{7,5},{8,9},{9,8},{10,11... | collective-permute-start | bytes 3538952 | tf_op jit(solution)/shard_map/ppermute | solution.py:706
  464.1 34.2 %collective-permute-start.54 = (bf16[2,4,144,512]{3,2,1,0:T(8,128)(2,1)}, bf16[2,4,144,512]{3,2,1,0:T(8,128)(2,1)}, u32[]{:S(2)}, u32[]{:S(2)}) collective-permute-start(bf16[2,4,144,512]{3,2,1,0:T(8,128)(2,1)} %pad_maximum_fusion), channel_id=1, source_target_pairs={{0,8},{4,12},{8,0},{12,4},{16,24},{20,28},{24,16},{28,20},{1,9},{5... | collective-permute-start | bytes 3538952 | tf_op jit(solution)/shard_map/ppermute | solution.py:709
  468.8 29.5 %collective-permute-start.50 = (bf16[4,144,512]{2,1,0:T(8,128)(2,1)}, bf16[4,144,512]{2,1,0:T(8,128)(2,1)}, u32[]{:S(2)}, u32[]{:S(2)}) collective-permute-start(bf16[4,144,512]{2,1,0:T(8,128)(2,1)} %get-tuple-element.778), channel_id=1, source_target_pairs={{0,1},{1,0},{2,3},{3,2},{4,5},{5,4},{6,7},{7,6},{8,10},{9,11},{10,... | collective-permute-start | bytes 1769480 | tf_op jit(solution)/shard_map/ppermute | solution.py:706
  470.2 28.1 %collective-permute-start.51 = (bf16[4,144,512]{2,1,0:T(8,128)(2,1)}, bf16[4,144,512]{2,1,0:T(8,128)(2,1)}, u32[]{:S(2)}, u32[]{:S(2)}) collective-permute-start(bf16[4,144,512]{2,1,0:T(8,128)(2,1)} %get-tuple-element.720), channel_id=1, source_target_pairs={{0,2},{1,3},{2,0},{3,1},{4,6},{5,7},{6,4},{7,5},{8,9},{9,8},{10,11... | collective-permute-start | bytes 1769480 | tf_op jit(solution)/shard_map/ppermute | solution.py:706
  508.6 34.2 %collective-permute-start.58 = (bf16[2,4,144,512]{3,2,1,0:T(8,128)(2,1)S(1)}, bf16[2,4,144,512]{3,2,1,0:T(8,128)(2,1)S(1)}, u32[]{:S(2)}, u32[]{:S(2)}) collective-permute-start(bf16[2,4,144,512]{3,2,1,0:T(8,128)(2,1)S(1)} %copy-done.127), channel_id=1, source_target_pairs={{0,8},{4,12},{8,0},{12,4},{16,24},{20,28},{24,16},{28,20},{1,9},{5... | collective-permute-start | bytes 3538952 | tf_op jit(solution)/shard_map/ppermute | solution.py:709
  545.5 29.1 %collective-permute-start.61 = (bf16[2,2,144,512]{3,2,0,1:T(8,128)(2,1)S(1)}, bf16[2,2,144,512]{3,2,0,1:T(8,128)(2,1)S(1)}, u32[]{:S(2)}, u32[]{:S(2)}) collective-permute-start(bf16[2,2,144,512]{3,2,0,1:T(8,128)(2,1)S(1)} %pad_maximum_fusion.11), channel_id=1, source_target_pairs={{0,16},{4,20},{8,24},{12,28},{16,0},{20,4},{24,8},{28,12},{1,17},{... | collective-permute-start | bytes 1769480 | tf_op jit(solution)/shard_map/ppermute | solution.py:709
  (164 other events, 1937.3 us)

commit v4 on v3

--- a/solution.py
+++ b/solution.py
@@ -444,8 +444,7 @@
     depth, lines = x_ref.shape[0] // 4, draw_ref.shape[0] // 8
     group = lines // 4
     chunk = 4 * LANES
-    first = order_ref[1]
-    here, half = (step // 2) ^ order_ref[2], (step % 2) ^ order_ref[0]
+    here = step ^ order_ref[2]
 
     @pl.when(step == 0)
     def _():
@@ -459,15 +458,14 @@
                     emit[:rows, to : to + LANES] = own_emit[:, at : at + LANES]
                     emit[rows:, to : to + LANES] = far_emit[:, at : at + LANES]
 
-    def body(left_ref):
-        left = left_ref[pl.ds(here * (2 * depth), 2 * depth), :]
-        dp = matmul(draw_ref[pl.ds((half * 2 + here) * (2 * lines), 2 * lines), :], emit[...]).astype(BF16)
-        for quarter in range(2):
-            dw = matmul(left, right[:, quarter * chunk : (quarter + 1) * chunk]).astype(BF16)
-
-            def store(out):
+    def body(outs):
+        for half, left_ref in enumerate((x_ref, kept_ref)):
+            left = left_ref[pl.ds(here * (2 * depth), 2 * depth), :]
+            dp = matmul(draw_ref[pl.ds((half * 2 + here) * (2 * lines), 2 * lines), :], emit[...]).astype(BF16)
+            for quarter, out in enumerate(outs):
+                dw = matmul(left, right[:, quarter * chunk : (quarter + 1) * chunk]).astype(BF16)
                 for side in range(2):
-                    to = side ^ first
+                    to = (half ^ order_ref[0]) * 2 + (side ^ order_ref[1])
                     out[to, :depth, :] = dw[side * depth : (side + 1) * depth]
                     for g in range(4):
                         at = side * lines + g * group
@@ -475,12 +473,9 @@
                             at : at + group, quarter * LANES : (quarter + 1) * LANES
                         ]
 
-            pl.when(tile == 0)(lambda: store((first_a, first_b)[quarter]))
-            pl.when((tile == 1) & (step < 2))(lambda: store(second_here.at[quarter]))
-            pl.when((tile == 1) & (step >= 2))(lambda: store(second_there.at[quarter]))
-
-    pl.when(half == 0)(lambda: body(x_ref))
-    pl.when(half == 1)(lambda: body(kept_ref))
+    pl.when(tile == 0)(lambda: body((first_a, first_b)))
+    pl.when((tile == 1) & (step == 0))(lambda: body((second_here.at[0], second_here.at[1])))
+    pl.when((tile == 1) & (step == 1))(lambda: body((second_there.at[0], second_there.at[1])))
 
 
 def block_grads(order, x_turned, kept_turned, draw_turned, own, far, emit_own, emit_far, b):
@@ -491,16 +486,15 @@
     emit = pl.BlockSpec((rows, 4 * LANES), lambda u, n, o: (0, b))
     slab = pl.BlockSpec((rows, 2 * chunk), lambda u, n, o: (0, u))
     left = pl.BlockSpec(memory_space=pltpu.VMEM)
-    first = pl.BlockSpec((2, high, chunk), lambda u, n, o: (jnp.where(u == 0, n, 3), 0, 0))
-    here = pl.BlockSpec((2, 2, high, chunk), lambda u, n, o: (0, jnp.where(u == 0, 0, jnp.minimum(n, 1)), 0, 0))
-    there = pl.BlockSpec((2, 2, high, chunk), lambda u, n, o: (0, jnp.where(u == 0, 0, jnp.maximum(n - 2, 0)), 0, 0))
+    first = pl.BlockSpec((4, high, chunk), lambda u, n, o: (jnp.where(u == 0, n, 1), 0, 0))
+    second = pl.BlockSpec((2, 4, high, chunk), lambda u, n, o: (0, 0, 0, 0))
     return pl.pallas_call(
         block_kernel,
         grid_spec=pltpu.PrefetchScalarGridSpec(
             num_scalar_prefetch=1,
-            grid=(2, 4),
+            grid=(2, 2),
             in_specs=[left, left, left, slab, slab, emit, emit],
-            out_specs=[first, first, here, there],
+            out_specs=[first, first, second, second],
             scratch_shapes=[pltpu.VMEM((2 * rows, 2 * chunk), BF16), pltpu.VMEM((2 * rows, 2 * LANES), BF16)],
         ),
         out_shape=[jax.ShapeDtypeStruct((8, high, chunk), BF16)] * 2

time: 592 us -> 583 us (0.985)
  Pallas kernels: 323 us -> 311 us
    pallas_call x4, Pallas kernels: 68.2 us -> 56.2 us  [block_grads(): pl.pallas_call(block_kernel, grid_spec=pltpu.PrefetchScalarGridSpec(num_s...]
  transfers between devices with their start and end apart: 67 -> 67, of which waited for: 27 -> 29; matrix products, arithmetic and copies ran while one was open for 7% -> 7% of each run, Pallas kernels for 53% -> 52%
where the time goes in v4:
time: 583 us; the launch traced here: 573 us
  Pallas kernels  311 us (53%)
  waiting for transfers between devices  116 us (20%)
  starting transfers between devices  56.8 us (10%)
  local copies, waits for them, and re-layouts  54.9 us (9%)
  other arithmetic  31.5 us (5%)
    pallas_call x1, Pallas kernels, run_backward(): pl.pallas_call(backward_kernel, grid=(steps,), out_shape=tuple([shape(hal...  86.9 us
    pallas_call x1, Pallas kernels, run_forward(): pl.pallas_call(forward_kernel, grid=(steps,), out_shape=tuple((jax.ShapeD...  86 us
    ppermute x40, waiting for transfers between devices, over_rows(): return lax.ppermute(value, 'rows', [(r, r ^ mask) for r in range(8)])  63.7 us
    pallas_call x4, Pallas kernels, block_grads(): pl.pallas_call(block_kernel, grid_spec=pltpu.PrefetchScalarGridSpec(num_s...  56.2 us
    unnamed x259, local copies, waits for them, and re-layouts  37.7 us
    ppermute x23, waiting for transfers between devices, over_chips(): return lax.ppermute(value, ('rows', 'cols'), pairs)  37.2 us
    pallas_call x8, Pallas kernels, own_piece(): pl.pallas_call(own_piece_kernel, grid_spec=pltpu.PrefetchScalarGridSpec(n...  28.7 us
    ppermute x23, starting transfers between devices, over_chips(): return lax.ppermute(value, ('rows', 'cols'), pairs)  25.5 us
  transfers between devices with their start and end apart: 67, of which 29 were waited for; matrix products, arithmetic and copies ran while one was open for 7% of the time, Pallas kernels for 52%

profile of v4, /device:TPU:0, one launch (start us, length us, event | category | flops | bytes accessed | tf_op | source)
XLA Modules:
  0.0 573.5 jit_solution(2160185239053813544)
XLA Ops:
  1.3 5.6 own_piece.8.w0.refs_2_
  19.3 5.8 %copy-done.2 = bf16[2,1024,4,1024]{3,2,1,0:T(4,128)(2,1)S(1)} copy-done((bf16[2,1024,4,1024]{3,2,1,0:T(4,128)(2,1)S(1)}, bf16[2,1024,4,1024]{3,2,1,0:T(4,128)(2,1)}, u32[]{:S(2)}) %copy-start.2) | copy-done | bytes 16777240
  25.1 3.3 own_piece.10.refs_0_.refs_4_.refs_5_
  41.6 5.8 %copy-done.4 = bf16[2,1024,4,1024]{3,2,1,0:T(4,128)(2,1)S(1)} copy-done((bf16[2,1024,4,1024]{3,2,1,0:T(4,128)(2,1)S(1)}, bf16[2,1024,4,1024]{3,2,1,0:T(4,128)(2,1)}, u32[]{:S(2)}) %copy-start.4) | copy-done | bytes 16777240
  47.4 3.3 own_piece.13.refs_1_.refs_5_.refs_6_
  50.7 3.3 own_piece.11.w2.refs_4_
  59.0 5.8 %collective-permute-done.4.w1.refs_3_ = bf16[528,1024]{1,0:T(8,128)(2,1)S(1)} collective-permute-done((bf16[528,1024]{1,0:T(8,128)(2,1)}, bf16[528,1024]{1,0:T(8,128)(2,1)S(1)}, u32[]{:S(2)}, u32[]{:S(2)}) %collective-permute-start.4) | collective-permute-done | bytes 1081376 | tf_op jit(solution)/shard_map/ppermute | solution.py:703
  70.3 3.3 own_piece.14.refs_2_.refs_6_.refs_7_
  73.7 3.3 own_piece.15.refs_3_.refs_7_.refs_8_
  82.6 11.8 %collective-permute-done.8.w1.refs_3_ = bf16[528,1024]{1,0:T(8,128)(2,1)S(1)} collective-permute-done((bf16[528,1024]{1,0:T(8,128)(2,1)S(1)}, bf16[528,1024]{1,0:T(8,128)(2,1)S(1)}, u32[]{:S(2)}, u32[]{:S(2)}) %collective-permute-start.8) | collective-permute-done | bytes 1081376 | tf_op jit(solution)/shard_map/ppermute | solution.py:700
  94.6 4.1 collective-permute-done.12.refs_0_.refs_4_.refs_17_
  110.9 4.8 input_gates.6
  118.0 4.8 input_gates.5
  125.1 4.7 collective-permute-done.16.refs_1_.refs_5_.refs_10_
  157.5 86.0 %forward_chain.1 = (bf16[20,32,16384]{2,1,0:T(8,128)(2,1)}, f32[20,32,4096]{2,1,0:T(8,128)}, bf16[20,32,2048]{2,1,0:T(8,128)(2,1)}, bf16[20,32,2048]{2,1,0:T(8,1...) custom-call(bf16[20,32,4096]{2,1,0:T(8,128)(2,1)} %bitcast.175, ...), custom_call_target="tpu_custom_call" | custom-call | flops 107374182400 | bytes 83886080 | tf_op jit(solution)/shard_map/forward_chain/pallas_call | solution.py:322
  247.1 86.9 %backward_chain.1 = (bf16[20,32,2048]{2,1,0:T(8,128)(2,1)}, bf16[20,32,2048]{2,1,0:T(8,128)(2,1)}, bf16[20,32,2048]{2,1,0:T(8,128)(2,1)}, bf16[20,32,2048]{2,1,0...) custom-call(bf16[20,32,16384]{2,1,0:T(8,128)(2,1)} %get-tuple-elemen, ...), custom_call_target="tpu_custom_call" | custom-call | flops 107374182400 | bytes 83886080 | tf_op jit(solution)/shard_map/backward_chain/pallas_call | solution.py:421
  341.7 14.0 %weight_gradients.4 = (bf16[8,144,512]{2,1,0:T(8,128)(2,1)}, bf16[8,144,512]{2,1,0:T(8,128)(2,1)}, bf16[2,4,144,512]{3,2,1,0:T(8,128)(2,1)}, bf16[2,4,144,512]{3,2,1,0:T(8,128)(2,1)}) custom-call(s32[3]{0:T(128)} %pad_add_fusion.4.order_ref, bf16[512,1280]{1,0:T(8,128)(2,1)} %copy-done.6, bf16[512,1280]{1,0:T(8,128)(2,1)} %copy-done.7, ...), custom_call_target="tpu_custom_call" | custom-call | flops 1 | bytes 1 | tf_op jit(solution)/shard_map/weight_gradients/pallas_call | solution.py:491
  364.4 13.9 %weight_gradients.5 = (bf16[8,144,512]{2,1,0:T(8,128)(2,1)}, bf16[8,144,512]{2,1,0:T(8,128)(2,1)}, bf16[2,4,144,512]{3,2,1,0:T(8,128)(2,1)}, bf16[2,4,144,512]{3,2,1,0:T(8,128)(2,1)}) custom-call(s32[3]{0:T(128)} %pad_add_fusion.4.order_ref, bf16[512,1280]{1,0:T(8,128)(2,1)} %copy-done.6, bf16[512,1280]{1,0:T(8,128)(2,1)} %copy-done.7, ...), custom_call_target="tpu_custom_call" | custom-call | flops 1 | bytes 1 | tf_op jit(solution)/shard_map/weight_gradients/pallas_call | solution.py:491
  378.3 13.7 %weight_gradients.6 = (bf16[8,144,512]{2,1,0:T(8,128)(2,1)}, bf16[8,144,512]{2,1,0:T(8,128)(2,1)}, bf16[2,4,144,512]{3,2,1,0:T(8,128)(2,1)}, bf16[2,4,144,512]{3,2,1,0:T(8,128)(2,1)}) custom-call(s32[3]{0:T(128)} %pad_add_fusion.4.order_ref, bf16[512,1280]{1,0:T(8,128)(2,1)} %copy-done.6, bf16[512,1280]{1,0:T(8,128)(2,1)} %copy-done.7, ...), custom_call_target="tpu_custom_call" | custom-call | flops 1 | bytes 1 | tf_op jit(solution)/shard_map/weight_gradients/pallas_call | solution.py:491
  405.1 14.6 %weight_gradients.7 = (bf16[8,144,512]{2,1,0:T(8,128)(2,1)}, bf16[8,144,512]{2,1,0:T(8,128)(2,1)}, bf16[2,4,144,512]{3,2,1,0:T(8,128)(2,1)}, bf16[2,4,144,512]{3,2,1,0:T(8,128)(2,1)}) custom-call(s32[3]{0:T(128)} %pad_add_fusion.4.order_ref, bf16[512,1280]{1,0:T(8,128)(2,1)} %copy-done.6, bf16[512,1280]{1,0:T(8,128)(2,1)} %copy-done.7, ...), custom_call_target="tpu_custom_call" | custom-call | flops 1 | bytes 1 | tf_op jit(solution)/shard_map/weight_gradients/pallas_call | solution.py:491
  428.0 4.6 input_gradient.4.refs_6_
  432.7 4.5 input_gradient.5.refs_6_
  437.3 4.5 input_gradient.6.refs_6_
  441.9 3.4 input_gradient.7
  465.4 8.7 %collective-permute-done.52 = bf16[4,144,512]{2,1,0:T(8,128)(2,1)} collective-permute-done((bf16[4,144,512]{2,1,0:T(8,128)(2,1)}, bf16[4,144,512]{2,1,0:T(8,128)(2,1)}, u32[]{:S(2)}, u32[]{:S(2)}) %collective-permute-start.52) | collective-permute-done | bytes 589856 | tf_op jit(solution)/shard_map/ppermute | solution.py:700
  475.4 13.6 %collective-permute-done.55 = bf16[336,512]{1,0:T(8,128)(2,1)S(1)} collective-permute-done((bf16[336,512]{1,0:T(8,128)(2,1)}, bf16[336,512]{1,0:T(8,128)(2,1)S(1)}, u32[]{:S(2)}, u32[]{:S(2)}) %collective-permute-start.55) | collective-permute-done | bytes 344096 | tf_op jit(solution)/shard_map/ppermute | solution.py:703
  505.6 13.7 %collective-permute-done.59 = bf16[2,2,144,512]{3,2,0,1:T(8,128)(2,1)S(1)} collective-permute-done((bf16[2,2,144,512]{3,2,0,1:T(8,128)(2,1)S(1)}, bf16[2,2,144,512]{3,2,0,1:T(8,128)(2,1)S(1)}, u32[]{:S(2)}, u32[]{:S(2)}) %collective-permute-start.59) | collective-permute-done | bytes 589856 | tf_op jit(solution)/shard_map/ppermute | solution.py:703
  519.5 14.3 %collective-permute-done.58 = bf16[2,4,144,512]{3,2,1,0:T(8,128)(2,1)S(1)} collective-permute-done((bf16[2,4,144,512]{3,2,1,0:T(8,128)(2,1)S(1)}, bf16[2,4,144,512]{3,2,1,0:T(8,128)(2,1)S(1)}, u32[]{:S(2)}, u32[]{:S(2)}) %collective-permute-start.58) | collective-permute-done | bytes 1179680 | tf_op jit(solution)/shard_map/ppermute | solution.py:703
  538.3 14.4 %collective-permute-done.63 = bf16[320,1152]{1,0:T(8,128)(2,1)S(1)} collective-permute-done((bf16[320,1152]{1,0:T(8,128)(2,1)S(1)}, bf16[320,1152]{1,0:T(8,128)(2,1)S(1)}, u32[]{:S(2)}, u32[]{:S(2)}) %collective-permute-start.63) | collective-permute-done | bytes 737312 | tf_op jit(solution)/shard_map/ppermute | solution.py:814
  553.4 4.3 layer_sum.1
  557.8 7.8 %collective-permute-done.61 = bf16[2,2,144,512]{3,2,0,1:T(8,128)(2,1)S(1)} collective-permute-done((bf16[2,2,144,512]{3,2,0,1:T(8,128)(2,1)S(1)}, bf16[2,2,144,512]{3,2,0,1:T(8,128)(2,1)S(1)}, u32[]{:S(2)}, u32[]{:S(2)}) %collective-permute-start.61) | collective-permute-done | bytes 589856 | tf_op jit(solution)/shard_map/ppermute | solution.py:703
  567.8 5.3 assemble_gradients.1
  (487 shorter events, 172.5 us)
Async XLA Ops:
  7.0 30.7 %collective-permute-start = (bf16[528,1024]{1,0:T(8,128)(2,1)}, bf16[528,1024]{1,0:T(8,128)(2,1)}, u32[]{:S(2)}, u32[]{:S(2)}) collective-permute-start(bf16[528,1024]{1,0:T(8,128)(2,1)} %own_piece.8.w0.refs_2_), channel_id=1, source_target_pairs={{0,1},{1,0},{2,3},{3,2},{4,5},{5,4},{6,7},{7,6},{8,10},{9,11},{10,... | collective-permute-start | bytes 3244040 | tf_op jit(solution)/shard_map/ppermute | solution.py:700
  9.9 27.8 %collective-permute-start.1 = (bf16[528,1024]{1,0:T(8,128)(2,1)}, bf16[528,1024]{1,0:T(8,128)(2,1)}, u32[]{:S(2)}, u32[]{:S(2)}) collective-permute-start(bf16[528,1024]{1,0:T(8,128)(2,1)} %own_piece.8.w0.refs_2_), channel_id=1, source_target_pairs={{0,2},{1,3},{2,0},{3,1},{4,6},{5,7},{6,4},{7,5},{8,9},{9,8},{10,11... | collective-permute-start | bytes 3244040 | tf_op jit(solution)/shard_map/ppermute | solution.py:700
  37.7 29.7 %collective-permute-start.7 = (bf16[640,1024]{1,0:T(8,128)(2,1)S(1)}, bf16[640,1024]{1,0:T(8,128)(2,1)S(1)}, u32[]{:S(2)}, u32[]{:S(2)}) collective-permute-start(bf16[640,1024]{1,0:T(8,128)(2,1)S(1)} %own_piece.10.refs_0_.refs_4_.refs_5_), channel_id=1, source_target_pairs={{0,1},{1,0},{2,3},{3,2},{4,5},{5,4},{6,7},{7,6},{8,10},{9,11},{10,... | collective-permute-start | bytes 3932168 | tf_op jit(solution)/shard_map/ppermute | solution.py:700
  38.3 26.5 %collective-permute-start.4 = (bf16[528,1024]{1,0:T(8,128)(2,1)}, bf16[528,1024]{1,0:T(8,128)(2,1)S(1)}, u32[]{:S(2)}, u32[]{:S(2)}) collective-permute-start(bf16[528,1024]{1,0:T(8,128)(2,1)} %collective-permute-done.w0.refs_2_), channel_id=1, source_target_pairs={{0,8},{4,12},{8,0},{12,4},{16,24},{20,28},{24,16},{28,20},{1,9},{5... | collective-permute-start | bytes 3244040 | tf_op jit(solution)/shard_map/ppermute | solution.py:703
  40.1 26.3 %collective-permute-start.6 = (bf16[528,1024]{1,0:T(8,128)(2,1)}, bf16[528,1024]{1,0:T(8,128)(2,1)S(1)}, u32[]{:S(2)}, u32[]{:S(2)}) collective-permute-start(bf16[528,1024]{1,0:T(8,128)(2,1)} %collective-permute-done.w0.refs_2_), channel_id=1, source_target_pairs={{0,2},{1,3},{2,0},{3,1},{4,6},{5,7},{6,4},{7,5},{8,9},{9,8},{10,11... | collective-permute-start | bytes 3244040 | tf_op jit(solution)/shard_map/ppermute | solution.py:700
  67.5 27.1 %collective-permute-start.11 = (bf16[640,1024]{1,0:T(8,128)(2,1)S(1)}, bf16[640,1024]{1,0:T(8,128)(2,1)S(1)}, u32[]{:S(2)}, u32[]{:S(2)}) collective-permute-start(bf16[640,1024]{1,0:T(8,128)(2,1)S(1)} %collective-permute-done.7.refs_0_.refs_4_.refs_9_), channel_id=1, source_target_pairs={{0,4},{4,0},{8,12},{12,8},{16,20},{20,16},{24,28},{28,24},{1,5},{5... | collective-permute-start | bytes 3932168 | tf_op jit(solution)/shard_map/ppermute | solution.py:703
  67.5 31.2 %collective-permute-start.12 = (bf16[640,1024]{1,0:T(8,128)(2,1)S(1)}, bf16[640,1024]{1,0:T(8,128)(2,1)S(1)}, u32[]{:S(2)}, u32[]{:S(2)}) collective-permute-start(bf16[640,1024]{1,0:T(8,128)(2,1)S(1)} %collective-permute-done.7.refs_0_.refs_4_.refs_9_), channel_id=1, source_target_pairs={{0,2},{1,3},{2,0},{3,1},{4,6},{5,7},{6,4},{7,5},{8,9},{9,8},{10,11... | collective-permute-start | bytes 3932168 | tf_op jit(solution)/shard_map/ppermute | solution.py:700
  98.7 31.2 %collective-permute-start.16 = (bf16[640,1024]{1,0:T(8,128)(2,1)S(1)}, bf16[640,1024]{1,0:T(8,128)(2,1)S(1)}, u32[]{:S(2)}, u32[]{:S(2)}) collective-permute-start(bf16[640,1024]{1,0:T(8,128)(2,1)S(1)} %own_piece.13.refs_1_.refs_5_.refs_6_), channel_id=1, source_target_pairs={{0,1},{1,0},{2,3},{3,2},{4,5},{5,4},{6,7},{7,6},{8,10},{9,11},{10,... | collective-permute-start | bytes 3932168 | tf_op jit(solution)/shard_map/ppermute | solution.py:700
  99.2 30.9 %collective-permute-start.17 = (bf16[640,1024]{1,0:T(8,128)(2,1)S(1)}, bf16[640,1024]{1,0:T(8,128)(2,1)S(1)}, u32[]{:S(2)}, u32[]{:S(2)}) collective-permute-start(bf16[640,1024]{1,0:T(8,128)(2,1)S(1)} %own_piece.10.refs_0_.refs_4_.refs_5_), channel_id=1, source_target_pairs={{0,2},{1,3},{2,0},{3,1},{4,6},{5,7},{6,4},{7,5},{8,9},{9,8},{10,11... | collective-permute-start | bytes 3932168 | tf_op jit(solution)/shard_map/ppermute | solution.py:700
  99.7 30.6 %collective-permute-start.18 = (bf16[640,1024]{1,0:T(8,128)(2,1)S(1)}, bf16[640,1024]{1,0:T(8,128)(2,1)S(1)}, u32[]{:S(2)}, u32[]{:S(2)}) collective-permute-start(bf16[640,1024]{1,0:T(8,128)(2,1)S(1)} %collective-permute-done.7.refs_0_.refs_4_.refs_9_), channel_id=1, source_target_pairs={{0,8},{4,12},{8,0},{12,4},{16,24},{20,28},{24,16},{28,20},{1,9},{5... | collective-permute-start | bytes 3932168 | tf_op jit(solution)/shard_map/ppermute | solution.py:703
  156.1 87.4 %collective-permute-start.27 = (bf16[20,16,512]{2,1,0:T(8,128)(2,1)S(1)}, bf16[20,16,512]{2,1,0:T(8,128)(2,1)S(1)}, u32[]{:S(2)}, u32[]{:S(2)}) collective-permute-start(bf16[20,16,512]{2,1,0:T(8,128)(2,1)S(1)} %get-tuple-element.558), channel_id=1, source_target_pairs={{0,16},{4,20},{8,24},{12,28},{16,0},{20,4},{24,8},{28,12},{1,17},{... | collective-permute-start | bytes 983048 | tf_op jit(solution)/shard_map/ppermute | solution.py:703
  244.8 89.2 %collective-permute-start.30 = (bf16[640,2048]{1,0:T(8,128)(2,1)}, bf16[640,2048]{1,0:T(8,128)(2,1)S(1)}, u32[]{:S(2)}, u32[]{:S(2)}) collective-permute-start(bf16[640,2048]{1,0:T(8,128)(2,1)} %bitcast.205), channel_id=1, source_target_pairs={{0,4},{4,0},{8,12},{12,8},{16,20},{20,16},{24,28},{28,24},{1,5},{5... | collective-permute-start | bytes 7864328 | tf_op jit(solution)/shard_map/ppermute | solution.py:703
  245.1 88.9 %collective-permute-start.28 = (bf16[20,16,512]{2,1,0:T(8,128)(2,1)S(1)}, bf16[20,16,512]{2,1,0:T(8,128)(2,1)S(1)}, u32[]{:S(2)}, u32[]{:S(2)}) collective-permute-start(bf16[20,16,512]{2,1,0:T(8,128)(2,1)S(1)} %get-tuple-element.807), channel_id=1, source_target_pairs={{0,16},{4,20},{8,24},{12,28},{16,0},{20,4},{24,8},{28,12},{1,17},{... | collective-permute-start | bytes 983048 | tf_op jit(solution)/shard_map/ppermute | solution.py:703
  246.8 87.2 %collective-permute-start.29 = (bf16[640,512]{1,0:T(8,128)(2,1)S(1)}, bf16[640,512]{1,0:T(8,128)(2,1)S(1)}, u32[]{:S(2)}, u32[]{:S(2)}) collective-permute-start(bf16[640,512]{1,0:T(8,128)(2,1)S(1)} %bitcast.186), channel_id=1, source_target_pairs={{0,4},{4,0},{8,12},{12,8},{16,20},{20,16},{24,28},{28,24},{1,5},{5... | collective-permute-start | bytes 1966088 | tf_op jit(solution)/shard_map/ppermute | solution.py:703
  356.1 35.9 %collective-permute-start.36 = (bf16[8,144,512]{2,1,0:T(8,128)(2,1)}, bf16[8,144,512]{2,1,0:T(8,128)(2,1)}, u32[]{:S(2)}, u32[]{:S(2)}) collective-permute-start(bf16[8,144,512]{2,1,0:T(8,128)(2,1)} %get-tuple-element.631), channel_id=1, source_target_pairs={{0,1},{1,0},{2,3},{3,2},{4,5},{5,4},{6,7},{7,6},{8,10},{9,11},{10,... | collective-permute-start | bytes 3538952 | tf_op jit(solution)/shard_map/ppermute | solution.py:700
  357.6 34.4 %collective-permute-start.37 = (bf16[8,144,512]{2,1,0:T(8,128)(2,1)}, bf16[8,144,512]{2,1,0:T(8,128)(2,1)}, u32[]{:S(2)}, u32[]{:S(2)}) collective-permute-start(bf16[8,144,512]{2,1,0:T(8,128)(2,1)} %get-tuple-element.632), channel_id=1, source_target_pairs={{0,2},{1,3},{2,0},{3,1},{4,6},{5,7},{6,4},{7,5},{8,9},{9,8},{10,11... | collective-permute-start | bytes 3538952 | tf_op jit(solution)/shard_map/ppermute | solution.py:700
  359.1 32.9 %collective-permute-start.38 = (bf16[2,4,144,512]{3,2,1,0:T(8,128)(2,1)}, bf16[2,4,144,512]{3,2,1,0:T(8,128)(2,1)}, u32[]{:S(2)}, u32[]{:S(2)}) collective-permute-start(bf16[2,4,144,512]{3,2,1,0:T(8,128)(2,1)} %get-tuple-element.633), channel_id=1, source_target_pairs={{0,8},{4,12},{8,0},{12,4},{16,24},{20,28},{24,16},{28,20},{1,9},{5... | collective-permute-start | bytes 3538952 | tf_op jit(solution)/shard_map/ppermute | solution.py:703
  360.8 31.2 %collective-permute-start.39 = (f32[4,512]{1,0:T(4,128)S(1)}, f32[4,512]{1,0:T(4,128)S(1)}, u32[]{:S(2)}, u32[]{:S(2)}) collective-permute-start(f32[4,512]{1,0:T(4,128)S(1)} %get-tuple-element.825), channel_id=1, source_target_pairs={{0,1},{1,0},{2,3},{3,2},{4,5},{5,4},{6,7},{7,6},{8,10},{9,11},{10,... | collective-permute-start | bytes 24584 | tf_op jit(solution)/shard_map/ppermute | solution.py:700
  361.4 30.6 %collective-permute-start.40 = (f32[4,512]{1,0:T(4,128)S(1)}, f32[4,512]{1,0:T(4,128)S(1)}, u32[]{:S(2)}, u32[]{:S(2)}) collective-permute-start(f32[4,512]{1,0:T(4,128)S(1)} %get-tuple-element.824), channel_id=1, source_target_pairs={{0,2},{1,3},{2,0},{3,1},{4,6},{5,7},{6,4},{7,5},{8,9},{9,8},{10,11... | collective-permute-start | bytes 24584 | tf_op jit(solution)/shard_map/ppermute | solution.py:700
  392.1 27.6 %collective-permute-start.45 = (f32[4,512]{1,0:T(4,128)S(1)}, f32[4,512]{1,0:T(4,128)S(1)}, u32[]{:S(2)}, u32[]{:S(2)}) collective-permute-start(f32[4,512]{1,0:T(4,128)S(1)} %get-tuple-element.823), channel_id=1, source_target_pairs={{0,3},{1,2},{2,1},{3,0},{4,7},{5,6},{6,5},{7,4},{8,11},{9,10},{10,... | collective-permute-start | bytes 24584 | tf_op jit(solution)/shard_map/ppermute | solution.py:814
  394.2 28.1 %collective-permute-start.41 = (bf16[8,144,512]{2,1,0:T(8,128)(2,1)}, bf16[8,144,512]{2,1,0:T(8,128)(2,1)}, u32[]{:S(2)}, u32[]{:S(2)}) collective-permute-start(bf16[8,144,512]{2,1,0:T(8,128)(2,1)} %get-tuple-element.655), channel_id=1, source_target_pairs={{0,1},{1,0},{2,3},{3,2},{4,5},{5,4},{6,7},{7,6},{8,10},{9,11},{10,... | collective-permute-start | bytes 3538952 | tf_op jit(solution)/shard_map/ppermute | solution.py:700
  394.7 27.8 %collective-permute-start.42 = (bf16[8,144,512]{2,1,0:T(8,128)(2,1)}, bf16[8,144,512]{2,1,0:T(8,128)(2,1)}, u32[]{:S(2)}, u32[]{:S(2)}) collective-permute-start(bf16[8,144,512]{2,1,0:T(8,128)(2,1)} %get-tuple-element.656), channel_id=1, source_target_pairs={{0,2},{1,3},{2,0},{3,1},{4,6},{5,7},{6,4},{7,5},{8,9},{9,8},{10,11... | collective-permute-start | bytes 3538952 | tf_op jit(solution)/shard_map/ppermute | solution.py:700
  395.7 27.8 %collective-permute-start.43 = (bf16[2,4,144,512]{3,2,1,0:T(8,128)(2,1)}, bf16[2,4,144,512]{3,2,1,0:T(8,128)(2,1)}, u32[]{:S(2)}, u32[]{:S(2)}) collective-permute-start(bf16[2,4,144,512]{3,2,1,0:T(8,128)(2,1)} %get-tuple-element.657), channel_id=1, source_target_pairs={{0,8},{4,12},{8,0},{12,4},{16,24},{20,28},{24,16},{28,20},{1,9},{5... | collective-permute-start | bytes 3538952 | tf_op jit(solution)/shard_map/ppermute | solution.py:703
  423.5 29.4 %collective-permute-start.49 = (f32[4,512]{1,0:T(4,128)S(1)}, f32[4,512]{1,0:T(4,128)S(1)}, u32[]{:S(2)}, u32[]{:S(2)}) collective-permute-start(f32[4,512]{1,0:T(4,128)S(1)} %maximum_select_fusion), channel_id=1, source_target_pairs={{0,8},{4,12},{8,0},{12,4},{16,24},{20,28},{24,16},{28,20},{1,9},{5... | collective-permute-start | bytes 24584 | tf_op jit(solution)/shard_map/ppermute | solution.py:703
  424.5 28.4 %collective-permute-start.46 = (bf16[8,144,512]{2,1,0:T(8,128)(2,1)}, bf16[8,144,512]{2,1,0:T(8,128)(2,1)S(1)}, u32[]{:S(2)}, u32[]{:S(2)}) collective-permute-start(bf16[8,144,512]{2,1,0:T(8,128)(2,1)} %add_convert_fusion.3), channel_id=1, source_target_pairs={{0,1},{1,0},{2,3},{3,2},{4,5},{5,4},{6,7},{7,6},{8,10},{9,11},{10,... | collective-permute-start | bytes 3538952 | tf_op jit(solution)/shard_map/ppermute | solution.py:700
  426.0 26.9 %collective-permute-start.47 = (bf16[8,144,512]{2,1,0:T(8,128)(2,1)}, bf16[8,144,512]{2,1,0:T(8,128)(2,1)S(1)}, u32[]{:S(2)}, u32[]{:S(2)}) collective-permute-start(bf16[8,144,512]{2,1,0:T(8,128)(2,1)} %add_convert_fusion.2), channel_id=1, source_target_pairs={{0,2},{1,3},{2,0},{3,1},{4,6},{5,7},{6,4},{7,5},{8,9},{9,8},{10,11... | collective-permute-start | bytes 3538952 | tf_op jit(solution)/shard_map/ppermute | solution.py:700
  455.0 33.9 %collective-permute-start.54 = (bf16[2,4,144,512]{3,2,1,0:T(8,128)(2,1)}, bf16[2,4,144,512]{3,2,1,0:T(8,128)(2,1)}, u32[]{:S(2)}, u32[]{:S(2)}) collective-permute-start(bf16[2,4,144,512]{3,2,1,0:T(8,128)(2,1)} %pad_maximum_fusion), channel_id=1, source_target_pairs={{0,8},{4,12},{8,0},{12,4},{16,24},{20,28},{24,16},{28,20},{1,9},{5... | collective-permute-start | bytes 3538952 | tf_op jit(solution)/shard_map/ppermute | solution.py:703
  459.8 29.1 %collective-permute-start.50 = (bf16[4,144,512]{2,1,0:T(8,128)(2,1)}, bf16[4,144,512]{2,1,0:T(8,128)(2,1)}, u32[]{:S(2)}, u32[]{:S(2)}) collective-permute-start(bf16[4,144,512]{2,1,0:T(8,128)(2,1)} %get-tuple-element.778), channel_id=1, source_target_pairs={{0,1},{1,0},{2,3},{3,2},{4,5},{5,4},{6,7},{7,6},{8,10},{9,11},{10,... | collective-permute-start | bytes 1769480 | tf_op jit(solution)/shard_map/ppermute | solution.py:700
  461.2 27.7 %collective-permute-start.51 = (bf16[4,144,512]{2,1,0:T(8,128)(2,1)}, bf16[4,144,512]{2,1,0:T(8,128)(2,1)}, u32[]{:S(2)}, u32[]{:S(2)}) collective-permute-start(bf16[4,144,512]{2,1,0:T(8,128)(2,1)} %get-tuple-element.720), channel_id=1, source_target_pairs={{0,2},{1,3},{2,0},{3,1},{4,6},{5,7},{6,4},{7,5},{8,9},{9,8},{10,11... | collective-permute-start | bytes 1769480 | tf_op jit(solution)/shard_map/ppermute | solution.py:700
  493.2 26.3 %collective-permute-start.60 = (bf16[320,1152]{1,0:T(8,128)(2,1)S(1)}, bf16[320,1152]{1,0:T(8,128)(2,1)S(1)}, u32[]{:S(2)}, u32[]{:S(2)}) collective-permute-start(bf16[320,1152]{1,0:T(8,128)(2,1)S(1)} %get-tuple-element.800), channel_id=1, source_target_pairs={{0,3},{1,2},{2,1},{3,0},{4,7},{5,6},{6,5},{7,4},{8,11},{9,10},{10,... | collective-permute-start | bytes 2211848 | tf_op jit(solution)/shard_map/ppermute | solution.py:814
  499.6 34.2 %collective-permute-start.58 = (bf16[2,4,144,512]{3,2,1,0:T(8,128)(2,1)S(1)}, bf16[2,4,144,512]{3,2,1,0:T(8,128)(2,1)S(1)}, u32[]{:S(2)}, u32[]{:S(2)}) collective-permute-start(bf16[2,4,144,512]{3,2,1,0:T(8,128)(2,1)S(1)} %copy-done.127), channel_id=1, source_target_pairs={{0,8},{4,12},{8,0},{12,4},{16,24},{20,28},{24,16},{28,20},{1,9},{5... | collective-permute-start | bytes 3538952 | tf_op jit(solution)/shard_map/ppermute | solution.py:703
  537.2 28.3 %collective-permute-start.61 = (bf16[2,2,144,512]{3,2,0,1:T(8,128)(2,1)S(1)}, bf16[2,2,144,512]{3,2,0,1:T(8,128)(2,1)S(1)}, u32[]{:S(2)}, u32[]{:S(2)}) collective-permute-start(bf16[2,2,144,512]{3,2,0,1:T(8,128)(2,1)S(1)} %pad_maximum_fusion.11), channel_id=1, source_target_pairs={{0,16},{4,20},{8,24},{12,28},{16,0},{20,4},{24,8},{28,12},{1,17},{... | collective-permute-start | bytes 1769480 | tf_op jit(solution)/shard_map/ppermute | solution.py:703
  (164 other events, 1926.0 us)

commit v5 on v4

--- a/solution.py
+++ b/solution.py
@@ -281,7 +281,7 @@
     kept = (h_scr[...] * keep).astype(BF16)
     kept_out[0] = kept
     raw = jnp.zeros((rows, hidden), F32)
-    for b in range(BLOCKS):
+    def products(b):
         parts, proj = [], []
         for s in range(PARTS):
             w_ref = w_refs[b * PARTS + s]
@@ -290,6 +290,13 @@
             pre_out[0, :, at : at + width] = pre.astype(BF16)
             parts.append(pre)
             proj += [w_ref[hidden:, :hidden], w_ref[hidden:, hidden:]]
+        return parts, proj
+
+    following = products(0)
+    for b in range(BLOCKS):
+        parts, proj = following
+        if b + 1 < BLOCKS:
+            following = products(b + 1)
         gates = [
             jnp.concatenate(
                 [part[:, (u * 4 + q) * LANES : (u * 4 + q + 1) * LANES] for part in parts for u in range(tiles)], axis=1
@@ -360,9 +367,13 @@
     draw = ((grad_ref[0].astype(F32) + dk_scr[...]) * (1.0 - tangent * tangent)).astype(BF16)
     draw_out[0] = draw
     dk = jnp.zeros((rows, hidden), F32)
+    emitted = lambda b: matmul(draw, jnp.concatenate([pt_refs[b * PARTS + s][...] for s in range(PARTS)], axis=1))
+    following = emitted(0)
     for b in range(BLOCKS):
         at = b * cells
-        demit = matmul(draw, jnp.concatenate([pt_refs[b * PARTS + s][...] for s in range(PARTS)], axis=1))
+        demit = following
+        if b + 1 < BLOCKS:
+            following = emitted(b + 1)
         gates = [
             jnp.concatenate(
                 [

time: 583 us -> 580 us (level)
  no operation moved by 1% of the time
where the time goes in v5:
time: 580 us; the launch traced here: 571 us
  Pallas kernels  309 us (53%)
  waiting for transfers between devices  116 us (20%)
  starting transfers between devices  56.8 us (10%)
  local copies, waits for them, and re-layouts  54.9 us (9%)
  other arithmetic  31.5 us (5%)
    pallas_call x1, Pallas kernels, run_backward(): pl.pallas_call(backward_kernel, grid=(steps,), out_shape=tuple([shape(hal...  85.3 us
    pallas_call x1, Pallas kernels, run_forward(): pl.pallas_call(forward_kernel, grid=(steps,), out_shape=tuple((jax.ShapeD...  85.1 us
    ppermute x40, waiting for transfers between devices, over_rows(): return lax.ppermute(value, 'rows', [(r, r ^ mask) for r in range(8)])  63.6 us
    pallas_call x4, Pallas kernels, block_grads(): pl.pallas_call(block_kernel, grid_spec=pltpu.PrefetchScalarGridSpec(num_s...  56.2 us
    unnamed x259, local copies, waits for them, and re-layouts  37.7 us
    ppermute x23, waiting for transfers between devices, over_chips(): return lax.ppermute(value, ('rows', 'cols'), pairs)  37.3 us
    pallas_call x8, Pallas kernels, own_piece(): pl.pallas_call(own_piece_kernel, grid_spec=pltpu.PrefetchScalarGridSpec(n...  28.7 us
    ppermute x23, starting transfers between devices, over_chips(): return lax.ppermute(value, ('rows', 'cols'), pairs)  25.5 us
  transfers between devices with their start and end apart: 67, of which 29 were waited for; matrix products, arithmetic and copies ran while one was open for 7% of the time, Pallas kernels for 52%

profile of v5, /device:TPU:0, one launch (start us, length us, event | category | flops | bytes accessed | tf_op | source)
XLA Modules:
  0.0 571.0 jit_solution(8005124240201523572)
XLA Ops:
  1.3 5.6 own_piece.8.w0.refs_2_
  19.3 5.8 %copy-done.2 = bf16[2,1024,4,1024]{3,2,1,0:T(4,128)(2,1)S(1)} copy-done((bf16[2,1024,4,1024]{3,2,1,0:T(4,128)(2,1)S(1)}, bf16[2,1024,4,1024]{3,2,1,0:T(4,128)(2,1)}, u32[]{:S(2)}) %copy-start.2) | copy-done | bytes 16777240
  25.1 3.3 own_piece.10.refs_0_.refs_4_.refs_5_
  41.6 5.8 %copy-done.4 = bf16[2,1024,4,1024]{3,2,1,0:T(4,128)(2,1)S(1)} copy-done((bf16[2,1024,4,1024]{3,2,1,0:T(4,128)(2,1)S(1)}, bf16[2,1024,4,1024]{3,2,1,0:T(4,128)(2,1)}, u32[]{:S(2)}) %copy-start.4) | copy-done | bytes 16777240
  47.4 3.3 own_piece.13.refs_1_.refs_5_.refs_6_
  50.7 3.3 own_piece.11.w2.refs_4_
  59.0 5.8 %collective-permute-done.4.w1.refs_3_ = bf16[528,1024]{1,0:T(8,128)(2,1)S(1)} collective-permute-done((bf16[528,1024]{1,0:T(8,128)(2,1)}, bf16[528,1024]{1,0:T(8,128)(2,1)S(1)}, u32[]{:S(2)}, u32[]{:S(2)}) %collective-permute-start.4) | collective-permute-done | bytes 1081376 | tf_op jit(solution)/shard_map/ppermute | solution.py:714
  70.3 3.3 own_piece.14.refs_2_.refs_6_.refs_7_
  73.7 3.3 own_piece.15.refs_3_.refs_7_.refs_8_
  82.6 11.8 %collective-permute-done.8.w1.refs_3_ = bf16[528,1024]{1,0:T(8,128)(2,1)S(1)} collective-permute-done((bf16[528,1024]{1,0:T(8,128)(2,1)S(1)}, bf16[528,1024]{1,0:T(8,128)(2,1)S(1)}, u32[]{:S(2)}, u32[]{:S(2)}) %collective-permute-start.8) | collective-permute-done | bytes 1081376 | tf_op jit(solution)/shard_map/ppermute | solution.py:711
  94.6 4.1 collective-permute-done.12.refs_0_.refs_4_.refs_17_
  110.9 4.8 input_gates.6
  118.0 4.8 input_gates.5
  125.1 4.7 collective-permute-done.16.refs_1_.refs_5_.refs_10_
  157.5 85.1 %forward_chain.1 = (bf16[20,32,16384]{2,1,0:T(8,128)(2,1)}, f32[20,32,4096]{2,1,0:T(8,128)}, bf16[20,32,2048]{2,1,0:T(8,128)(2,1)}, bf16[20,32,2048]{2,1,0:T(8,1...) custom-call(bf16[20,32,4096]{2,1,0:T(8,128)(2,1)} %bitcast.175, ...), custom_call_target="tpu_custom_call" | custom-call | flops 107374182400 | bytes 83886080 | tf_op jit(solution)/shard_map/forward_chain/pallas_call | solution.py:329
  246.2 85.3 %backward_chain.1 = (bf16[20,32,2048]{2,1,0:T(8,128)(2,1)}, bf16[20,32,2048]{2,1,0:T(8,128)(2,1)}, bf16[20,32,2048]{2,1,0:T(8,128)(2,1)}, bf16[20,32,2048]{2,1,0...) custom-call(bf16[20,32,16384]{2,1,0:T(8,128)(2,1)} %get-tuple-elemen, ...), custom_call_target="tpu_custom_call" | custom-call | flops 107374182400 | bytes 83886080 | tf_op jit(solution)/shard_map/backward_chain/pallas_call | solution.py:432
  339.3 14.0 %weight_gradients.4 = (bf16[8,144,512]{2,1,0:T(8,128)(2,1)}, bf16[8,144,512]{2,1,0:T(8,128)(2,1)}, bf16[2,4,144,512]{3,2,1,0:T(8,128)(2,1)}, bf16[2,4,144,512]{3,2,1,0:T(8,128)(2,1)}) custom-call(s32[3]{0:T(128)} %pad_add_fusion.4.order_ref, bf16[512,1280]{1,0:T(8,128)(2,1)} %copy-done.6, bf16[512,1280]{1,0:T(8,128)(2,1)} %copy-done.7, ...), custom_call_target="tpu_custom_call" | custom-call | flops 1 | bytes 1 | tf_op jit(solution)/shard_map/weight_gradients/pallas_call | solution.py:502
  361.9 13.9 %weight_gradients.5 = (bf16[8,144,512]{2,1,0:T(8,128)(2,1)}, bf16[8,144,512]{2,1,0:T(8,128)(2,1)}, bf16[2,4,144,512]{3,2,1,0:T(8,128)(2,1)}, bf16[2,4,144,512]{3,2,1,0:T(8,128)(2,1)}) custom-call(s32[3]{0:T(128)} %pad_add_fusion.4.order_ref, bf16[512,1280]{1,0:T(8,128)(2,1)} %copy-done.6, bf16[512,1280]{1,0:T(8,128)(2,1)} %copy-done.7, ...), custom_call_target="tpu_custom_call" | custom-call | flops 1 | bytes 1 | tf_op jit(solution)/shard_map/weight_gradients/pallas_call | solution.py:502
  375.8 13.7 %weight_gradients.6 = (bf16[8,144,512]{2,1,0:T(8,128)(2,1)}, bf16[8,144,512]{2,1,0:T(8,128)(2,1)}, bf16[2,4,144,512]{3,2,1,0:T(8,128)(2,1)}, bf16[2,4,144,512]{3,2,1,0:T(8,128)(2,1)}) custom-call(s32[3]{0:T(128)} %pad_add_fusion.4.order_ref, bf16[512,1280]{1,0:T(8,128)(2,1)} %copy-done.6, bf16[512,1280]{1,0:T(8,128)(2,1)} %copy-done.7, ...), custom_call_target="tpu_custom_call" | custom-call | flops 1 | bytes 1 | tf_op jit(solution)/shard_map/weight_gradients/pallas_call | solution.py:502
  402.7 14.6 %weight_gradients.7 = (bf16[8,144,512]{2,1,0:T(8,128)(2,1)}, bf16[8,144,512]{2,1,0:T(8,128)(2,1)}, bf16[2,4,144,512]{3,2,1,0:T(8,128)(2,1)}, bf16[2,4,144,512]{3,2,1,0:T(8,128)(2,1)}) custom-call(s32[3]{0:T(128)} %pad_add_fusion.4.order_ref, bf16[512,1280]{1,0:T(8,128)(2,1)} %copy-done.6, bf16[512,1280]{1,0:T(8,128)(2,1)} %copy-done.7, ...), custom_call_target="tpu_custom_call" | custom-call | flops 1 | bytes 1 | tf_op jit(solution)/shard_map/weight_gradients/pallas_call | solution.py:502
  425.6 4.6 input_gradient.4.refs_6_
  430.3 4.5 input_gradient.5.refs_6_
  434.9 4.5 input_gradient.6.refs_6_
  439.5 3.4 input_gradient.7
  462.9 8.7 %collective-permute-done.52 = bf16[4,144,512]{2,1,0:T(8,128)(2,1)} collective-permute-done((bf16[4,144,512]{2,1,0:T(8,128)(2,1)}, bf16[4,144,512]{2,1,0:T(8,128)(2,1)}, u32[]{:S(2)}, u32[]{:S(2)}) %collective-permute-start.52) | collective-permute-done | bytes 589856 | tf_op jit(solution)/shard_map/ppermute | solution.py:711
  472.9 13.6 %collective-permute-done.55 = bf16[336,512]{1,0:T(8,128)(2,1)S(1)} collective-permute-done((bf16[336,512]{1,0:T(8,128)(2,1)}, bf16[336,512]{1,0:T(8,128)(2,1)S(1)}, u32[]{:S(2)}, u32[]{:S(2)}) %collective-permute-start.55) | collective-permute-done | bytes 344096 | tf_op jit(solution)/shard_map/ppermute | solution.py:714
  503.1 13.7 %collective-permute-done.59 = bf16[2,2,144,512]{3,2,0,1:T(8,128)(2,1)S(1)} collective-permute-done((bf16[2,2,144,512]{3,2,0,1:T(8,128)(2,1)S(1)}, bf16[2,2,144,512]{3,2,0,1:T(8,128)(2,1)S(1)}, u32[]{:S(2)}, u32[]{:S(2)}) %collective-permute-start.59) | collective-permute-done | bytes 589856 | tf_op jit(solution)/shard_map/ppermute | solution.py:714
  517.0 14.3 %collective-permute-done.58 = bf16[2,4,144,512]{3,2,1,0:T(8,128)(2,1)S(1)} collective-permute-done((bf16[2,4,144,512]{3,2,1,0:T(8,128)(2,1)S(1)}, bf16[2,4,144,512]{3,2,1,0:T(8,128)(2,1)S(1)}, u32[]{:S(2)}, u32[]{:S(2)}) %collective-permute-start.58) | collective-permute-done | bytes 1179680 | tf_op jit(solution)/shard_map/ppermute | solution.py:714
  535.8 14.4 %collective-permute-done.63 = bf16[320,1152]{1,0:T(8,128)(2,1)S(1)} collective-permute-done((bf16[320,1152]{1,0:T(8,128)(2,1)S(1)}, bf16[320,1152]{1,0:T(8,128)(2,1)S(1)}, u32[]{:S(2)}, u32[]{:S(2)}) %collective-permute-start.63) | collective-permute-done | bytes 737312 | tf_op jit(solution)/shard_map/ppermute | solution.py:825
  550.9 4.3 layer_sum.1
  555.3 7.8 %collective-permute-done.61 = bf16[2,2,144,512]{3,2,0,1:T(8,128)(2,1)S(1)} collective-permute-done((bf16[2,2,144,512]{3,2,0,1:T(8,128)(2,1)S(1)}, bf16[2,2,144,512]{3,2,0,1:T(8,128)(2,1)S(1)}, u32[]{:S(2)}, u32[]{:S(2)}) %collective-permute-start.61) | collective-permute-done | bytes 589856 | tf_op jit(solution)/shard_map/ppermute | solution.py:714
  565.3 5.3 assemble_gradients.1
  (487 shorter events, 172.6 us)
Async XLA Ops:
  7.0 30.7 %collective-permute-start = (bf16[528,1024]{1,0:T(8,128)(2,1)}, bf16[528,1024]{1,0:T(8,128)(2,1)}, u32[]{:S(2)}, u32[]{:S(2)}) collective-permute-start(bf16[528,1024]{1,0:T(8,128)(2,1)} %own_piece.8.w0.refs_2_), channel_id=1, source_target_pairs={{0,1},{1,0},{2,3},{3,2},{4,5},{5,4},{6,7},{7,6},{8,10},{9,11},{10,... | collective-permute-start | bytes 3244040 | tf_op jit(solution)/shard_map/ppermute | solution.py:711
  9.9 27.8 %collective-permute-start.1 = (bf16[528,1024]{1,0:T(8,128)(2,1)}, bf16[528,1024]{1,0:T(8,128)(2,1)}, u32[]{:S(2)}, u32[]{:S(2)}) collective-permute-start(bf16[528,1024]{1,0:T(8,128)(2,1)} %own_piece.8.w0.refs_2_), channel_id=1, source_target_pairs={{0,2},{1,3},{2,0},{3,1},{4,6},{5,7},{6,4},{7,5},{8,9},{9,8},{10,11... | collective-permute-start | bytes 3244040 | tf_op jit(solution)/shard_map/ppermute | solution.py:711
  37.7 29.7 %collective-permute-start.7 = (bf16[640,1024]{1,0:T(8,128)(2,1)S(1)}, bf16[640,1024]{1,0:T(8,128)(2,1)S(1)}, u32[]{:S(2)}, u32[]{:S(2)}) collective-permute-start(bf16[640,1024]{1,0:T(8,128)(2,1)S(1)} %own_piece.10.refs_0_.refs_4_.refs_5_), channel_id=1, source_target_pairs={{0,1},{1,0},{2,3},{3,2},{4,5},{5,4},{6,7},{7,6},{8,10},{9,11},{10,... | collective-permute-start | bytes 3932168 | tf_op jit(solution)/shard_map/ppermute | solution.py:711
  38.3 26.5 %collective-permute-start.4 = (bf16[528,1024]{1,0:T(8,128)(2,1)}, bf16[528,1024]{1,0:T(8,128)(2,1)S(1)}, u32[]{:S(2)}, u32[]{:S(2)}) collective-permute-start(bf16[528,1024]{1,0:T(8,128)(2,1)} %collective-permute-done.w0.refs_2_), channel_id=1, source_target_pairs={{0,8},{4,12},{8,0},{12,4},{16,24},{20,28},{24,16},{28,20},{1,9},{5... | collective-permute-start | bytes 3244040 | tf_op jit(solution)/shard_map/ppermute | solution.py:714
  40.1 26.3 %collective-permute-start.6 = (bf16[528,1024]{1,0:T(8,128)(2,1)}, bf16[528,1024]{1,0:T(8,128)(2,1)S(1)}, u32[]{:S(2)}, u32[]{:S(2)}) collective-permute-start(bf16[528,1024]{1,0:T(8,128)(2,1)} %collective-permute-done.w0.refs_2_), channel_id=1, source_target_pairs={{0,2},{1,3},{2,0},{3,1},{4,6},{5,7},{6,4},{7,5},{8,9},{9,8},{10,11... | collective-permute-start | bytes 3244040 | tf_op jit(solution)/shard_map/ppermute | solution.py:711
  67.5 27.1 %collective-permute-start.11 = (bf16[640,1024]{1,0:T(8,128)(2,1)S(1)}, bf16[640,1024]{1,0:T(8,128)(2,1)S(1)}, u32[]{:S(2)}, u32[]{:S(2)}) collective-permute-start(bf16[640,1024]{1,0:T(8,128)(2,1)S(1)} %collective-permute-done.7.refs_0_.refs_4_.refs_9_), channel_id=1, source_target_pairs={{0,4},{4,0},{8,12},{12,8},{16,20},{20,16},{24,28},{28,24},{1,5},{5... | collective-permute-start | bytes 3932168 | tf_op jit(solution)/shard_map/ppermute | solution.py:714
  67.5 31.2 %collective-permute-start.12 = (bf16[640,1024]{1,0:T(8,128)(2,1)S(1)}, bf16[640,1024]{1,0:T(8,128)(2,1)S(1)}, u32[]{:S(2)}, u32[]{:S(2)}) collective-permute-start(bf16[640,1024]{1,0:T(8,128)(2,1)S(1)} %collective-permute-done.7.refs_0_.refs_4_.refs_9_), channel_id=1, source_target_pairs={{0,2},{1,3},{2,0},{3,1},{4,6},{5,7},{6,4},{7,5},{8,9},{9,8},{10,11... | collective-permute-start | bytes 3932168 | tf_op jit(solution)/shard_map/ppermute | solution.py:711
  98.7 31.2 %collective-permute-start.16 = (bf16[640,1024]{1,0:T(8,128)(2,1)S(1)}, bf16[640,1024]{1,0:T(8,128)(2,1)S(1)}, u32[]{:S(2)}, u32[]{:S(2)}) collective-permute-start(bf16[640,1024]{1,0:T(8,128)(2,1)S(1)} %own_piece.13.refs_1_.refs_5_.refs_6_), channel_id=1, source_target_pairs={{0,1},{1,0},{2,3},{3,2},{4,5},{5,4},{6,7},{7,6},{8,10},{9,11},{10,... | collective-permute-start | bytes 3932168 | tf_op jit(solution)/shard_map/ppermute | solution.py:711
  99.2 30.9 %collective-permute-start.17 = (bf16[640,1024]{1,0:T(8,128)(2,1)S(1)}, bf16[640,1024]{1,0:T(8,128)(2,1)S(1)}, u32[]{:S(2)}, u32[]{:S(2)}) collective-permute-start(bf16[640,1024]{1,0:T(8,128)(2,1)S(1)} %own_piece.10.refs_0_.refs_4_.refs_5_), channel_id=1, source_target_pairs={{0,2},{1,3},{2,0},{3,1},{4,6},{5,7},{6,4},{7,5},{8,9},{9,8},{10,11... | collective-permute-start | bytes 3932168 | tf_op jit(solution)/shard_map/ppermute | solution.py:711
  99.7 30.6 %collective-permute-start.18 = (bf16[640,1024]{1,0:T(8,128)(2,1)S(1)}, bf16[640,1024]{1,0:T(8,128)(2,1)S(1)}, u32[]{:S(2)}, u32[]{:S(2)}) collective-permute-start(bf16[640,1024]{1,0:T(8,128)(2,1)S(1)} %collective-permute-done.7.refs_0_.refs_4_.refs_9_), channel_id=1, source_target_pairs={{0,8},{4,12},{8,0},{12,4},{16,24},{20,28},{24,16},{28,20},{1,9},{5... | collective-permute-start | bytes 3932168 | tf_op jit(solution)/shard_map/ppermute | solution.py:714
  156.1 86.5 %collective-permute-start.27 = (bf16[20,16,512]{2,1,0:T(8,128)(2,1)S(1)}, bf16[20,16,512]{2,1,0:T(8,128)(2,1)S(1)}, u32[]{:S(2)}, u32[]{:S(2)}) collective-permute-start(bf16[20,16,512]{2,1,0:T(8,128)(2,1)S(1)} %get-tuple-element.558), channel_id=1, source_target_pairs={{0,16},{4,20},{8,24},{12,28},{16,0},{20,4},{24,8},{28,12},{1,17},{... | collective-permute-start | bytes 983048 | tf_op jit(solution)/shard_map/ppermute | solution.py:714
  244.0 87.6 %collective-permute-start.30 = (bf16[640,2048]{1,0:T(8,128)(2,1)}, bf16[640,2048]{1,0:T(8,128)(2,1)S(1)}, u32[]{:S(2)}, u32[]{:S(2)}) collective-permute-start(bf16[640,2048]{1,0:T(8,128)(2,1)} %bitcast.205), channel_id=1, source_target_pairs={{0,4},{4,0},{8,12},{12,8},{16,20},{20,16},{24,28},{28,24},{1,5},{5... | collective-permute-start | bytes 7864328 | tf_op jit(solution)/shard_map/ppermute | solution.py:714
  244.2 87.3 %collective-permute-start.28 = (bf16[20,16,512]{2,1,0:T(8,128)(2,1)S(1)}, bf16[20,16,512]{2,1,0:T(8,128)(2,1)S(1)}, u32[]{:S(2)}, u32[]{:S(2)}) collective-permute-start(bf16[20,16,512]{2,1,0:T(8,128)(2,1)S(1)} %get-tuple-element.807), channel_id=1, source_target_pairs={{0,16},{4,20},{8,24},{12,28},{16,0},{20,4},{24,8},{28,12},{1,17},{... | collective-permute-start | bytes 983048 | tf_op jit(solution)/shard_map/ppermute | solution.py:714
  245.9 85.6 %collective-permute-start.29 = (bf16[640,512]{1,0:T(8,128)(2,1)S(1)}, bf16[640,512]{1,0:T(8,128)(2,1)S(1)}, u32[]{:S(2)}, u32[]{:S(2)}) collective-permute-start(bf16[640,512]{1,0:T(8,128)(2,1)S(1)} %bitcast.186), channel_id=1, source_target_pairs={{0,4},{4,0},{8,12},{12,8},{16,20},{20,16},{24,28},{28,24},{1,5},{5... | collective-permute-start | bytes 1966088 | tf_op jit(solution)/shard_map/ppermute | solution.py:714
  353.6 35.9 %collective-permute-start.36 = (bf16[8,144,512]{2,1,0:T(8,128)(2,1)}, bf16[8,144,512]{2,1,0:T(8,128)(2,1)}, u32[]{:S(2)}, u32[]{:S(2)}) collective-permute-start(bf16[8,144,512]{2,1,0:T(8,128)(2,1)} %get-tuple-element.631), channel_id=1, source_target_pairs={{0,1},{1,0},{2,3},{3,2},{4,5},{5,4},{6,7},{7,6},{8,10},{9,11},{10,... | collective-permute-start | bytes 3538952 | tf_op jit(solution)/shard_map/ppermute | solution.py:711
  355.1 34.4 %collective-permute-start.37 = (bf16[8,144,512]{2,1,0:T(8,128)(2,1)}, bf16[8,144,512]{2,1,0:T(8,128)(2,1)}, u32[]{:S(2)}, u32[]{:S(2)}) collective-permute-start(bf16[8,144,512]{2,1,0:T(8,128)(2,1)} %get-tuple-element.632), channel_id=1, source_target_pairs={{0,2},{1,3},{2,0},{3,1},{4,6},{5,7},{6,4},{7,5},{8,9},{9,8},{10,11... | collective-permute-start | bytes 3538952 | tf_op jit(solution)/shard_map/ppermute | solution.py:711
  356.7 32.9 %collective-permute-start.38 = (bf16[2,4,144,512]{3,2,1,0:T(8,128)(2,1)}, bf16[2,4,144,512]{3,2,1,0:T(8,128)(2,1)}, u32[]{:S(2)}, u32[]{:S(2)}) collective-permute-start(bf16[2,4,144,512]{3,2,1,0:T(8,128)(2,1)} %get-tuple-element.633), channel_id=1, source_target_pairs={{0,8},{4,12},{8,0},{12,4},{16,24},{20,28},{24,16},{28,20},{1,9},{5... | collective-permute-start | bytes 3538952 | tf_op jit(solution)/shard_map/ppermute | solution.py:714
  358.3 31.2 %collective-permute-start.39 = (f32[4,512]{1,0:T(4,128)S(1)}, f32[4,512]{1,0:T(4,128)S(1)}, u32[]{:S(2)}, u32[]{:S(2)}) collective-permute-start(f32[4,512]{1,0:T(4,128)S(1)} %get-tuple-element.825), channel_id=1, source_target_pairs={{0,1},{1,0},{2,3},{3,2},{4,5},{5,4},{6,7},{7,6},{8,10},{9,11},{10,... | collective-permute-start | bytes 24584 | tf_op jit(solution)/shard_map/ppermute | solution.py:711
  358.9 30.6 %collective-permute-start.40 = (f32[4,512]{1,0:T(4,128)S(1)}, f32[4,512]{1,0:T(4,128)S(1)}, u32[]{:S(2)}, u32[]{:S(2)}) collective-permute-start(f32[4,512]{1,0:T(4,128)S(1)} %get-tuple-element.824), channel_id=1, source_target_pairs={{0,2},{1,3},{2,0},{3,1},{4,6},{5,7},{6,4},{7,5},{8,9},{9,8},{10,11... | collective-permute-start | bytes 24584 | tf_op jit(solution)/shard_map/ppermute | solution.py:711
  389.6 27.6 %collective-permute-start.45 = (f32[4,512]{1,0:T(4,128)S(1)}, f32[4,512]{1,0:T(4,128)S(1)}, u32[]{:S(2)}, u32[]{:S(2)}) collective-permute-start(f32[4,512]{1,0:T(4,128)S(1)} %get-tuple-element.823), channel_id=1, source_target_pairs={{0,3},{1,2},{2,1},{3,0},{4,7},{5,6},{6,5},{7,4},{8,11},{9,10},{10,... | collective-permute-start | bytes 24584 | tf_op jit(solution)/shard_map/ppermute | solution.py:825
  391.7 28.1 %collective-permute-start.41 = (bf16[8,144,512]{2,1,0:T(8,128)(2,1)}, bf16[8,144,512]{2,1,0:T(8,128)(2,1)}, u32[]{:S(2)}, u32[]{:S(2)}) collective-permute-start(bf16[8,144,512]{2,1,0:T(8,128)(2,1)} %get-tuple-element.655), channel_id=1, source_target_pairs={{0,1},{1,0},{2,3},{3,2},{4,5},{5,4},{6,7},{7,6},{8,10},{9,11},{10,... | collective-permute-start | bytes 3538952 | tf_op jit(solution)/shard_map/ppermute | solution.py:711
  392.2 27.8 %collective-permute-start.42 = (bf16[8,144,512]{2,1,0:T(8,128)(2,1)}, bf16[8,144,512]{2,1,0:T(8,128)(2,1)}, u32[]{:S(2)}, u32[]{:S(2)}) collective-permute-start(bf16[8,144,512]{2,1,0:T(8,128)(2,1)} %get-tuple-element.656), channel_id=1, source_target_pairs={{0,2},{1,3},{2,0},{3,1},{4,6},{5,7},{6,4},{7,5},{8,9},{9,8},{10,11... | collective-permute-start | bytes 3538952 | tf_op jit(solution)/shard_map/ppermute | solution.py:711
  393.2 27.8 %collective-permute-start.43 = (bf16[2,4,144,512]{3,2,1,0:T(8,128)(2,1)}, bf16[2,4,144,512]{3,2,1,0:T(8,128)(2,1)}, u32[]{:S(2)}, u32[]{:S(2)}) collective-permute-start(bf16[2,4,144,512]{3,2,1,0:T(8,128)(2,1)} %get-tuple-element.657), channel_id=1, source_target_pairs={{0,8},{4,12},{8,0},{12,4},{16,24},{20,28},{24,16},{28,20},{1,9},{5... | collective-permute-start | bytes 3538952 | tf_op jit(solution)/shard_map/ppermute | solution.py:714
  421.0 29.4 %collective-permute-start.49 = (f32[4,512]{1,0:T(4,128)S(1)}, f32[4,512]{1,0:T(4,128)S(1)}, u32[]{:S(2)}, u32[]{:S(2)}) collective-permute-start(f32[4,512]{1,0:T(4,128)S(1)} %maximum_select_fusion), channel_id=1, source_target_pairs={{0,8},{4,12},{8,0},{12,4},{16,24},{20,28},{24,16},{28,20},{1,9},{5... | collective-permute-start | bytes 24584 | tf_op jit(solution)/shard_map/ppermute | solution.py:714
  422.0 28.5 %collective-permute-start.46 = (bf16[8,144,512]{2,1,0:T(8,128)(2,1)}, bf16[8,144,512]{2,1,0:T(8,128)(2,1)S(1)}, u32[]{:S(2)}, u32[]{:S(2)}) collective-permute-start(bf16[8,144,512]{2,1,0:T(8,128)(2,1)} %add_convert_fusion.3), channel_id=1, source_target_pairs={{0,1},{1,0},{2,3},{3,2},{4,5},{5,4},{6,7},{7,6},{8,10},{9,11},{10,... | collective-permute-start | bytes 3538952 | tf_op jit(solution)/shard_map/ppermute | solution.py:711
  423.5 27.0 %collective-permute-start.47 = (bf16[8,144,512]{2,1,0:T(8,128)(2,1)}, bf16[8,144,512]{2,1,0:T(8,128)(2,1)S(1)}, u32[]{:S(2)}, u32[]{:S(2)}) collective-permute-start(bf16[8,144,512]{2,1,0:T(8,128)(2,1)} %add_convert_fusion.2), channel_id=1, source_target_pairs={{0,2},{1,3},{2,0},{3,1},{4,6},{5,7},{6,4},{7,5},{8,9},{9,8},{10,11... | collective-permute-start | bytes 3538952 | tf_op jit(solution)/shard_map/ppermute | solution.py:711
  452.6 33.9 %collective-permute-start.54 = (bf16[2,4,144,512]{3,2,1,0:T(8,128)(2,1)}, bf16[2,4,144,512]{3,2,1,0:T(8,128)(2,1)}, u32[]{:S(2)}, u32[]{:S(2)}) collective-permute-start(bf16[2,4,144,512]{3,2,1,0:T(8,128)(2,1)} %pad_maximum_fusion), channel_id=1, source_target_pairs={{0,8},{4,12},{8,0},{12,4},{16,24},{20,28},{24,16},{28,20},{1,9},{5... | collective-permute-start | bytes 3538952 | tf_op jit(solution)/shard_map/ppermute | solution.py:714
  457.3 29.2 %collective-permute-start.50 = (bf16[4,144,512]{2,1,0:T(8,128)(2,1)}, bf16[4,144,512]{2,1,0:T(8,128)(2,1)}, u32[]{:S(2)}, u32[]{:S(2)}) collective-permute-start(bf16[4,144,512]{2,1,0:T(8,128)(2,1)} %get-tuple-element.778), channel_id=1, source_target_pairs={{0,1},{1,0},{2,3},{3,2},{4,5},{5,4},{6,7},{7,6},{8,10},{9,11},{10,... | collective-permute-start | bytes 1769480 | tf_op jit(solution)/shard_map/ppermute | solution.py:711
  458.7 27.8 %collective-permute-start.51 = (bf16[4,144,512]{2,1,0:T(8,128)(2,1)}, bf16[4,144,512]{2,1,0:T(8,128)(2,1)}, u32[]{:S(2)}, u32[]{:S(2)}) collective-permute-start(bf16[4,144,512]{2,1,0:T(8,128)(2,1)} %get-tuple-element.720), channel_id=1, source_target_pairs={{0,2},{1,3},{2,0},{3,1},{4,6},{5,7},{6,4},{7,5},{8,9},{9,8},{10,11... | collective-permute-start | bytes 1769480 | tf_op jit(solution)/shard_map/ppermute | solution.py:711
  490.8 26.3 %collective-permute-start.60 = (bf16[320,1152]{1,0:T(8,128)(2,1)S(1)}, bf16[320,1152]{1,0:T(8,128)(2,1)S(1)}, u32[]{:S(2)}, u32[]{:S(2)}) collective-permute-start(bf16[320,1152]{1,0:T(8,128)(2,1)S(1)} %get-tuple-element.800), channel_id=1, source_target_pairs={{0,3},{1,2},{2,1},{3,0},{4,7},{5,6},{6,5},{7,4},{8,11},{9,10},{10,... | collective-permute-start | bytes 2211848 | tf_op jit(solution)/shard_map/ppermute | solution.py:825
  497.1 34.2 %collective-permute-start.58 = (bf16[2,4,144,512]{3,2,1,0:T(8,128)(2,1)S(1)}, bf16[2,4,144,512]{3,2,1,0:T(8,128)(2,1)S(1)}, u32[]{:S(2)}, u32[]{:S(2)}) collective-permute-start(bf16[2,4,144,512]{3,2,1,0:T(8,128)(2,1)S(1)} %copy-done.127), channel_id=1, source_target_pairs={{0,8},{4,12},{8,0},{12,4},{16,24},{20,28},{24,16},{28,20},{1,9},{5... | collective-permute-start | bytes 3538952 | tf_op jit(solution)/shard_map/ppermute | solution.py:714
  534.7 28.4 %collective-permute-start.61 = (bf16[2,2,144,512]{3,2,0,1:T(8,128)(2,1)S(1)}, bf16[2,2,144,512]{3,2,0,1:T(8,128)(2,1)S(1)}, u32[]{:S(2)}, u32[]{:S(2)}) collective-permute-start(bf16[2,2,144,512]{3,2,0,1:T(8,128)(2,1)S(1)} %pad_maximum_fusion.11), channel_id=1, source_target_pairs={{0,16},{4,20},{8,24},{12,28},{16,0},{20,4},{24,8},{28,12},{1,17},{... | collective-permute-start | bytes 1769480 | tf_op jit(solution)/shard_map/ppermute | solution.py:714
  (164 other events, 1922.8 us)

commit v6 on v5

--- a/solution.py
+++ b/solution.py
@@ -601,27 +601,25 @@
     return results[:PARTS], results[PARTS:]
 
 
-def assemble_kernel(order_ref, *refs):
-    weight_out, proj_out = refs[4:]
+def assemble_kernel(order_ref, own_ref, far_ref, *refs):
+    weight_out, proj_out = refs[-2:]
     depth = weight_out.shape[1]
-    group = refs[0].shape[-2] - depth
-
-    def body(tiles):
-        for u, tile_ref in enumerate(tiles):
-            value = tile_ref[0, 0].astype(F32)
-            lanes = slice(u * LANES, (u + 1) * LANES)
-            for q in range(4):
-                columns = slice(q * LANES, (q + 1) * LANES)
-                weight_out[0, :, q, lanes] = value[:depth, columns]
-                proj_out[0, q * group : (q + 1) * group, lanes] = value[depth:, columns]
+    group = own_ref.shape[-2] - depth
+
+    def body(tile_ref):
+        value = tile_ref[0, 0].astype(F32)
+        for q in range(4):
+            columns = slice(q * LANES, (q + 1) * LANES)
+            weight_out[0, :, q, :] = value[:depth, columns]
+            proj_out[0, q * group : (q + 1) * group, :] = value[depth:, columns]
 
     far = (pl.program_id(1) // 2) ^ order_ref[1]
-    pl.when(far == 0)(lambda: body(refs[:2]))
-    pl.when(far == 1)(lambda: body(refs[2:4]))
-
-
-def assemble(order, own0, own1, far0, far1, depth):
-    lines = own0.shape[2]
+    pl.when(far == 0)(lambda: body(own_ref))
+    pl.when(far == 1)(lambda: body(far_ref))
+
+
+def assemble(order, own, far, u, depth, before=()):
+    lines = own.shape[2]
     group = lines - depth
     cells = 8 * LANES
     piece = pl.BlockSpec((1, 1, lines, 4 * LANES), lambda d, n, o: (d ^ o[0], (n % 2) ^ o[2], 0, 0))
@@ -630,20 +628,21 @@
         grid_spec=pltpu.PrefetchScalarGridSpec(
             num_scalar_prefetch=1,
             grid=(2, 4),
-            in_specs=[piece] * 4,
+            in_specs=[piece] * 2 + [pl.BlockSpec(memory_space=pl.ANY)] * len(before),
             out_specs=[
-                pl.BlockSpec((1, depth, 4, 2 * LANES), lambda d, n, o: (d, 0, 0, n)),
-                pl.BlockSpec((1, 4 * group, 2 * LANES), lambda d, n, o: (d, 0, n)),
+                pl.BlockSpec((1, depth, 4, LANES), lambda d, n, o: (d, 0, 0, n * 2 + u)),
+                pl.BlockSpec((1, 4 * group, LANES), lambda d, n, o: (d, 0, n * 2 + u)),
             ],
         ),
         out_shape=[
             jax.ShapeDtypeStruct((2, depth, 4, cells), F32),
             jax.ShapeDtypeStruct((2, 4 * group, cells), F32),
         ],
+        input_output_aliases={3 + n: n for n in range(len(before))},
         compiler_params=pltpu.CompilerParams(vmem_limit_bytes=16 * 2**20),
         cost_estimate=LIGHT,
         name="assemble_gradients",
-    )(order, own0, own1, far0, far1)
+    )(order, own, far, *before)
 
 
 def input_grad_kernel(has_sum, *refs):
@@ -754,7 +753,6 @@
     xk_here = jnp.concatenate([x_mine, by_dir(keep_wide)], axis=2)
     xk_sent = jnp.concatenate([x_mine, by_other(keep_wide)], axis=2)
     xk_met = half_swap(xk_sent)
-    w_in[0, 1] = input_piece(1)
     g_mine = lax.dynamic_slice_in_dim(grad_out, col * own_tokens, own_tokens, 0).reshape(share, STEPS, 2, model)
     g_dirs = (steps_first(g_mine[:, :, 0]), steps_first(g_mine[:, :, 1]))
     w_in, w_rec, xk_here, xk_met, g_dirs, places = after((w_in, w_rec, xk_here, xk_met, g_dirs, places))
@@ -764,7 +762,8 @@
     w_in[2, 1] = pair_swap(w_in[1, 0])
     for b in (1, 2):
         w_in[b, 2] = core_swap(w_in[b, 0])
-    w_rec[0, 1], w_in[0, 2], w_in[0, 3] = recurrent_piece(1), input_piece(2), input_piece(3)
+    w_in[0, 1], w_rec[0, 1] = input_piece(1), recurrent_piece(1)
+    w_in[0, 2], w_in[0, 3] = input_piece(2), input_piece(3)
     xk = in_run(jnp.concatenate([xk_here, xk_met], axis=1))
     x_run, keep_run = xk[..., :model], xk[..., model:].astype(F32)
     x_flat = x_run.reshape(STEPS * rows, model)
@@ -956,13 +955,14 @@
     for mask, value in enumerate(incoming):
         input_grad = lax.dynamic_update_slice(input_grad, value[:, 2 * model :], ((col ^ mask) * own_tokens, 0))
     bias_total = jnp.concatenate(by_side(bias_half, core_swap(bias_half)), axis=2)
-    here1, there1, kept0, met0, block_out, input_grad, bias_total = after(
-        (here1, there1, kept0, met0, block_out, input_grad, bias_total)
+    shares = assemble(order, kept0, met0, 0, 2 * model // 8)
+    here1, there1, shares, block_out, input_grad, bias_total = after(
+        (here1, there1, shares, block_out, input_grad, bias_total)
     )
 
     kept1, sent1 = two_directions(here1, there1)
     met1 = core_swap(sent1)
-    weight_share, proj_share = assemble(order, kept0, kept1, met0, met1, 2 * model // 8)
+    weight_share, proj_share = assemble(order, kept1, met1, 1, 2 * model // 8, shares)
     proj_share = jnp.swapaxes(proj_share, 1, 2)
     return (block_out, input_grad, weight_share, bias_total, proj_share)
 

time: 580 us -> 578 us (level)
    unnamed x259 -> x255, local copies, waits for them, and re-layouts: 37.7 us -> 34.3 us
  transfers between devices with their start and end apart: 67 -> 67, of which waited for: 29 -> 30; matrix products, arithmetic and copies ran while one was open for 7% -> 7% of each run, Pallas kernels for 52% -> 53%
where the time goes in v6:
time: 578 us; the launch traced here: 569 us
  Pallas kernels  312 us (54%)
  waiting for transfers between devices  111 us (19%)
  starting transfers between devices  60 us (10%)
  local copies, waits for them, and re-layouts  51.5 us (9%)
  other arithmetic  31.3 us (5%)
    pallas_call x1, Pallas kernels, run_backward(): pl.pallas_call(backward_kernel, grid=(steps,), out_shape=tuple([shape(hal...  85.3 us
    pallas_call x1, Pallas kernels, run_forward(): pl.pallas_call(forward_kernel, grid=(steps,), out_shape=tuple((jax.ShapeD...  85.1 us
    ppermute x40, waiting for transfers between devices, over_rows(): return lax.ppermute(value, 'rows', [(r, r ^ mask) for r in range(8)])  65.3 us
    pallas_call x4, Pallas kernels, block_grads(): pl.pallas_call(block_kernel, grid_spec=pltpu.PrefetchScalarGridSpec(num_s...  56.1 us
    ppermute x23, waiting for transfers between devices, over_chips(): return lax.ppermute(value, ('rows', 'cols'), pairs)  35.5 us
    unnamed x255, local copies, waits for them, and re-layouts  34.3 us
    pallas_call x8, Pallas kernels, own_piece(): pl.pallas_call(own_piece_kernel, grid_spec=pltpu.PrefetchScalarGridSpec(n...  28.7 us
    ppermute x23, starting transfers between devices, over_chips(): return lax.ppermute(value, ('rows', 'cols'), pairs)  27.1 us
  transfers between devices with their start and end apart: 67, of which 30 were waited for; matrix products, arithmetic and copies ran while one was open for 7% of the time, Pallas kernels for 53%

profile of v6, /device:TPU:0, one launch (start us, length us, event | category | flops | bytes accessed | tf_op | source)
XLA Modules:
  0.0 569.1 jit_solution(9995275764915622269)
XLA Ops:
  1.4 5.6 own_piece.8.w0.refs_2_
  19.4 5.8 %copy-done.2 = bf16[2,1024,4,1024]{3,2,1,0:T(4,128)(2,1)S(1)} copy-done((bf16[2,1024,4,1024]{3,2,1,0:T(4,128)(2,1)S(1)}, bf16[2,1024,4,1024]{3,2,1,0:T(4,128)(2,1)}, u32[]{:S(2)}) %copy-start.2) | copy-done | bytes 16777240
  25.1 3.3 own_piece.9.refs_0_.refs_4_.refs_5_
  31.0 3.9 collective-permute-done.2
  39.4 5.8 %copy-done.3 = bf16[2,1024,4,1024]{3,2,1,0:T(4,128)(2,1)S(1)} copy-done((bf16[2,1024,4,1024]{3,2,1,0:T(4,128)(2,1)S(1)}, bf16[2,1024,4,1024]{3,2,1,0:T(4,128)(2,1)}, u32[]{:S(2)}) %copy-start.3) | copy-done | bytes 16777240
  45.2 3.3 own_piece.13.refs_1_.refs_5_.refs_6_
  48.5 3.3 own_piece.10.w1.refs_3_
  68.8 3.3 own_piece.14.refs_2_.refs_6_.refs_7_
  72.2 3.3 own_piece.15.refs_3_.refs_7_.refs_8_
  81.1 11.6 %collective-permute-done.8.w1.refs_3_ = bf16[528,1024]{1,0:T(8,128)(2,1)S(1)} collective-permute-done((bf16[528,1024]{1,0:T(8,128)(2,1)S(1)}, bf16[528,1024]{1,0:T(8,128)(2,1)S(1)}, u32[]{:S(2)}, u32[]{:S(2)}) %collective-permute-start.8) | collective-permute-done | bytes 1081376 | tf_op jit(solution)/shard_map/ppermute | solution.py:710
  109.4 4.8 input_gates.6
  116.5 4.8 input_gates.5
  123.6 3.7 collective-permute-done.16.refs_1_.refs_5_.refs_10_
  157.5 85.1 %forward_chain.1 = (bf16[20,32,16384]{2,1,0:T(8,128)(2,1)}, f32[20,32,4096]{2,1,0:T(8,128)}, bf16[20,32,2048]{2,1,0:T(8,128)(2,1)}, bf16[20,32,2048]{2,1,0:T(8,1...) custom-call(bf16[20,32,4096]{2,1,0:T(8,128)(2,1)} %bitcast.175, ...), custom_call_target="tpu_custom_call" | custom-call | flops 107374182400 | bytes 83886080 | tf_op jit(solution)/shard_map/forward_chain/pallas_call | solution.py:329
  246.0 85.3 %backward_chain.1 = (bf16[20,32,2048]{2,1,0:T(8,128)(2,1)}, bf16[20,32,2048]{2,1,0:T(8,128)(2,1)}, bf16[20,32,2048]{2,1,0:T(8,128)(2,1)}, bf16[20,32,2048]{2,1,0...) custom-call(bf16[20,32,16384]{2,1,0:T(8,128)(2,1)} %get-tuple-elemen, ...), custom_call_target="tpu_custom_call" | custom-call | flops 107374182400 | bytes 83886080 | tf_op jit(solution)/shard_map/backward_chain/pallas_call | solution.py:432
  339.0 14.0 %weight_gradients.4 = (bf16[8,144,512]{2,1,0:T(8,128)(2,1)}, bf16[8,144,512]{2,1,0:T(8,128)(2,1)}, bf16[2,4,144,512]{3,2,1,0:T(8,128)(2,1)}, bf16[2,4,144,512]{3,2,1,0:T(8,128)(2,1)}) custom-call(s32[3]{0:T(128)} %pad_add_fusion.4.order_ref, bf16[512,1280]{1,0:T(8,128)(2,1)} %copy-done.5, bf16[512,1280]{1,0:T(8,128)(2,1)} %copy-done.6, ...), custom_call_target="tpu_custom_call" | custom-call | flops 1 | bytes 1 | tf_op jit(solution)/shard_map/weight_gradients/pallas_call | solution.py:502
  361.3 13.8 %weight_gradients.5 = (bf16[8,144,512]{2,1,0:T(8,128)(2,1)}, bf16[8,144,512]{2,1,0:T(8,128)(2,1)}, bf16[2,4,144,512]{3,2,1,0:T(8,128)(2,1)}, bf16[2,4,144,512]{3,2,1,0:T(8,128)(2,1)}) custom-call(s32[3]{0:T(128)} %pad_add_fusion.4.order_ref, bf16[512,1280]{1,0:T(8,128)(2,1)} %copy-done.5, bf16[512,1280]{1,0:T(8,128)(2,1)} %copy-done.6, ...), custom_call_target="tpu_custom_call" | custom-call | flops 1 | bytes 1 | tf_op jit(solution)/shard_map/weight_gradients/pallas_call | solution.py:502
  375.1 13.7 %weight_gradients.6 = (bf16[8,144,512]{2,1,0:T(8,128)(2,1)}, bf16[8,144,512]{2,1,0:T(8,128)(2,1)}, bf16[2,4,144,512]{3,2,1,0:T(8,128)(2,1)}, bf16[2,4,144,512]{3,2,1,0:T(8,128)(2,1)}) custom-call(s32[3]{0:T(128)} %pad_add_fusion.4.order_ref, bf16[512,1280]{1,0:T(8,128)(2,1)} %copy-done.5, bf16[512,1280]{1,0:T(8,128)(2,1)} %copy-done.6, ...), custom_call_target="tpu_custom_call" | custom-call | flops 1 | bytes 1 | tf_op jit(solution)/shard_map/weight_gradients/pallas_call | solution.py:502
  402.0 14.6 %weight_gradients.7 = (bf16[8,144,512]{2,1,0:T(8,128)(2,1)}, bf16[8,144,512]{2,1,0:T(8,128)(2,1)}, bf16[2,4,144,512]{3,2,1,0:T(8,128)(2,1)}, bf16[2,4,144,512]{3,2,1,0:T(8,128)(2,1)}) custom-call(s32[3]{0:T(128)} %pad_add_fusion.4.order_ref, bf16[512,1280]{1,0:T(8,128)(2,1)} %copy-done.5, bf16[512,1280]{1,0:T(8,128)(2,1)} %copy-done.6, ...), custom_call_target="tpu_custom_call" | custom-call | flops 1 | bytes 1 | tf_op jit(solution)/shard_map/weight_gradients/pallas_call | solution.py:502
  424.3 4.6 input_gradient.4.refs_6_
  429.0 4.5 input_gradient.5.refs_6_
  433.6 4.5 input_gradient.6.refs_6_
  438.2 3.4 input_gradient.7
  461.9 8.7 %collective-permute-done.52 = bf16[4,144,512]{2,1,0:T(8,128)(2,1)} collective-permute-done((bf16[4,144,512]{2,1,0:T(8,128)(2,1)}, bf16[4,144,512]{2,1,0:T(8,128)(2,1)}, u32[]{:S(2)}, u32[]{:S(2)}) %collective-permute-start.52) | collective-permute-done | bytes 589856 | tf_op jit(solution)/shard_map/ppermute | solution.py:710
  472.1 13.4 %collective-permute-done.55 = bf16[336,512]{1,0:T(8,128)(2,1)S(1)} collective-permute-done((bf16[336,512]{1,0:T(8,128)(2,1)}, bf16[336,512]{1,0:T(8,128)(2,1)S(1)}, u32[]{:S(2)}, u32[]{:S(2)}) %collective-permute-start.55) | collective-permute-done | bytes 344096 | tf_op jit(solution)/shard_map/ppermute | solution.py:713
  502.5 13.1 %collective-permute-done.59 = bf16[2,2,144,512]{3,2,0,1:T(8,128)(2,1)S(1)} collective-permute-done((bf16[2,2,144,512]{3,2,0,1:T(8,128)(2,1)S(1)}, bf16[2,2,144,512]{3,2,0,1:T(8,128)(2,1)S(1)}, u32[]{:S(2)}, u32[]{:S(2)}) %collective-permute-start.59) | collective-permute-done | bytes 589856 | tf_op jit(solution)/shard_map/ppermute | solution.py:713
  516.0 13.3 %collective-permute-done.58 = bf16[2,4,144,512]{3,2,1,0:T(8,128)(2,1)S(1)} collective-permute-done((bf16[2,4,144,512]{3,2,1,0:T(8,128)(2,1)S(1)}, bf16[2,4,144,512]{3,2,1,0:T(8,128)(2,1)S(1)}, u32[]{:S(2)}, u32[]{:S(2)}) %collective-permute-start.58) | collective-permute-done | bytes 1179680 | tf_op jit(solution)/shard_map/ppermute | solution.py:713
  534.9 4.2 assemble_gradients.2
  539.1 9.1 %collective-permute-done.63 = bf16[320,1152]{1,0:T(8,128)(2,1)S(1)} collective-permute-done((bf16[320,1152]{1,0:T(8,128)(2,1)S(1)}, bf16[320,1152]{1,0:T(8,128)(2,1)S(1)}, u32[]{:S(2)}, u32[]{:S(2)}) %collective-permute-start.63) | collective-permute-done | bytes 737312 | tf_op jit(solution)/shard_map/ppermute | solution.py:824
  549.6 4.3 layer_sum.1
  554.0 8.3 %collective-permute-done.61 = bf16[2,2,144,512]{3,2,0,1:T(8,128)(2,1)S(1)} collective-permute-done((bf16[2,2,144,512]{3,2,0,1:T(8,128)(2,1)S(1)}, bf16[2,2,144,512]{3,2,0,1:T(8,128)(2,1)S(1)}, u32[]{:S(2)}, u32[]{:S(2)}) %collective-permute-start.61) | collective-permute-done | bytes 589856 | tf_op jit(solution)/shard_map/ppermute | solution.py:713
  564.4 4.2 assemble_gradients.3
  (484 shorter events, 181.3 us)
Async XLA Ops:
  7.0 27.9 %collective-permute-start = (bf16[528,1024]{1,0:T(8,128)(2,1)}, bf16[528,1024]{1,0:T(8,128)(2,1)}, u32[]{:S(2)}, u32[]{:S(2)}) collective-permute-start(bf16[528,1024]{1,0:T(8,128)(2,1)} %own_piece.8.w0.refs_2_), channel_id=1, source_target_pairs={{0,1},{1,0},{2,3},{3,2},{4,5},{5,4},{6,7},{7,6},{8,10},{9,11},{10,... | collective-permute-start | bytes 3244040 | tf_op jit(solution)/shard_map/ppermute | solution.py:710
  35.6 29.3 %collective-permute-start.7 = (bf16[640,1024]{1,0:T(8,128)(2,1)S(1)}, bf16[640,1024]{1,0:T(8,128)(2,1)S(1)}, u32[]{:S(2)}, u32[]{:S(2)}) collective-permute-start(bf16[640,1024]{1,0:T(8,128)(2,1)S(1)} %own_piece.9.refs_0_.refs_4_.refs_5_), channel_id=1, source_target_pairs={{0,1},{1,0},{2,3},{3,2},{4,5},{5,4},{6,7},{7,6},{8,10},{9,11},{10,... | collective-permute-start | bytes 3932168 | tf_op jit(solution)/shard_map/ppermute | solution.py:710
  35.9 26.5 %collective-permute-start.4 = (bf16[528,1024]{1,0:T(8,128)(2,1)}, bf16[528,1024]{1,0:T(8,128)(2,1)S(1)}, u32[]{:S(2)}, u32[]{:S(2)}) collective-permute-start(bf16[528,1024]{1,0:T(8,128)(2,1)} %collective-permute-done.w0.refs_2_), channel_id=1, source_target_pairs={{0,8},{4,12},{8,0},{12,4},{16,24},{20,28},{24,16},{28,20},{1,9},{5... | collective-permute-start | bytes 3244040 | tf_op jit(solution)/shard_map/ppermute | solution.py:713
  37.9 26.3 %collective-permute-start.6 = (bf16[528,1024]{1,0:T(8,128)(2,1)}, bf16[528,1024]{1,0:T(8,128)(2,1)S(1)}, u32[]{:S(2)}, u32[]{:S(2)}) collective-permute-start(bf16[528,1024]{1,0:T(8,128)(2,1)} %collective-permute-done.w0.refs_2_), channel_id=1, source_target_pairs={{0,2},{1,3},{2,0},{3,1},{4,6},{5,7},{6,4},{7,5},{8,9},{9,8},{10,11... | collective-permute-start | bytes 3244040 | tf_op jit(solution)/shard_map/ppermute | solution.py:710
  64.9 28.4 %collective-permute-start.11 = (bf16[640,1024]{1,0:T(8,128)(2,1)S(1)}, bf16[640,1024]{1,0:T(8,128)(2,1)S(1)}, u32[]{:S(2)}, u32[]{:S(2)}) collective-permute-start(bf16[640,1024]{1,0:T(8,128)(2,1)S(1)} %collective-permute-done.7.refs_0_.refs_4_.refs_9_), channel_id=1, source_target_pairs={{0,4},{4,0},{8,12},{12,8},{16,20},{20,16},{24,28},{28,24},{1,5},{5... | collective-permute-start | bytes 3932168 | tf_op jit(solution)/shard_map/ppermute | solution.py:713
  64.9 31.2 %collective-permute-start.12 = (bf16[640,1024]{1,0:T(8,128)(2,1)S(1)}, bf16[640,1024]{1,0:T(8,128)(2,1)S(1)}, u32[]{:S(2)}, u32[]{:S(2)}) collective-permute-start(bf16[640,1024]{1,0:T(8,128)(2,1)S(1)} %collective-permute-done.7.refs_0_.refs_4_.refs_9_), channel_id=1, source_target_pairs={{0,2},{1,3},{2,0},{3,1},{4,6},{5,7},{6,4},{7,5},{8,9},{9,8},{10,11... | collective-permute-start | bytes 3932168 | tf_op jit(solution)/shard_map/ppermute | solution.py:710
  66.7 26.0 %collective-permute-start.8 = (bf16[528,1024]{1,0:T(8,128)(2,1)S(1)}, bf16[528,1024]{1,0:T(8,128)(2,1)S(1)}, u32[]{:S(2)}, u32[]{:S(2)}) collective-permute-start(bf16[528,1024]{1,0:T(8,128)(2,1)S(1)} %own_piece.10.w1.refs_3_), channel_id=1, source_target_pairs={{0,1},{1,0},{2,3},{3,2},{4,5},{5,4},{6,7},{7,6},{8,10},{9,11},{10,... | collective-permute-start | bytes 3244040 | tf_op jit(solution)/shard_map/ppermute | solution.py:710
  96.1 31.2 %collective-permute-start.16 = (bf16[640,1024]{1,0:T(8,128)(2,1)S(1)}, bf16[640,1024]{1,0:T(8,128)(2,1)S(1)}, u32[]{:S(2)}, u32[]{:S(2)}) collective-permute-start(bf16[640,1024]{1,0:T(8,128)(2,1)S(1)} %own_piece.13.refs_1_.refs_5_.refs_6_), channel_id=1, source_target_pairs={{0,1},{1,0},{2,3},{3,2},{4,5},{5,4},{6,7},{7,6},{8,10},{9,11},{10,... | collective-permute-start | bytes 3932168 | tf_op jit(solution)/shard_map/ppermute | solution.py:710
  97.0 30.9 %collective-permute-start.17 = (bf16[640,1024]{1,0:T(8,128)(2,1)S(1)}, bf16[640,1024]{1,0:T(8,128)(2,1)S(1)}, u32[]{:S(2)}, u32[]{:S(2)}) collective-permute-start(bf16[640,1024]{1,0:T(8,128)(2,1)S(1)} %own_piece.9.refs_0_.refs_4_.refs_5_), channel_id=1, source_target_pairs={{0,2},{1,3},{2,0},{3,1},{4,6},{5,7},{6,4},{7,5},{8,9},{9,8},{10,11... | collective-permute-start | bytes 3932168 | tf_op jit(solution)/shard_map/ppermute | solution.py:710
  98.5 30.6 %collective-permute-start.18 = (bf16[640,1024]{1,0:T(8,128)(2,1)S(1)}, bf16[640,1024]{1,0:T(8,128)(2,1)S(1)}, u32[]{:S(2)}, u32[]{:S(2)}) collective-permute-start(bf16[640,1024]{1,0:T(8,128)(2,1)S(1)} %collective-permute-done.7.refs_0_.refs_4_.refs_9_), channel_id=1, source_target_pairs={{0,8},{4,12},{8,0},{12,4},{16,24},{20,28},{24,16},{28,20},{1,9},{5... | collective-permute-start | bytes 3932168 | tf_op jit(solution)/shard_map/ppermute | solution.py:713
  154.8 87.8 %collective-permute-start.27 = (bf16[20,16,512]{2,1,0:T(8,128)(2,1)S(1)}, bf16[20,16,512]{2,1,0:T(8,128)(2,1)S(1)}, u32[]{:S(2)}, u32[]{:S(2)}) collective-permute-start(bf16[20,16,512]{2,1,0:T(8,128)(2,1)S(1)} %get-tuple-element.558), channel_id=1, source_target_pairs={{0,16},{4,20},{8,24},{12,28},{16,0},{20,4},{24,8},{28,12},{1,17},{... | collective-permute-start | bytes 983048 | tf_op jit(solution)/shard_map/ppermute | solution.py:713
  244.0 87.3 %collective-permute-start.30 = (bf16[640,2048]{1,0:T(8,128)(2,1)}, bf16[640,2048]{1,0:T(8,128)(2,1)S(1)}, u32[]{:S(2)}, u32[]{:S(2)}) collective-permute-start(bf16[640,2048]{1,0:T(8,128)(2,1)} %bitcast.206), channel_id=1, source_target_pairs={{0,4},{4,0},{8,12},{12,8},{16,20},{20,16},{24,28},{28,24},{1,5},{5... | collective-permute-start | bytes 7864328 | tf_op jit(solution)/shard_map/ppermute | solution.py:713
  244.3 87.0 %collective-permute-start.28 = (bf16[20,16,512]{2,1,0:T(8,128)(2,1)S(1)}, bf16[20,16,512]{2,1,0:T(8,128)(2,1)S(1)}, u32[]{:S(2)}, u32[]{:S(2)}) collective-permute-start(bf16[20,16,512]{2,1,0:T(8,128)(2,1)S(1)} %get-tuple-element.809), channel_id=1, source_target_pairs={{0,16},{4,20},{8,24},{12,28},{16,0},{20,4},{24,8},{28,12},{1,17},{... | collective-permute-start | bytes 983048 | tf_op jit(solution)/shard_map/ppermute | solution.py:713
  245.7 85.6 %collective-permute-start.29 = (bf16[640,512]{1,0:T(8,128)(2,1)S(1)}, bf16[640,512]{1,0:T(8,128)(2,1)S(1)}, u32[]{:S(2)}, u32[]{:S(2)}) collective-permute-start(bf16[640,512]{1,0:T(8,128)(2,1)S(1)} %bitcast.186), channel_id=1, source_target_pairs={{0,4},{4,0},{8,12},{12,8},{16,20},{20,16},{24,28},{28,24},{1,5},{5... | collective-permute-start | bytes 1966088 | tf_op jit(solution)/shard_map/ppermute | solution.py:713
  353.4 35.4 %collective-permute-start.36 = (bf16[8,144,512]{2,1,0:T(8,128)(2,1)}, bf16[8,144,512]{2,1,0:T(8,128)(2,1)}, u32[]{:S(2)}, u32[]{:S(2)}) collective-permute-start(bf16[8,144,512]{2,1,0:T(8,128)(2,1)} %get-tuple-element.631), channel_id=1, source_target_pairs={{0,1},{1,0},{2,3},{3,2},{4,5},{5,4},{6,7},{7,6},{8,10},{9,11},{10,... | collective-permute-start | bytes 3538952 | tf_op jit(solution)/shard_map/ppermute | solution.py:710
  354.6 34.3 %collective-permute-start.37 = (bf16[8,144,512]{2,1,0:T(8,128)(2,1)}, bf16[8,144,512]{2,1,0:T(8,128)(2,1)}, u32[]{:S(2)}, u32[]{:S(2)}) collective-permute-start(bf16[8,144,512]{2,1,0:T(8,128)(2,1)} %get-tuple-element.632), channel_id=1, source_target_pairs={{0,2},{1,3},{2,0},{3,1},{4,6},{5,7},{6,4},{7,5},{8,9},{9,8},{10,11... | collective-permute-start | bytes 3538952 | tf_op jit(solution)/shard_map/ppermute | solution.py:710
  355.5 33.3 %collective-permute-start.38 = (bf16[2,4,144,512]{3,2,1,0:T(8,128)(2,1)}, bf16[2,4,144,512]{3,2,1,0:T(8,128)(2,1)}, u32[]{:S(2)}, u32[]{:S(2)}) collective-permute-start(bf16[2,4,144,512]{3,2,1,0:T(8,128)(2,1)} %get-tuple-element.633), channel_id=1, source_target_pairs={{0,8},{4,12},{8,0},{12,4},{16,24},{20,28},{24,16},{28,20},{1,9},{5... | collective-permute-start | bytes 3538952 | tf_op jit(solution)/shard_map/ppermute | solution.py:713
  357.3 31.5 %collective-permute-start.39 = (f32[4,512]{1,0:T(4,128)S(1)}, f32[4,512]{1,0:T(4,128)S(1)}, u32[]{:S(2)}, u32[]{:S(2)}) collective-permute-start(f32[4,512]{1,0:T(4,128)S(1)} %get-tuple-element.827), channel_id=1, source_target_pairs={{0,1},{1,0},{2,3},{3,2},{4,5},{5,4},{6,7},{7,6},{8,10},{9,11},{10,... | collective-permute-start | bytes 24584 | tf_op jit(solution)/shard_map/ppermute | solution.py:710
  358.3 30.5 %collective-permute-start.40 = (f32[4,512]{1,0:T(4,128)S(1)}, f32[4,512]{1,0:T(4,128)S(1)}, u32[]{:S(2)}, u32[]{:S(2)}) collective-permute-start(f32[4,512]{1,0:T(4,128)S(1)} %get-tuple-element.826), channel_id=1, source_target_pairs={{0,2},{1,3},{2,0},{3,1},{4,6},{5,7},{6,4},{7,5},{8,9},{9,8},{10,11... | collective-permute-start | bytes 24584 | tf_op jit(solution)/shard_map/ppermute | solution.py:710
  389.0 27.6 %collective-permute-start.45 = (f32[4,512]{1,0:T(4,128)S(1)}, f32[4,512]{1,0:T(4,128)S(1)}, u32[]{:S(2)}, u32[]{:S(2)}) collective-permute-start(f32[4,512]{1,0:T(4,128)S(1)} %get-tuple-element.825), channel_id=1, source_target_pairs={{0,3},{1,2},{2,1},{3,0},{4,7},{5,6},{6,5},{7,4},{8,11},{9,10},{10,... | collective-permute-start | bytes 24584 | tf_op jit(solution)/shard_map/ppermute | solution.py:824
  390.5 28.1 %collective-permute-start.41 = (bf16[8,144,512]{2,1,0:T(8,128)(2,1)}, bf16[8,144,512]{2,1,0:T(8,128)(2,1)}, u32[]{:S(2)}, u32[]{:S(2)}) collective-permute-start(bf16[8,144,512]{2,1,0:T(8,128)(2,1)} %get-tuple-element.655), channel_id=1, source_target_pairs={{0,1},{1,0},{2,3},{3,2},{4,5},{5,4},{6,7},{7,6},{8,10},{9,11},{10,... | collective-permute-start | bytes 3538952 | tf_op jit(solution)/shard_map/ppermute | solution.py:710
  391.4 27.8 %collective-permute-start.42 = (bf16[8,144,512]{2,1,0:T(8,128)(2,1)}, bf16[8,144,512]{2,1,0:T(8,128)(2,1)}, u32[]{:S(2)}, u32[]{:S(2)}) collective-permute-start(bf16[8,144,512]{2,1,0:T(8,128)(2,1)} %get-tuple-element.656), channel_id=1, source_target_pairs={{0,2},{1,3},{2,0},{3,1},{4,6},{5,7},{6,4},{7,5},{8,9},{9,8},{10,11... | collective-permute-start | bytes 3538952 | tf_op jit(solution)/shard_map/ppermute | solution.py:710
  392.5 27.8 %collective-permute-start.43 = (bf16[2,4,144,512]{3,2,1,0:T(8,128)(2,1)}, bf16[2,4,144,512]{3,2,1,0:T(8,128)(2,1)}, u32[]{:S(2)}, u32[]{:S(2)}) collective-permute-start(bf16[2,4,144,512]{3,2,1,0:T(8,128)(2,1)} %get-tuple-element.657), channel_id=1, source_target_pairs={{0,8},{4,12},{8,0},{12,4},{16,24},{20,28},{24,16},{28,20},{1,9},{5... | collective-permute-start | bytes 3538952 | tf_op jit(solution)/shard_map/ppermute | solution.py:713
  420.4 28.9 %collective-permute-start.49 = (f32[4,512]{1,0:T(4,128)S(1)}, f32[4,512]{1,0:T(4,128)S(1)}, u32[]{:S(2)}, u32[]{:S(2)}) collective-permute-start(f32[4,512]{1,0:T(4,128)S(1)} %maximum_select_fusion), channel_id=1, source_target_pairs={{0,8},{4,12},{8,0},{12,4},{16,24},{20,28},{24,16},{28,20},{1,9},{5... | collective-permute-start | bytes 24584 | tf_op jit(solution)/shard_map/ppermute | solution.py:713
  421.4 27.9 %collective-permute-start.46 = (bf16[8,144,512]{2,1,0:T(8,128)(2,1)}, bf16[8,144,512]{2,1,0:T(8,128)(2,1)S(1)}, u32[]{:S(2)}, u32[]{:S(2)}) collective-permute-start(bf16[8,144,512]{2,1,0:T(8,128)(2,1)} %add_convert_fusion.3), channel_id=1, source_target_pairs={{0,1},{1,0},{2,3},{3,2},{4,5},{5,4},{6,7},{7,6},{8,10},{9,11},{10,... | collective-permute-start | bytes 3538952 | tf_op jit(solution)/shard_map/ppermute | solution.py:710
  422.5 26.8 %collective-permute-start.47 = (bf16[8,144,512]{2,1,0:T(8,128)(2,1)}, bf16[8,144,512]{2,1,0:T(8,128)(2,1)S(1)}, u32[]{:S(2)}, u32[]{:S(2)}) collective-permute-start(bf16[8,144,512]{2,1,0:T(8,128)(2,1)} %add_convert_fusion.2), channel_id=1, source_target_pairs={{0,2},{1,3},{2,0},{3,1},{4,6},{5,7},{6,4},{7,5},{8,9},{9,8},{10,11... | collective-permute-start | bytes 3538952 | tf_op jit(solution)/shard_map/ppermute | solution.py:710
  451.5 34.1 %collective-permute-start.54 = (bf16[2,4,144,512]{3,2,1,0:T(8,128)(2,1)}, bf16[2,4,144,512]{3,2,1,0:T(8,128)(2,1)}, u32[]{:S(2)}, u32[]{:S(2)}) collective-permute-start(bf16[2,4,144,512]{3,2,1,0:T(8,128)(2,1)} %pad_maximum_fusion), channel_id=1, source_target_pairs={{0,8},{4,12},{8,0},{12,4},{16,24},{20,28},{24,16},{28,20},{1,9},{5... | collective-permute-start | bytes 3538952 | tf_op jit(solution)/shard_map/ppermute | solution.py:713
  456.6 28.9 %collective-permute-start.50 = (bf16[4,144,512]{2,1,0:T(8,128)(2,1)}, bf16[4,144,512]{2,1,0:T(8,128)(2,1)}, u32[]{:S(2)}, u32[]{:S(2)}) collective-permute-start(bf16[4,144,512]{2,1,0:T(8,128)(2,1)} %get-tuple-element.780), channel_id=1, source_target_pairs={{0,1},{1,0},{2,3},{3,2},{4,5},{5,4},{6,7},{7,6},{8,10},{9,11},{10,... | collective-permute-start | bytes 1769480 | tf_op jit(solution)/shard_map/ppermute | solution.py:710
  457.8 27.8 %collective-permute-start.51 = (bf16[4,144,512]{2,1,0:T(8,128)(2,1)}, bf16[4,144,512]{2,1,0:T(8,128)(2,1)}, u32[]{:S(2)}, u32[]{:S(2)}) collective-permute-start(bf16[4,144,512]{2,1,0:T(8,128)(2,1)} %get-tuple-element.720), channel_id=1, source_target_pairs={{0,2},{1,3},{2,0},{3,1},{4,6},{5,7},{6,4},{7,5},{8,9},{9,8},{10,11... | collective-permute-start | bytes 1769480 | tf_op jit(solution)/shard_map/ppermute | solution.py:710
  489.9 26.1 %collective-permute-start.60 = (bf16[320,1152]{1,0:T(8,128)(2,1)S(1)}, bf16[320,1152]{1,0:T(8,128)(2,1)S(1)}, u32[]{:S(2)}, u32[]{:S(2)}) collective-permute-start(bf16[320,1152]{1,0:T(8,128)(2,1)S(1)} %get-tuple-element.802), channel_id=1, source_target_pairs={{0,3},{1,2},{2,1},{3,0},{4,7},{5,6},{6,5},{7,4},{8,11},{9,10},{10,... | collective-permute-start | bytes 2211848 | tf_op jit(solution)/shard_map/ppermute | solution.py:824
  496.4 32.9 %collective-permute-start.58 = (bf16[2,4,144,512]{3,2,1,0:T(8,128)(2,1)S(1)}, bf16[2,4,144,512]{3,2,1,0:T(8,128)(2,1)S(1)}, u32[]{:S(2)}, u32[]{:S(2)}) collective-permute-start(bf16[2,4,144,512]{3,2,1,0:T(8,128)(2,1)S(1)} %copy-done.125), channel_id=1, source_target_pairs={{0,8},{4,12},{8,0},{12,4},{16,24},{20,28},{24,16},{28,20},{1,9},{5... | collective-permute-start | bytes 3538952 | tf_op jit(solution)/shard_map/ppermute | solution.py:713
  533.4 28.9 %collective-permute-start.61 = (bf16[2,2,144,512]{3,2,0,1:T(8,128)(2,1)S(1)}, bf16[2,2,144,512]{3,2,0,1:T(8,128)(2,1)S(1)}, u32[]{:S(2)}, u32[]{:S(2)}) collective-permute-start(bf16[2,2,144,512]{3,2,0,1:T(8,128)(2,1)S(1)} %pad_maximum_fusion.11), channel_id=1, source_target_pairs={{0,16},{4,20},{8,24},{12,28},{16,0},{20,4},{24,8},{28,12},{1,17},{... | collective-permute-start | bytes 1769480 | tf_op jit(solution)/shard_map/ppermute | solution.py:713
  (162 other events, 1899.3 us)
